TPU v7x, 512 devices: a whole 4x8x8 slice. The times are simulated.
512 devices in a mesh: replica: 32 (over y, x), tensor: 16 (over z, core).
Axes of the slice: x: 4, y: 8, z: 8, core: 2. Of those that a mesh axis runs over, the one named last changes fastest.
Arguments:
- tokens_x: bfloat16 [4096, 8192], P('replica', 'tensor'), may hold values from -6 to 6
- cotangent: bfloat16 [256, 4096], P('tensor', 'replica'), may hold values from -6 to 6
- weight: bfloat16 [256, 8192], P('tensor'), may hold values from -0.375 to 0.375
- error_fb: float32 [32, 256, 8192], P('replica', 'tensor'), may hold values from -420 to 420, as said below
- momentum: float32 [256, 8192], P('tensor'), may hold values from -1.2 to 1.2
- q_prev: float32 [32, 8192], replicated, may hold values from -6 to 6
Outputs:
- input_grad: bfloat16 [4096, 8192], P('replica', 'tensor')
- error_new: float32 [32, 256, 8192], P('replica', 'tensor')
- momentum_new: float32 [256, 8192], P('tensor')
- q_new: float32 [32, 8192], replicated
Inputs may be any that keep to these rules, and one draw needn't show every extreme that they name: `error_fb`: finite values.
All inputs are finite; a program needn't handle non-finite values.
Results may differ from a plain program's by a relative error of at most 0.0011.
Values may be sent and summed in bfloat16 or wider, within the bound.
No kernel may reach another device: no remote copies, remote signals or barrier semaphores. Data moves between devices by JAX's collectives and lax.ppermute only.
A program may use at most 64 MiB of HBM per device.

v0:
```python
import jax
import jax.numpy as jnp
from jax import lax
from jax.sharding import PartitionSpec as P

CLIPPING = 0.2
BETA = 0.9


def body(tokens_x, cotangent, weight, error_fb, momentum, q_prev):
    highest = lax.Precision.HIGHEST
    n_tensor = lax.axis_size("tensor")
    n_replica = lax.axis_size("replica")
    position = lax.axis_index("tensor")
    rows = cotangent.shape[0]
    width = weight.shape[1]
    rank = q_prev.shape[0]
    ff_win = rows * n_tensor
    partial_dx = lax.dot_general(
        cotangent, weight, (((0,), (0,)), ((), ())), preferred_element_type=jnp.float32
    )
    input_grad = lax.psum_scatter(partial_dx, "tensor", scatter_dimension=1, tiled=True).astype(
        jnp.bfloat16
    )
    local_grad = jnp.dot(
        cotangent,
        lax.all_gather(tokens_x, "tensor", axis=1, tiled=True),
        preferred_element_type=jnp.float32,
    )
    merged = local_grad + error_fb[0]
    p_local = jnp.dot(merged, q_prev.T, precision=highest)
    placed = lax.dynamic_update_slice_in_dim(
        jnp.zeros((ff_win, rank), jnp.float32), p_local, position * rows, 0
    )
    p_sum = lax.psum(placed, ("replica", "tensor"))
    gram = jnp.dot(p_sum.T, p_sum, precision=highest)
    lower = jnp.linalg.cholesky(gram)
    p_mine = lax.dynamic_slice_in_dim(p_sum, position * rows, rows, 0)
    basis_t = lax.linalg.triangular_solve(lower, p_mine.T, left_side=True, lower=True)
    q_part = jnp.dot(basis_t, merged, precision=highest)
    q_sum = lax.psum(q_part, ("replica", "tensor"))
    q_new = q_sum / n_replica
    approx = jnp.dot(basis_t.T, q_new, precision=highest)
    error_new = (merged - approx)[None]
    total = lax.psum(jnp.sum(approx * approx), "tensor")
    scale = jnp.minimum(1.0, CLIPPING * jnp.sqrt(jnp.float32(ff_win * width)) / jnp.sqrt(total))
    momentum_new = BETA * momentum + scale * approx
    return (input_grad, error_new, momentum_new, q_new)


def solution(mesh):
    placed = (
        P("replica", "tensor"),
        P("tensor", "replica"),
        P("tensor", None),
        P("replica", "tensor", None),
        P("tensor", None),
        P(),
    )
    return jax.shard_map(
        body,
        mesh=mesh,
        in_specs=placed,
        out_specs=(P("replica", "tensor"), P("replica", "tensor", None), P("tensor", None), P()),
        check_vma=False,
    )
```

profile of v0, /device:TPU:1, one launch (start us, length us, event | category | flops | bytes accessed | tf_op | source)
XLA Modules:
  0.0 506.9 jit_solution(2141900320034253402)
XLA Ops:
  7.2 0.0 copy-start
  7.2 0.0 all-gather.2.cloned.1.call-start
  7.2 0.7 all-gather.2.cloned.1.call-update
  7.9 0.0 all-reduce.2.cloned.1.call-start
  8.0 51.3 %all-gather.2.cloned.1.call-done = bf16[128,8192]{1,0:T(8,128)(2,1)} async-done(((bf16[128,512]{1,0:T(8,128)(2,1)}), bf16[128,8192]{1,0:T(8,128)(2,1)}) %all-gather.2.cloned.1.call-update) | async-done | bytes 2097168 | tf_op jit(solution)/shard_map/all_gather | solution.py:27
  59.3 2.1 convolution_add_fusion
  61.4 0.0 copy-done
  61.4 0.0 copy-start.2
  61.4 0.0 copy-start.3
  61.4 0.9 convolution_dynamic-update-slice_fusion
  62.4 97.1 %psum.21 = f32[256,32]{1,0:T(8,128)S(1)} all-reduce(f32[256,32]{1,0:T(8,128)S(1)} %convolution_dynamic-update-slice_fusion), channel_id=1, replica_groups=mesh['replica'=32,'tensor'=16] {'replica','tensor'}, use_global_device_ids=true, to_apply=%region_1.0 | all-reduce | flops 8192 | bytes 65536 | tf_op jit(solution)/shard_map/psum | solution.py:35
  159.5 0.4 fusion.7
  159.8 0.1 copy.10
  159.9 2.9 cholesky.16
  162.9 0.6 compare_reduce_fusion
  163.5 0.7 fusion
  164.2 2.4 custom-call.6
  166.6 0.2 fusion.1
  166.8 2.0 fusion.8
  168.8 0.0 all-reduce.2.cloned.1.call-update
  168.8 0.0 reduce-scatter.2.cloned.1.call-start
  168.9 2.7 fusion.6
  171.5 0.0 reduce-scatter.2.cloned.1.call-update
  171.6 264.6 %all-reduce.2.cloned.1.call-done = f32[32,8192]{1,0:T(8,128)} async-done(((f32[32,8192]{1,0:T(8,128)}), f32[32,8192]{1,0:T(8,128)}) %all-reduce.2.cloned.1.call-update) | async-done | bytes 1048592 | tf_op jit(solution)/shard_map/psum | solution.py:41
  436.1 1.3 broadcast_multiply_fusion
  437.4 0.0 copy-start.1
  437.4 1.3 multiply_reduce_fusion
  438.7 22.6 %psum.23 = f32[]{:T(128)} all-reduce(f32[]{:T(128)} %get-tuple-element.6), channel_id=1, replica_groups=mesh['replica'=32,'tensor'=16] {'tensor'}, use_global_device_ids=true, to_apply=%region_6.7 | all-reduce | flops 1 | bytes 8 | tf_op jit(solution)/shard_map/psum | solution.py:45
  462.1 2.1 multiply_add_fusion
  464.2 0.0 copy-done.1
  464.2 34.5 %reduce-scatter.2.cloned.1.call-done = f32[128,512]{1,0:T(8,128)} async-done(((f32[128,8192]{1,0:T(8,128)}), f32[128,512]{1,0:T(8,128)}) %reduce-scatter.2.cloned.1.call-update) | async-done | bytes 262160 | tf_op jit(solution)/shard_map/reduce_scatter | solution.py:22
  498.7 1.6 convert_element_type.3
  (5 shorter events, 0.1 us)
Async XLA Ops:
  7.2 54.2 %copy-start = (f32[32,8192]{1,0:T(8,128)S(1)}, f32[32,8192]{1,0:T(8,128)}, u32[]{:S(2)}) copy-start(f32[32,8192]{1,0:T(8,128)} %param.11) | copy-start | bytes 3145732
  7.2 52.1 %all-gather.2.cloned.1.call-start = ((), (), s32[]{:S(2)}) async-start(), calls=%async_computation.2 | async-start | bytes 2228224 | tf_op jit(solution)/shard_map/all_gather | solution.py:27
  7.9 428.2 %all-reduce.2.cloned.1.call-start = ((), (), s32[]{:S(2)}) async-start(), calls=%async_computation.3 | async-start | bytes 2097152 | tf_op jit(solution)/shard_map/psum | solution.py:41
  61.4 107.5 %copy-start.2 = (bf16[16,8192]{1,0:T(8,128)(2,1)S(1)}, bf16[16,8192]{1,0:T(8,128)(2,1)}, u32[]{:S(2)}) copy-start(bf16[16,8192]{1,0:T(8,128)(2,1)} %param.8) | copy-start | bytes 786436
  61.4 107.5 %copy-start.3 = (bf16[16,128]{1,0:T(8,128)(2,1)S(1)}, bf16[16,128]{1,0:T(8,128)(2,1)}, u32[]{:S(2)}) copy-start(bf16[16,128]{1,0:T(8,128)(2,1)} %param.7) | copy-start | bytes 12292
  168.8 329.9 %reduce-scatter.2.cloned.1.call-start = ((), (), s32[]{:S(2)}) async-start(), calls=%async_computation.1 | async-start | bytes 4456448 | tf_op jit(solution)/shard_map/reduce_scatter | solution.py:22
  437.4 26.7 %copy-start.1 = (f32[32,8192]{1,0:T(8,128)}, f32[32,8192]{1,0:T(8,128)S(1)}, u32[]{:S(2)}) copy-start(f32[32,8192]{1,0:T(8,128)S(1)} %broadcast_multiply_fusion) | copy-start | bytes 3145732
Sparse Core Ops, SparseCore 0:
  10.2 49.1 all-gather.1
  168.9 267.1 all-reduce.1
  439.2 59.4 reduce-scatter.1
where the time goes:
time: 509 us; the launch traced here: 507 us
  waiting for transfers between devices  351 us (69%)
  blocking collectives  120 us (24%)
  between operations  14.5 us (3%)
  other arithmetic  11.7 us (2%)
  matrix products  9.47 us (2%)
    psum x1, waiting for transfers between devices, body(): q_sum = lax.psum(q_part, ('replica', 'tensor'))  265 us
    psum x1, blocking collectives, body(): p_sum = lax.psum(placed, ('replica', 'tensor'))  97.1 us
    all_gather x1, waiting for transfers between devices, body(): lax.all_gather(tokens_x, 'tensor', axis=1, tiled=True)  51.3 us
    reduce_scatter x1, waiting for transfers between devices, body(): lax.psum_scatter(partial_dx, 'tensor', scatter_dimension=1, tiled=True)  34.5 us
    psum x1, blocking collectives, body(): total = lax.psum(jnp.sum(approx * approx), 'tensor')  22.6 us
  transfers between devices with their start and end apart: 3, of which 3 were waited for; matrix products, arithmetic and copies ran while one was open for 1% of the time, Pallas kernels for 0%

commit v1 on v0

v1 whole, which is shorter than its diff:
```python
import jax
import jax.numpy as jnp
from jax import lax
from jax.sharding import Mesh, PartitionSpec as P

CLIPPING = 0.2
BETA = 0.9
HIGHEST = lax.Precision.HIGHEST
LANES = 128

T = ("z", "core")
R = ("y", "x")


def exchange(parts, axes):
    return lax.all_to_all(parts, axes, 0, 0, tiled=True)


def spread(block, axes):
    return exchange(jnp.broadcast_to(block[None], (lax.axis_size(axes), *block.shape)), axes)


def body(tokens_x, cotangent, weight, error_fb, momentum, q_prev):
    n_t, n_r = lax.axis_size(T), lax.axis_size(R)
    t = lax.axis_index(T)
    core = lax.axis_index("core")
    tokens, wide = tokens_x.shape
    rows, width = weight.shape
    rank = q_prev.shape[0]
    ff_win = rows * n_t
    own = wide // n_r
    error = error_fb[0]

    x_all = lax.all_gather(tokens_x, T, axis=1, tiled=True)
    w_all = lax.all_gather(weight, T, axis=0, tiled=True)

    q_mine = lax.dynamic_slice_in_dim(q_prev, t * wide, wide, 1)
    y_t = lax.dot_general(
        q_mine, tokens_x.astype(jnp.float32), (((1,), (1,)), ((), ())), precision=HIGHEST
    )
    p_error = lax.dot_general(error, q_prev, (((1,), (1,)), ((), ())), precision=HIGHEST)
    fold = rank // rows
    y_fold = y_t.reshape(fold, rows, tokens).transpose(1, 0, 2).reshape(rows, fold * tokens)
    same = jnp.concatenate([cotangent.astype(jnp.float32), y_fold], 1)
    first = jnp.concatenate(
        [
            error.reshape(rows, n_t, wide).transpose(1, 0, 2),
            jnp.broadcast_to(same[None], (n_t, *same.shape)),
        ],
        2,
    )
    first = exchange(first, T)
    error_cols = first[:, :, :wide].reshape(ff_win, wide)
    cot_all = first[:, :, wide : wide + tokens].reshape(ff_win, tokens).astype(jnp.bfloat16)
    y_sum = jnp.sum(first[:, :, wide + tokens :], 0)
    y_sum = y_sum.reshape(rows, fold, tokens).transpose(1, 0, 2).reshape(rank, tokens)
    p_mine = p_error + lax.dot_general(
        cotangent.astype(jnp.float32), y_sum, (((1,), (1,)), ((), ())), precision=HIGHEST
    )

    merged_t = error_cols.T + lax.dot_general(
        tokens_x, cot_all, (((0,), (1,)), ((), ())), preferred_element_type=jnp.float32
    )
    flat = rows * rank // LANES
    second = jnp.concatenate(
        [
            merged_t.reshape(n_r, own * ff_win // LANES, LANES),
            jnp.broadcast_to(p_mine.reshape(1, flat, LANES), (n_r, flat, LANES)),
        ],
        1,
    )
    second = jnp.sum(exchange(second, R), 0)
    total_t = second[: own * ff_win // LANES].reshape(own, ff_win)
    p_sum = spread(second[own * ff_win // LANES :], T).reshape(ff_win, rank)

    gram = lax.dot_general(p_sum, p_sum, (((0,), (0,)), ((), ())), precision=HIGHEST)
    lower = jnp.linalg.cholesky(gram)
    basis_t = lax.linalg.triangular_solve(lower, p_sum.T, left_side=True, lower=True)
    q_own = lax.dot_general(total_t, basis_t, (((1,), (1,)), ((), ())), precision=HIGHEST) / n_r

    q_cols = spread(q_own.reshape(own * rank // LANES, LANES), R).reshape(wide, rank).T
    q_z = spread(q_cols, "z")
    q_other = lax.ppermute(q_z, "core", [(0, 1), (1, 0)])
    q_pair = jnp.where(core == 0, jnp.stack([q_z, q_other], 1), jnp.stack([q_other, q_z], 1))
    q_new = q_pair.reshape(n_t, rank, wide).transpose(1, 0, 2).reshape(rank, width)

    basis_mine = lax.dynamic_slice_in_dim(basis_t, t * rows, rows, 1)
    approx = lax.dot_general(basis_mine, q_new, (((0,), (0,)), ((), ())), precision=HIGHEST)
    merged = error + jnp.dot(cotangent, x_all, preferred_element_type=jnp.float32)
    error_new = (merged - approx)[None]
    basis_gram = lax.dot_general(basis_t, basis_t, (((1,), (1,)), ((), ())), precision=HIGHEST)
    q_gram = lax.dot_general(q_new, q_new, (((1,), (1,)), ((), ())), precision=HIGHEST)
    total = jnp.sum(basis_gram * q_gram)
    scale = jnp.minimum(1.0, CLIPPING * jnp.sqrt(jnp.float32(ff_win * width)) / jnp.sqrt(total))
    momentum_new = BETA * momentum + scale * approx

    w_cols = lax.dynamic_slice_in_dim(w_all, t * wide, wide, 1)
    input_grad = lax.dot_general(
        cot_all, w_cols, (((0,), (0,)), ((), ())), preferred_element_type=jnp.float32
    ).astype(jnp.bfloat16)
    return (input_grad, error_new, momentum_new, q_new)


def solution(mesh):
    n_r, n_t = mesh.devices.shape
    x = 4 if n_r % 4 == 0 and n_r > 4 else 2
    split = Mesh(mesh.devices.reshape(n_r // x, x, n_t // 2, 2), ("y", "x", "z", "core"))
    placed = (P(R, T), P(T, R), P(T, None), P(R, T, None), P(T, None), P())
    return jax.shard_map(
        body,
        mesh=split,
        in_specs=placed,
        out_specs=(P(R, T), P(R, T, None), P(T, None), P()),
        check_vma=False,
    )
```

time: 509 us -> 165 us (0.32)
  waiting for transfers between devices: 351 us -> 10.1 us
  blocking collectives: 120 us -> 103 us
  starting transfers between devices: 0.12 us -> 9.44 us
  local copies, waits for them, and re-layouts: 0.11 us -> 5.23 us
    psum x1 -> x0, waiting for transfers between devices: 265 us -> none  [body(): q_sum = lax.psum(q_part, ('replica', 'tensor'))]
    psum x2 -> x0, blocking collectives: 120 us -> none  [the longest x1 97.1 us: body(): p_sum = lax.psum(placed, ('replica', 'tensor'))]
    all_to_all x0 -> x4, blocking collectives: none -> 103 us  [exchange(): return lax.all_to_all(parts, axes, 0, 0, tiled=True)]
    all_gather x1 -> x2, waiting for transfers between devices: 51.3 us -> 0.01 us  [the longest x1 0.01 us: body(): x_all = lax.all_gather(tokens_x, T, axis=1, tiled=True)]
    reduce_scatter x1 -> x0, waiting for transfers between devices: 34.5 us -> none  [body(): lax.psum_scatter(partial_dx, 'tensor', scatter_dimension=1, tiled=True)]
    all_to_all x0 -> x1, waiting for transfers between devices: none -> 7.36 us  [exchange(): return lax.all_to_all(parts, axes, 0, 0, tiled=True)]
    ppermute x0 -> x1, starting transfers between devices: none -> 5.6 us  [body(): q_other = lax.ppermute(q_z, 'core', [(0, 1), (1, 0)])]
    dot_general x6 -> x11, matrix products: 9.32 us -> 12.1 us  [the longest x1 2.89 us: body(): lax.dot_general(basis_mine, q_new, (((0,), (0,)), ((), ())), precision=HI...]
  transfers between devices with their start and end apart: 3 -> 4, of which waited for: 3 -> 2; matrix products, arithmetic and copies ran while one was open for 1% -> 15% of each run, Pallas kernels for 0% -> 0%
where the time goes in v1:
time: 165 us
  blocking collectives  103 us (62%)
  between operations  15 us (9%)
  matrix products  12.4 us (8%)
  waiting for transfers between devices  10.1 us (6%)
  starting transfers between devices  9.44 us (6%)
  other arithmetic  8.99 us (5%)
  local copies, waits for them, and re-layouts  5.23 us (3%)
    all_to_all x4, blocking collectives, exchange(): return lax.all_to_all(parts, axes, 0, 0, tiled=True)  103 us
    all_to_all x1, waiting for transfers between devices, exchange(): return lax.all_to_all(parts, axes, 0, 0, tiled=True)  7.36 us
    ppermute x1, starting transfers between devices, body(): q_other = lax.ppermute(q_z, 'core', [(0, 1), (1, 0)])  5.6 us
    all_to_all x1, starting transfers between devices, exchange(): return lax.all_to_all(parts, axes, 0, 0, tiled=True)  3.76 us
    another operation x3, other arithmetic, body(): lower = jnp.linalg.cholesky(gram)  3.6 us
  transfers between devices with their start and end apart: 4, of which 2 were waited for; matrix products, arithmetic and copies ran while one was open for 15% of the time, Pallas kernels for 0%

profile of v1, /device:TPU:1, one launch (start us, length us, event | category | flops | bytes accessed | tf_op | source)
XLA Modules:
  0.0 164.6 jit_solution(12766152531623546464)
XLA Ops:
  7.2 0.7 all-gather.5.cloned.1.call-update
  8.0 0.7 all-gather.3.cloned.1.call-update
  8.7 1.1 fusion.7
  9.9 0.7 convert_element_type.12
  10.5 1.3 copy.27
  11.9 0.3 copy.31
  12.4 43.4 %all_to_all.25 = f32[16,16,896]{2,1,0:T(8,128)S(1)} all-to-all(f32[16,16,896]{2,1,0:T(8,128)S(1)} %pad_maximum_fusion), channel_id=1, replica_groups=mesh['y'=8,'x'=4,'z'=8,'core'=2] {'z','core'}, dimensions={0} | all-to-all | bytes 1835008 | tf_op jit(solution)/shard_map/all_to_all | solution.py:16
  56.0 1.0 convolution_add_fusion.2
  57.1 0.2 fusion.2
  57.4 0.2 copy.21
  57.7 29.5 %all_to_all.26 = f32[32,36,128]{2,1,0:T(8,128)S(1)} all-to-all(f32[32,36,128]{2,1,0:T(8,128)S(1)} %pad_maximum_fusion.1), channel_id=1, replica_groups=mesh['y'=8,'x'=4,'z'=8,'core'=2] {'y','x'}, dimensions={0} | all-to-all | bytes 1179648 | tf_op jit(solution)/shard_map/all_to_all | solution.py:16
  87.2 0.6 broadcast_in_dim.40
  87.8 3.8 %all-to-all-start.2 = ((f32[16,4,128]{2,1,0:T(4,128)}), f32[16,4,128]{2,1,0:T(4,128)S(1)}, u32[]{:S(2)}, u32[]{:S(2)}) async-start(f32[16,4,128]{2,1,0:T(4,128)} %broadcast_in_dim.40), calls=%async_computation.2 | async-start | bytes 65536 | tf_op jit(solution)/shard_map/all_to_all | solution.py:16
  91.6 7.4 %all-to-all-done.2 = f32[16,4,128]{2,1,0:T(4,128)S(1)} async-done(((f32[16,4,128]{2,1,0:T(4,128)}), f32[16,4,128]{2,1,0:T(4,128)S(1)}, u32[]{:S(2)}, u32[]{:S(2)}) %all-to-all-start.2) | async-done | bytes 32800 | tf_op jit(solution)/shard_map/all_to_all | solution.py:16
  99.1 0.4 fusion.18
  99.5 2.9 %cholesky.16 = f32[32,32]{1,0:T(8,128)S(1)} custom-call(f32[32,32]{1,0:T(8,128)S(1)} %fusion.12), custom_call_target="Cholesky" | custom-call | tf_op jit(solution)/shard_map/jit(cholesky)/cholesky | solution.py:77
  102.5 0.6 compare_reduce_fusion
  103.1 0.7 fusion.9
  103.8 2.4 %custom-call.6 = f32[1,32,32]{1,2,0:T(8,128)S(1)} custom-call(f32[1,32,32]{2,1,0:T(8,128)S(1)} %fusion.9), custom_call_target="InvertDiagBlocksLowerTriangular" | custom-call | tf_op jit(solution)/shard_map/triangular_solve | solution.py:78
  106.2 0.3 fusion.10
  106.8 13.4 %all_to_all.27 = f32[32,4,128]{2,1,0:T(4,128)S(1)} all-to-all(f32[32,4,128]{2,1,0:T(4,128)S(1)} %broadcast_in_dim.42), channel_id=1, replica_groups=mesh['y'=8,'x'=4,'z'=8,'core'=2] {'y','x'}, dimensions={0} | all-to-all | bytes 131072 | tf_op jit(solution)/shard_map/all_to_all | solution.py:16
  120.5 17.2 %all_to_all.28 = f32[8,32,512]{2,1,0:T(8,128)S(1)} all-to-all(f32[8,32,512]{2,1,0:T(8,128)S(1)} %broadcast_in_dim.43), channel_id=1, replica_groups=mesh['y'=8,'x'=4,'z'=8,'core'=2] {'z'}, dimensions={0} | all-to-all | bytes 1048576 | tf_op jit(solution)/shard_map/all_to_all | solution.py:16
  137.7 5.6 %collective-permute-start = (f32[8,32,512]{2,1,0:T(8,128)S(1)}, f32[8,32,512]{2,1,0:T(8,128)S(1)}, u32[]{:S(2)}, u32[]{:S(2)}) collective-permute-start(f32[8,32,512]{2,1,0:T(8,128)S(1)} %all_to_all.28), channel_id=1, source_target_pairs={{0,1},{1,0},{2,3},{3,2},{4,5},{5,4},{6,7},{7,6},{8,9},{9,8},{10,11... | collective-permute-start | bytes 1572872 | tf_op jit(solution)/shard_map/ppermute | solution.py:83
  143.3 0.2 fusion.19
  143.4 1.3 collective-permute-done
  144.8 0.8 copy-done.3
  145.6 1.4 maximum_select_fusion
  147.0 1.6 fusion.4
  149.2 1.1 copy.26
  150.3 2.9 %multiply_add_fusion = (f32[16,8192]{1,0:T(8,128)}, f32[16,8192]{1,0:T(8,128)S(1)}) fusion(f32[16,8192]{1,0:T(8,128)} %param.10, f32[]{:T(128)S(6)} %min_shard_map.3, f32[32,8192]{1,0:T(8,128)} %bitcast.71, f32[32,256]{1,0:T(8,128)S(1)} %fusion.10, s32[]{:T(128)S(6)} %select_n.25), kind=kOutput, calls=%fused_computation.17 | convolution fusion | flops 50724864 | bytes 2637832 | tf_op jit(solution)/shard_map/dot_general | solution.py:88
  153.2 2.8 %fusion.1 = f32[1,16,8192]{2,1,0:T(8,128)} fusion(f32[16,8192]{1,0:T(8,128)S(1)} %get-tuple-element.5, bf16[16,128]{1,0:T(8,128)(2,1)S(1)} %copy-done.4, bf16[128,8192]{1,0:T(8,128)(2,1)} %all-gather.5.cloned.1.call-done, f32[1,16,8192]{2,1,0:T(8,128)S(1)} %copy-done.1), kind=kOutput, calls=%fused_computation.2 | convolution fusion | flops 33816576 | bytes 3674112 | tf_op jit(solution)/shard_map/dot_general | solution.py:89
  156.0 1.8 %convolution_convert_fusion = bf16[128,512]{1,0:T(8,128)(2,1)} fusion(bf16[256,128]{1,0:T(8,128)(2,1)S(1)} %bitcast.79, bf16[256,8192]{1,0:T(8,128)(2,1)} %all-gather.3.cloned.1.call-done, s32[]{:T(128)S(6)} %select_n.23), kind=kOutput, calls=%fused_computation.5 | convolution fusion | flops 33619968 | bytes 458756 | tf_op jit(solution)/shard_map/dot_general | solution.py:98
  (42 shorter events, 1.5 us)
Async XLA Ops:
  7.2 1.5 copy-start
  7.2 146.0 %all-gather.5.cloned.1.call-start = ((), (), s32[]{:S(2)}) async-start(), calls=%async_computation.6 | async-start | bytes 2228224 | tf_op jit(solution)/shard_map/all_gather | solution.py:34
  7.9 148.1 %all-gather.3.cloned.1.call-start = ((), (), s32[]{:S(2)}) async-start(), calls=%async_computation.5 | async-start | bytes 4456448 | tf_op jit(solution)/shard_map/all_gather | solution.py:35
  12.2 43.6 %copy-start.4 = (bf16[16,128]{1,0:T(8,128)(2,1)S(1)}, bf16[16,128]{1,0:T(8,128)(2,1)}, u32[]{:S(2)}) copy-start(bf16[16,128]{1,0:T(8,128)(2,1)} %param.7) | copy-start | bytes 12292
  12.3 43.7 %copy-start.1 = (f32[1,16,8192]{2,1,0:T(8,128)S(1)}, f32[1,16,8192]{2,1,0:T(8,128)}, u32[]{:S(2)}) copy-start(f32[1,16,8192]{2,1,0:T(8,128)} %param.9) | copy-start | bytes 1572868
  12.3 44.8 %copy-start.2 = (bf16[128,512]{1,0:T(8,128)(2,1)S(1)}, bf16[128,512]{1,0:T(8,128)(2,1)}, u32[]{:S(2)}) copy-start(bf16[128,512]{1,0:T(8,128)(2,1)} %param.6) | copy-start | bytes 393220
  87.8 11.1 %all-to-all-start.2 = ((f32[16,4,128]{2,1,0:T(4,128)}), f32[16,4,128]{2,1,0:T(4,128)S(1)}, u32[]{:S(2)}, u32[]{:S(2)}) async-start(f32[16,4,128]{2,1,0:T(4,128)} %broadcast_in_dim.40), calls=%async_computation.2 | async-start | bytes 65536 | tf_op jit(solution)/shard_map/all_to_all | solution.py:16
  137.7 7.1 %collective-permute-start = (f32[8,32,512]{2,1,0:T(8,128)S(1)}, f32[8,32,512]{2,1,0:T(8,128)S(1)}, u32[]{:S(2)}, u32[]{:S(2)}) collective-permute-start(f32[8,32,512]{2,1,0:T(8,128)S(1)} %all_to_all.28), channel_id=1, source_target_pairs={{0,1},{1,0},{2,3},{3,2},{4,5},{5,4},{6,7},{7,6},{8,9},{9,8},{10,11... | collective-permute-start | bytes 1572872 | tf_op jit(solution)/shard_map/ppermute | solution.py:83
  144.8 0.8 copy-start.3
Sparse Core Ops, SparseCore 0:
  10.2 55.4 all-gather.4
  67.8 43.7 all-gather.2

commit v2 on v1

--- a/solution.py
+++ b/solution.py
@@ -31,9 +31,6 @@
     own = wide // n_r
     error = error_fb[0]
 
-    x_all = lax.all_gather(tokens_x, T, axis=1, tiled=True)
-    w_all = lax.all_gather(weight, T, axis=0, tiled=True)
-
     q_mine = lax.dynamic_slice_in_dim(q_prev, t * wide, wide, 1)
     y_t = lax.dot_general(
         q_mine, tokens_x.astype(jnp.float32), (((1,), (1,)), ((), ())), precision=HIGHEST
@@ -45,14 +42,16 @@
     first = jnp.concatenate(
         [
             error.reshape(rows, n_t, wide).transpose(1, 0, 2),
+            weight.astype(jnp.float32).reshape(rows, n_t, wide).transpose(1, 0, 2),
             jnp.broadcast_to(same[None], (n_t, *same.shape)),
         ],
         2,
     )
     first = exchange(first, T)
     error_cols = first[:, :, :wide].reshape(ff_win, wide)
-    cot_all = first[:, :, wide : wide + tokens].reshape(ff_win, tokens).astype(jnp.bfloat16)
-    y_sum = jnp.sum(first[:, :, wide + tokens :], 0)
+    w_cols = first[:, :, wide : 2 * wide].reshape(ff_win, wide).astype(jnp.bfloat16)
+    cot_all = first[:, :, 2 * wide : 2 * wide + tokens].reshape(ff_win, tokens).astype(jnp.bfloat16)
+    y_sum = jnp.sum(first[:, :, 2 * wide + tokens :], 0)
     y_sum = y_sum.reshape(rows, fold, tokens).transpose(1, 0, 2).reshape(rank, tokens)
     p_mine = p_error + lax.dot_general(
         cotangent.astype(jnp.float32), y_sum, (((1,), (1,)), ((), ())), precision=HIGHEST
@@ -71,7 +70,20 @@
     )
     second = jnp.sum(exchange(second, R), 0)
     total_t = second[: own * ff_win // LANES].reshape(own, ff_win)
-    p_sum = spread(second[own * ff_win // LANES :], T).reshape(ff_win, rank)
+
+    grad_cols = jnp.dot(cot_all, tokens_x, preferred_element_type=jnp.float32)
+    tiles = wide // LANES
+    third = jnp.concatenate(
+        [
+            grad_cols.reshape(n_t, rows, tiles, LANES).transpose(0, 2, 1, 3).reshape(n_t, tiles * rows, LANES),
+            jnp.broadcast_to(second[None, own * ff_win // LANES :], (n_t, flat, LANES)),
+        ],
+        1,
+    )
+    third = exchange(third, T)
+    p_sum = third[:, tiles * rows :].reshape(ff_win, rank)
+    grad_rows = third[:, : tiles * rows].reshape(n_t, tiles, rows, LANES)
+    grad_rows = grad_rows.transpose(2, 0, 1, 3).reshape(rows, width)
 
     gram = lax.dot_general(p_sum, p_sum, (((0,), (0,)), ((), ())), precision=HIGHEST)
     lower = jnp.linalg.cholesky(gram)
@@ -86,15 +98,13 @@
 
     basis_mine = lax.dynamic_slice_in_dim(basis_t, t * rows, rows, 1)
     approx = lax.dot_general(basis_mine, q_new, (((0,), (0,)), ((), ())), precision=HIGHEST)
-    merged = error + jnp.dot(cotangent, x_all, preferred_element_type=jnp.float32)
-    error_new = (merged - approx)[None]
+    error_new = (error + grad_rows - approx)[None]
     basis_gram = lax.dot_general(basis_t, basis_t, (((1,), (1,)), ((), ())), precision=HIGHEST)
     q_gram = lax.dot_general(q_new, q_new, (((1,), (1,)), ((), ())), precision=HIGHEST)
     total = jnp.sum(basis_gram * q_gram)
     scale = jnp.minimum(1.0, CLIPPING * jnp.sqrt(jnp.float32(ff_win * width)) / jnp.sqrt(total))
     momentum_new = BETA * momentum + scale * approx
 
-    w_cols = lax.dynamic_slice_in_dim(w_all, t * wide, wide, 1)
     input_grad = lax.dot_general(
         cot_all, w_cols, (((0,), (0,)), ((), ())), preferred_element_type=jnp.float32
     ).astype(jnp.bfloat16)

time: 165 us -> 175 us (1.061)
  waiting for transfers between devices: 10.1 us -> 36 us
  blocking collectives: 103 us -> 80.3 us
  between operations: 15 us -> 1.7 us
  starting transfers between devices: 9.44 us -> 19.4 us
  local copies, waits for them, and re-layouts: 5.23 us -> 12 us
  other arithmetic: 8.99 us -> 13.4 us
    all_to_all x1 -> x2, waiting for transfers between devices: 7.36 us -> 36 us  [exchange(): return lax.all_to_all(parts, axes, 0, 0, tiled=True)]
    all_to_all x4 -> x3, blocking collectives: 103 us -> 80.3 us  [exchange(): return lax.all_to_all(parts, axes, 0, 0, tiled=True)]
    all_to_all x1 -> x2, starting transfers between devices: 3.76 us -> 14.2 us  [exchange(): return lax.all_to_all(parts, axes, 0, 0, tiled=True)]
    slice x2 -> x4, local copies, waits for them, and re-layouts: 0.02 us -> 2.64 us  [the longest x1 1.09 us: body(): grad_rows = third[:, :tiles * rows].reshape(n_t, tiles, rows, LANES)]
  transfers between devices with their start and end apart: 4 -> 3, of which waited for: 2 -> 2; matrix products, arithmetic and copies ran while one was open for 15% -> 4% of each run, Pallas kernels for 0% -> 0%
where the time goes in v2:
time: 175 us; the launch traced here: 174 us
  blocking collectives  80.3 us (46%)
  waiting for transfers between devices  36 us (21%)
  starting transfers between devices  19.4 us (11%)
  other arithmetic  13.4 us (8%)
  local copies, waits for them, and re-layouts  12 us (7%)
  matrix products  10.9 us (6%)
    all_to_all x3, blocking collectives, exchange(): return lax.all_to_all(parts, axes, 0, 0, tiled=True)  80.3 us
    all_to_all x2, waiting for transfers between devices, exchange(): return lax.all_to_all(parts, axes, 0, 0, tiled=True)  36 us
    all_to_all x2, starting transfers between devices, exchange(): return lax.all_to_all(parts, axes, 0, 0, tiled=True)  14.2 us
    ppermute x1, starting transfers between devices, body(): q_other = lax.ppermute(q_z, 'core', [(0, 1), (1, 0)])  5.26 us
    another operation x3, other arithmetic, body(): lower = jnp.linalg.cholesky(gram)  3.6 us
  transfers between devices with their start and end apart: 3, of which 2 were waited for; matrix products, arithmetic and copies ran while one was open for 4% of the time, Pallas kernels for 0%

profile of v2, /device:TPU:1, one launch (start us, length us, event | category | flops | bytes accessed | tf_op | source)
XLA Modules:
  0.0 173.7 jit_solution(14465748251319202809)
XLA Ops:
  0.7 1.2 copy-done
  1.9 1.1 fusion.9
  3.0 0.7 convert_element_type.19
  3.7 1.0 transpose.67
  5.6 48.6 %all_to_all.25 = f32[16,16,1408]{2,1,0:T(8,128)S(1)} all-to-all(f32[16,16,1408]{2,1,0:T(8,128)S(1)} %pad_maximum_fusion), channel_id=1, replica_groups=mesh['y'=8,'x'=4,'z'=8,'core'=2] {'z','core'}, dimensions={0} | all-to-all | bytes 2883584 | tf_op jit(solution)/shard_map/all_to_all | solution.py:16
  54.3 1.0 convolution_add_fusion.1
  55.5 1.1 fusion
  56.6 1.0 copy.27
  57.6 1.1 reshape.84
  58.7 0.9 pad_maximum_fusion.1
  59.6 9.8 %all-to-all-start.1 = ((f32[32,36,128]{2,1,0:T(8,128)}), f32[32,36,128]{2,1,0:T(8,128)}, u32[]{:S(2)}, u32[]{:S(2)}) async-start(f32[32,36,128]{2,1,0:T(8,128)} %pad_maximum_fusion.1), calls=%async_computation.1 | async-start | bytes 1310720 | tf_op jit(solution)/shard_map/all_to_all | solution.py:16
  69.4 1.7 copy.34
  71.1 1.1 fusion.7
  72.2 17.3 %all-to-all-done.1 = f32[32,36,128]{2,1,0:T(8,128)} async-done(((f32[32,36,128]{2,1,0:T(8,128)}), f32[32,36,128]{2,1,0:T(8,128)}, u32[]{:S(2)}, u32[]{:S(2)}) %all-to-all-start.1) | async-done | bytes 589856 | tf_op jit(solution)/shard_map/all_to_all | solution.py:16
  89.5 1.7 %reduce_sum.28 = f32[36,128]{1,0:T(8,128)} reduce(f32[32,36,128]{2,1,0:T(8,128)} %all-to-all-done.1, f32[]{:T(128)} %constant.61.clone.1), dimensions={0}, to_apply=%region_1.0 | reduce | flops 142848 | bytes 608260 | tf_op jit(solution)/shard_map/reduce_sum | solution.py:71
  91.2 0.7 slice.47
  91.9 0.9 pad_maximum_fusion.2
  92.8 4.4 %all-to-all-start.2 = ((f32[16,68,128]{2,1,0:T(8,128)}), f32[16,68,128]{2,1,0:T(8,128)}, u32[]{:S(2)}, u32[]{:S(2)}) async-start(f32[16,68,128]{2,1,0:T(8,128)} %pad_maximum_fusion.2), calls=%async_computation.2 | async-start | bytes 1179648 | tf_op jit(solution)/shard_map/all_to_all | solution.py:16
  97.2 18.7 %all-to-all-done.2 = f32[16,68,128]{2,1,0:T(8,128)} async-done(((f32[16,68,128]{2,1,0:T(8,128)}), f32[16,68,128]{2,1,0:T(8,128)}, u32[]{:S(2)}, u32[]{:S(2)}) %all-to-all-start.2) | async-done | bytes 557088 | tf_op jit(solution)/shard_map/all_to_all | solution.py:16
  115.9 0.8 slice.49
  117.3 2.9 %cholesky.16 = f32[32,32]{1,0:T(8,128)S(1)} custom-call(f32[32,32]{1,0:T(8,128)S(1)} %fusion.14), custom_call_target="Cholesky" | custom-call | tf_op jit(solution)/shard_map/jit(cholesky)/cholesky | solution.py:89
  121.6 2.4 %custom-call.6 = f32[1,32,32]{1,2,0:T(8,128)S(1)} custom-call(f32[1,32,32]{2,1,0:T(8,128)S(1)} %fusion.11), custom_call_target="InvertDiagBlocksLowerTriangular" | custom-call | tf_op jit(solution)/shard_map/triangular_solve | solution.py:90
  125.2 14.2 %all_to_all.26 = f32[32,4,128]{2,1,0:T(4,128)S(1)} all-to-all(f32[32,4,128]{2,1,0:T(4,128)S(1)} %broadcast_in_dim.42), channel_id=1, replica_groups=mesh['y'=8,'x'=4,'z'=8,'core'=2] {'y','x'}, dimensions={0} | all-to-all | bytes 131072 | tf_op jit(solution)/shard_map/all_to_all | solution.py:16
  139.7 17.5 %all_to_all.27 = f32[8,32,512]{2,1,0:T(8,128)S(1)} all-to-all(f32[8,32,512]{2,1,0:T(8,128)S(1)} %broadcast_in_dim.43), channel_id=1, replica_groups=mesh['y'=8,'x'=4,'z'=8,'core'=2] {'z'}, dimensions={0} | all-to-all | bytes 1048576 | tf_op jit(solution)/shard_map/all_to_all | solution.py:16
  157.2 5.3 %collective-permute-start = (f32[8,32,512]{2,1,0:T(8,128)S(1)}, f32[8,32,512]{2,1,0:T(8,128)}, u32[]{:S(2)}, u32[]{:S(2)}) collective-permute-start(f32[8,32,512]{2,1,0:T(8,128)S(1)} %all_to_all.27), channel_id=1, source_target_pairs={{0,1},{1,0},{2,3},{3,2},{4,5},{5,4},{6,7},{7,6},{8,9},{9,8},{10,11... | collective-permute-start | bytes 1572872 | tf_op jit(solution)/shard_map/ppermute | solution.py:95
  162.5 0.9 fusion.1
  163.3 1.1 slice.48
  164.6 1.0 reshape.88
  165.8 1.4 maximum_select_fusion
  167.3 1.6 fusion.3
  169.6 1.1 copy.36
  170.6 3.1 %multiply_add_fusion = (f32[16,8192]{1,0:T(8,128)}, f32[1,16,8192]{2,1,0:T(8,128)}) fusion(f32[16,8192]{1,0:T(8,128)} %param.10, f32[]{:T(128)S(6)} %min_shard_map.3, f32[16,8192]{1,0:T(8,128)S(1)} %copy-done.2, f32[1,16,8192]{2,1,0:T(8,128)S(1)} %copy-done.1, f32[32,8192]{1,0:T(8,128)} %bitcast.100, f32[32,256]{1,0:T(8,128)S(1)} %copy-done.5, s32[]{:T(128)S(6)} %select_n.24), kind=kOutput, calls=%fused_computation.22 | convolution fusion | flops 50987008 | bytes 3686408 | tf_op jit(solution)/shard_map/dot_general | solution.py:100
  (50 shorter events, 4.9 us)
Async XLA Ops:
  0.6 1.2 copy-start
  0.6 4.1 %copy-start.1 = (f32[1,16,8192]{2,1,0:T(8,128)S(1)}, f32[1,16,8192]{2,1,0:T(8,128)}, u32[]{:S(2)}) copy-start(f32[1,16,8192]{2,1,0:T(8,128)} %param.9) | copy-start | bytes 1572868
  5.5 48.7 %copy-start.6 = (bf16[16,128]{1,0:T(8,128)(2,1)S(1)}, bf16[16,128]{1,0:T(8,128)(2,1)}, u32[]{:S(2)}) copy-start(bf16[16,128]{1,0:T(8,128)(2,1)} %param.7) | copy-start | bytes 12292
  59.6 29.9 %all-to-all-start.1 = ((f32[32,36,128]{2,1,0:T(8,128)}), f32[32,36,128]{2,1,0:T(8,128)}, u32[]{:S(2)}, u32[]{:S(2)}) async-start(f32[32,36,128]{2,1,0:T(8,128)} %pad_maximum_fusion.1), calls=%async_computation.1 | async-start | bytes 1310720 | tf_op jit(solution)/shard_map/all_to_all | solution.py:16
  91.2 6.0 %slice-start = ((f32[36,128]{1,0:T(8,128)}), f32[32,128]{1,0:T(8,128)S(1)}, s32[]{:S(2)}) async-start(f32[36,128]{1,0:T(8,128)} %reduce_sum.28), calls=%async_computation.5 | async-start | bytes 32768 | tf_op jit(solution)/shard_map/slice | solution.py:72
  92.8 23.1 %all-to-all-start.2 = ((f32[16,68,128]{2,1,0:T(8,128)}), f32[16,68,128]{2,1,0:T(8,128)}, u32[]{:S(2)}, u32[]{:S(2)}) async-start(f32[16,68,128]{2,1,0:T(8,128)} %pad_maximum_fusion.2), calls=%async_computation.2 | async-start | bytes 1179648 | tf_op jit(solution)/shard_map/all_to_all | solution.py:16
  124.3 0.6 copy-start.3
  157.2 8.6 %collective-permute-start = (f32[8,32,512]{2,1,0:T(8,128)S(1)}, f32[8,32,512]{2,1,0:T(8,128)}, u32[]{:S(2)}, u32[]{:S(2)}) collective-permute-start(f32[8,32,512]{2,1,0:T(8,128)S(1)} %all_to_all.27), channel_id=1, source_target_pairs={{0,1},{1,0},{2,3},{3,2},{4,5},{5,4},{6,7},{7,6},{8,9},{9,8},{10,11... | collective-permute-start | bytes 1572872 | tf_op jit(solution)/shard_map/ppermute | solution.py:95
  163.3 2.3 %copy-start.4 = (f32[32,256]{1,0:T(8,128)S(1)}, f32[32,256]{1,0:T(8,128)}, u32[]{:S(2)}) copy-start(f32[32,256]{1,0:T(8,128)} %copy-done.3) | copy-start | bytes 98308
  168.8 1.8 %copy-start.2 = (f32[16,8192]{1,0:T(8,128)S(1)}, f32[16,8192]{1,0:T(8,128)}, u32[]{:S(2)}) copy-start(f32[16,8192]{1,0:T(8,128)} %reshape.88) | copy-start | bytes 1572868
  168.8 1.8 %copy-start.5 = (f32[32,256]{1,0:T(8,128)S(1)}, f32[32,256]{1,0:T(8,128)}, u32[]{:S(2)}) copy-start(f32[32,256]{1,0:T(8,128)} %copy-done.3) | copy-start | bytes 98308

commit v3 on v0

v3 whole, which is shorter than its diff:
```python
import functools
import math

import jax
import jax.numpy as jnp
from jax import lax
from jax.experimental import pallas as pl
from jax.experimental.pallas import tpu as pltpu
from jax.sharding import Mesh, PartitionSpec as P

CLIPPING = 0.2
BETA = 0.9
HIGHEST = lax.Precision.HIGHEST
LANES = 128
SUB = 8
F32 = jnp.float32
BF16 = jnp.bfloat16

T = ("z", "core")
R = ("y", "x")
CHIPS = ("z", "y", "x")

VMEM = pl.BlockSpec(memory_space=pltpu.VMEM)
SMEM = pl.BlockSpec(memory_space=pltpu.SMEM)


def exchange(parts, axes):
    return lax.all_to_all(parts, axes, 0, 0, tiled=True)


def call(kernel, outs, in_specs=None, out_specs=None, flops=0, moved=0, **more):
    outs = [jax.ShapeDtypeStruct(*o) for o in outs]
    return functools.partial(
        pl.pallas_call,
        kernel,
        out_shape=outs,
        out_specs=out_specs or [VMEM] * len(outs),
        cost_estimate=pl.CostEstimate(flops=flops, bytes_accessed=moved, transcendentals=0),
        compiler_params=pltpu.CompilerParams(vmem_limit_bytes=48 * 2**20),
        **more,
    )(in_specs=in_specs)


def iota(shape, axis):
    return lax.broadcasted_iota(jnp.int32, shape, axis)


def nt(a, b, precision=HIGHEST):
    return lax.dot_general(a, b, (((1,), (1,)), ((), ())), precision=precision, preferred_element_type=F32)


def tn(a, b, precision=HIGHEST):
    return lax.dot_general(a, b, (((0,), (0,)), ((), ())), precision=precision, preferred_element_type=F32)


def dot(a, b, precision=HIGHEST):
    return jnp.dot(a, b, precision=precision, preferred_element_type=F32)


def fold_rows(tiled, group):
    n = tiled.shape[0]
    kept = jnp.where(iota(tiled.shape, 0) // group == iota(tiled.shape, 1) // 32, tiled, 0.0)
    out = max(group, SUB)
    pick = (iota((out, n), 1) % group == iota((out, n), 0)).astype(F32)
    return dot(pick, kept)


def first_kernel(t_ref, x_ref, c_ref, e_ref, q_ref, send_ref, pe_ref):
    n_t, rows, _ = send_ref.shape
    tokens, wide = x_ref.shape
    start = pl.multiple_of(t_ref[0] * wide, wide)
    y = nt(q_ref[:, pl.ds(start, wide)], x_ref[...].astype(F32))
    c = c_ref[...].astype(F32)
    for k in range(n_t):
        send_ref[k, :, :wide] = e_ref[:, k * wide : (k + 1) * wide]
        send_ref[k, :, wide : wide + tokens] = c
        for g in range(y.shape[0] // rows):
            at = wide + tokens + g * tokens
            send_ref[k, :, at : at + tokens] = y[g * rows : (g + 1) * rows]
    pe_ref[...] = nt(e_ref[...], q_ref[...])


def merge_kernel(got_ref, x_ref, c_ref, pe_ref, send_ref, cot_ref):
    n_t, rows, _ = got_ref.shape
    tokens, wide = x_ref.shape
    n_r = send_ref.shape[0]
    group = LANES // n_r
    ff_win = n_t * rows
    cot = got_ref[:, :, wide : wide + tokens].reshape(ff_win, tokens).astype(BF16)
    cot_ref[...] = cot
    y = jnp.sum(got_ref[:, :, wide + tokens :], 0)
    folds = y.shape[1] // tokens
    y = jnp.concatenate([y[:, g * tokens : (g + 1) * tokens] for g in range(folds)], 0)
    rank = y.shape[0]
    y4 = jnp.concatenate([y] * (LANES // rank), 0)
    tile = (iota((rank, LANES), 1) % rank == iota((rank, LANES), 0)).astype(F32)
    p4 = nt(c_ref[...].astype(F32), y4) + dot(pe_ref[...], tile)
    p_pack = fold_rows(p4, rows // 4)

    merged = got_ref[:, :, :wide].reshape(ff_win, wide) + dot(cot, x_ref[...], None)
    out, col = iota((wide, wide), 0), iota((wide, wide), 1)
    own = wide // n_r
    r, b, a = out // own, out % own // group, out % group
    turn = (col == b * LANES + r * group + a).astype(BF16)
    turned = jnp.zeros((wide, ff_win), F32)
    rest = merged
    for _ in range(3):
        piece = rest.astype(BF16)
        turned += nt(turn, piece, None)
        rest -= piece.astype(F32)
    halves = ff_win // LANES if ff_win >= LANES else 1
    width = ff_win // halves
    for k in range(n_r):
        for h in range(halves):
            send_ref[k, h * own : (h + 1) * own, :width] = turned[
                k * own : (k + 1) * own, h * width : (h + 1) * width
            ]
        send_ref[k, halves * own :, :] = p_pack[: send_ref.shape[1] - halves * own]


def rows_kernel(cot_ref, x_ref, send_ref):
    n_t = send_ref.shape[0]
    rows = cot_ref.shape[0] // n_t
    grad = dot(cot_ref[...], x_ref[...], None)
    for k in range(n_t):
        for b in range(grad.shape[1] // LANES):
            send_ref[k, b * rows : (b + 1) * rows, :] = grad[
                k * rows : (k + 1) * rows, b * LANES : (b + 1) * LANES
            ]


def sum_kernel(got_ref, held_ref, total_ref, pack_ref, send_ref, scratch, sem):
    n_r = got_ref.shape[0]
    n_t, tall, _ = send_ref.shape
    own, long = total_ref.shape
    ff_win = long // 2
    rows = ff_win // n_t
    got = jnp.sum(got_ref[...], 0)
    pack = got[got.shape[0] - 4 :]
    pack = jnp.concatenate([pack, jnp.zeros_like(pack)], 0)
    pack_ref[...] = pack
    for k in range(n_t):
        scratch[k] = pack
    copy = pltpu.make_async_copy(scratch, send_ref.at[:, pl.ds(tall - SUB, SUB), :], sem)
    copy.start()
    halves = ff_win // LANES if ff_win >= LANES else 1
    width = ff_win // halves
    total = jnp.zeros(total_ref.shape, F32)
    for h in range(halves):
        unit, lane = iota((width, long), 0) + h * width, iota((width, long), 1)
        t, b, a = unit // rows, unit % rows // 4, unit % 4
        move = (lane == b * (SUB * n_t) + t * SUB + a).astype(F32)
        total += dot(got[h * own : (h + 1) * own, :width], move)
    total_ref[...] = total
    copy.wait()


def factor_kernel(n_r, pack_ref, total_ref, send_ref, gram_ref, inverse_ref):
    n_t = pack_ref.shape[0]
    own = total_ref.shape[0]
    rank = gram_ref.shape[0]
    group = own // 4
    pack = pack_ref[...].reshape(n_t * SUB, LANES)
    gram4 = tn(pack, pack)
    gram = sum(gram4[b * rank : (b + 1) * rank, b * rank : (b + 1) * rank] for b in range(4))
    gram_ref[...] = gram
    row, lane = iota((rank, LANES), 0), iota((rank, LANES), 1)
    work = jnp.concatenate([gram, jnp.zeros((rank, LANES - rank), F32)], 1)
    work = jnp.where(lane == row + rank, 1.0, work)
    for j in range(rank):
        pivot = work[j : j + 1, :]
        factor = work[:, j : j + 1] / work[j : j + 1, j : j + 1]
        work = jnp.where(row > j, work - factor * pivot, work)
    diagonal = jnp.sum(jnp.where(lane == row, work, 0.0), 1, keepdims=True)
    inverse = (work * lax.rsqrt(diagonal))[:, rank : 2 * rank]
    inverse_ref[...] = inverse
    inverse16 = jnp.concatenate([inverse] * 4, 0)
    inverse16 = jnp.concatenate([inverse16] * 4, 1)
    total = total_ref[...]
    span = SUB * n_t
    product = jnp.zeros((own, LANES), F32)
    for b in range(4):
        part = dot(total[:, b * span : (b + 1) * span], pack)
        product = jnp.where(iota(part.shape, 1) // rank == b, part, product)
    q4 = nt(product, inverse16) / n_r
    q_pack = fold_rows(q4, group)[:group]
    send_ref[...] = jnp.broadcast_to(q_pack[None], send_ref.shape)


def last_kernel(limit, core_ref, mine_ref, other_ref, basis_ref, weigh_ref, e_ref, g_ref, m_ref, q_ref, error_ref, momentum_ref, approx):
    n_z = mine_ref.shape[0]
    rows = e_ref.shape[0]
    rank = q_ref.shape[0]
    core = core_ref[0]
    wide = 4 * LANES
    square = (LANES, LANES)
    basis4 = basis_ref[...]
    stack = jnp.concatenate(
        [(iota(square, 0) == iota(square, 1)).astype(F32)]
        + [jnp.where(iota(basis4.shape, 1) // rank == b, basis4, 0.0) for b in range(4)],
        0,
    )
    gram = jnp.zeros(square, F32)
    for z in range(n_z):
        for ref, c in ((mine_ref, core), (other_ref, 1 - core)):
            block = ref[z]
            gram += tn(block, block)
            both = nt(stack, block)
            t = 2 * z + c
            for b in range(4):
                at = pl.ds(pl.multiple_of(t * wide + b * LANES, LANES), LANES)
                near = both[LANES + b * rows : LANES + (b + 1) * rows]
                q_ref[:, at] = both[b * rank : (b + 1) * rank]
                approx[:, at] = near
                error_ref[:, at] = e_ref[:, at] + g_ref[t, b * rows : (b + 1) * rows, :] - near
    total = jnp.sum(gram * weigh_ref[...], keepdims=True)
    scale = jnp.minimum(1.0, limit / jnp.sqrt(total))
    momentum_ref[...] = BETA * m_ref[...] + scale * approx[...]


def body(tokens_x, cotangent, weight, error_fb, momentum, q_prev):
    n_t, n_r, n_z = lax.axis_size(T), lax.axis_size(R), lax.axis_size("z")
    t = lax.axis_index(T)[None]
    core = lax.axis_index("core")[None]
    tokens, wide = tokens_x.shape
    rows, width = weight.shape
    rank = q_prev.shape[0]
    ff_win = rows * n_t
    own = wide // n_r
    group = own // 4
    error = error_fb[0]
    halves = ff_win // LANES if ff_win >= LANES else 1

    first, p_error = call(
        first_kernel,
        [((n_t, rows, wide + tokens + rank // rows * tokens), F32), ((rows, rank), F32)],
        [SMEM, VMEM, VMEM, VMEM, VMEM],
        moved=3 * 2**20,
    )(t, tokens_x, cotangent, error, q_prev)
    first = exchange(first, T)

    tall = wide // LANES * rows + SUB
    second, cot_all = call(
        merge_kernel,
        [((n_r, halves * own + 4, LANES), F32), ((ff_win, tokens), BF16)],
        [VMEM] * 4,
        moved=2 * 2**20,
    )(first, tokens_x, cotangent, p_error)
    (third,) = call(
        rows_kernel, [((n_t, tall, LANES), F32)], [VMEM] * 2, flops=2**25, moved=2**20
    )(cot_all, tokens_x)
    second = exchange(second, R)

    total_t, p_pack, third = call(
        sum_kernel,
        [((own, 2 * ff_win), F32), ((SUB, LANES), F32), (third.shape, F32)],
        [VMEM, pl.BlockSpec(memory_space=pl.ANY)],
        [VMEM, VMEM, pl.BlockSpec(memory_space=pl.ANY)],
        moved=2**20,
        scratch_shapes=[pltpu.VMEM((n_t, SUB, LANES), F32), pltpu.SemaphoreType.DMA(())],
        input_output_aliases={1: 2},
    )(second, third)
    third = exchange(third, T)

    q_send, gram, inverse = call(
        functools.partial(factor_kernel, n_r),
        [((n_r * n_z, group, LANES), F32), ((rank, rank), F32), ((rank, rank), F32)],
        [
            pl.BlockSpec((n_t, SUB, LANES), lambda i: (0, tall // SUB - 1, 0)),
            pl.BlockSpec((own, 2 * ff_win), lambda i: (0, 0)),
        ],
        [
            pl.BlockSpec((n_r * n_z, group, LANES), lambda i: (0, 0, 0)),
            pl.BlockSpec((rank, rank), lambda i: (0, 0)),
            pl.BlockSpec((rank, rank), lambda i: (0, 0)),
        ],
        moved=2**20,
        grid=(1,),
    )(third, total_t)
    mine = exchange(q_send, CHIPS)
    basis_gram = dot(dot(inverse, gram), inverse.T)
    p_rows = p_pack[:4].reshape(4, 4, rank).transpose(1, 0, 2).reshape(rows, rank)
    basis4 = jnp.tile(dot(p_rows, inverse.T), (1, 4))
    square = (LANES, LANES)
    weigh = jnp.where(
        iota(square, 0) // rank == iota(square, 1) // rank, jnp.tile(basis_gram, (4, 4)), 0.0
    )
    weight, mine = lax.optimization_barrier((weight, mine))
    w_cols = exchange(weight.reshape(rows, n_t, wide).transpose(1, 0, 2), T).reshape(ff_win, wide)
    other = lax.ppermute(mine, "core", [(0, 1), (1, 0)])
    blocks = (n_z, LANES, LANES)
    limit = CLIPPING * math.sqrt(ff_win * width)
    q_new, error_new, momentum_new = call(
        functools.partial(last_kernel, limit),
        [((rank, width), F32), ((rows, width), F32), ((rows, width), F32)],
        [SMEM] + [VMEM] * 7,
        flops=2**30,
        moved=5 * 2**20,
        scratch_shapes=[pltpu.VMEM((rows, width), F32)],
    )(core, mine.reshape(blocks), other.reshape(blocks), basis4, weigh, error, third, momentum)

    input_grad = tn(cot_all, w_cols, None).astype(BF16)
    return (input_grad, error_new[None], momentum_new, q_new)


def solution(mesh):
    n_r, n_t = mesh.devices.shape
    x = 4 if n_r > 4 else 2
    split = Mesh(mesh.devices.reshape(n_r // x, x, n_t // 2, 2), (*R, *T))
    placed = (P(R, T), P(T, R), P(T, None), P(R, T, None), P(T, None), P())
    return jax.shard_map(
        body,
        mesh=split,
        in_specs=placed,
        out_specs=(P(R, T), P(R, T, None), P(T, None), P()),
        check_vma=False,
    )
```

time: 509 us -> 154 us (0.30)
  waiting for transfers between devices: 351 us -> 46.7 us
  blocking collectives: 120 us -> 59.9 us
  starting transfers between devices: 0.12 us -> 27.5 us
  between operations: 14.5 us -> 0.77 us
  Pallas kernels: 0 us -> 12.4 us
  other arithmetic: 11.7 us -> 0.13 us
  matrix products: 9.47 us -> 1.27 us
    psum x1 -> x0, waiting for transfers between devices: 265 us -> none  [body(): q_sum = lax.psum(q_part, ('replica', 'tensor'))]
    psum x2 -> x0, blocking collectives: 120 us -> none  [the longest x1 97.1 us: body(): p_sum = lax.psum(placed, ('replica', 'tensor'))]
    all_to_all x0 -> x2, blocking collectives: none -> 59.9 us  [exchange(): return lax.all_to_all(parts, axes, 0, 0, tiled=True)]
    all_gather x1 -> x0, waiting for transfers between devices: 51.3 us -> none  [body(): lax.all_gather(tokens_x, 'tensor', axis=1, tiled=True)]
    all_to_all x0 -> x3, waiting for transfers between devices: none -> 46.7 us  [exchange(): return lax.all_to_all(parts, axes, 0, 0, tiled=True)]
    reduce_scatter x1 -> x0, waiting for transfers between devices: 34.5 us -> none  [body(): lax.psum_scatter(partial_dx, 'tensor', scatter_dimension=1, tiled=True)]
    all_to_all x0 -> x3, starting transfers between devices: none -> 25.5 us  [exchange(): return lax.all_to_all(parts, axes, 0, 0, tiled=True)]
    pallas_call x0 -> x6, Pallas kernels: none -> 12.4 us  [the longest x1 4.34 us: body(): call(functools.partial(factor_kernel, n_r), [((n_r * n_z, group, LANES),...]
  transfers between devices with their start and end apart: 3 -> 4, of which waited for: 3 -> 3; matrix products, arithmetic and copies ran while one was open for 1% -> 1% of each run, Pallas kernels for 0% -> 0%
where the time goes in v3:
time: 154 us
  blocking collectives  59.9 us (39%)
  waiting for transfers between devices  46.7 us (30%)
  starting transfers between devices  27.5 us (18%)
  Pallas kernels  12.4 us (8%)
  local copies, waits for them, and re-layouts  5.19 us (3%)
    all_to_all x2, blocking collectives, exchange(): return lax.all_to_all(parts, axes, 0, 0, tiled=True)  59.9 us
    all_to_all x3, waiting for transfers between devices, exchange(): return lax.all_to_all(parts, axes, 0, 0, tiled=True)  46.7 us
    all_to_all x3, starting transfers between devices, exchange(): return lax.all_to_all(parts, axes, 0, 0, tiled=True)  25.5 us
    pallas_call x1, Pallas kernels, body(): call(functools.partial(factor_kernel, n_r), [((n_r * n_z, group, LANES),...  4.34 us
    pallas_call x1, Pallas kernels, body(): call(functools.partial(last_kernel, limit), [((rank, width), F32), ((rows...  4.09 us
    unnamed x17, local copies, waits for them, and re-layouts  3.94 us
  transfers between devices with their start and end apart: 4, of which 3 were waited for; matrix products, arithmetic and copies ran while one was open for 1% of the time, Pallas kernels for 0%

profile of v3, /device:TPU:1, one launch (start us, length us, event | category | flops | bytes accessed | tf_op | source)
XLA Modules:
  0.0 153.8 jit_solution(13293244223379827938)
XLA Ops:
  0.7 0.7 copy-done.5
  1.3 0.9 copy-done
  2.2 1.2 copy-done.2
  3.5 1.0 copy-done.3
  4.5 1.2 shard_map.93
  5.7 37.5 %all_to_all.25.got_ref = f32[16,16,896]{2,1,0:T(8,128)S(1)} all-to-all(f32[16,16,896]{2,1,0:T(8,128)S(1)} %get-tuple-element.19), channel_id=1, replica_groups=mesh['y'=8,'x'=4,'z'=8,'core'=2] {'z','core'}, dimensions={0} | all-to-all | bytes 1835008 | tf_op jit(solution)/shard_map/all_to_all | solution.py:28
  43.2 2.1 %shard_map.94 = (f32[32,36,128]{2,1,0:T(8,128)}, bf16[256,128]{1,0:T(8,128)(2,1)S(1)}) custom-call(f32[16,16,896]{2,1,0:T(8,128)S(1)} %all_to_all.25.got_ref, bf16[128,512]{1,0:T(8,128)(2,1)S(1)} %copy-done.1, bf16[16,128]{1,0:T(8,128)(2,1)S(1)} %copy-done.5, f32[16,32]{1,0:T(8,128)S(1)} %get-tuple-element.20.pe_ref), custom_call_target="tpu_custom_call" | custom-call | bytes 2097152 | tf_op jit(solution)/shard_map/pallas_call | solution.py:243
  45.3 9.7 %all-to-all-start.1 = ((f32[32,36,128]{2,1,0:T(8,128)}), f32[32,36,128]{2,1,0:T(8,128)S(1)}, u32[]{:S(2)}, u32[]{:S(2)}) async-start(f32[32,36,128]{2,1,0:T(8,128)} %get-tuple-element.22), calls=%async_computation.1 | async-start | bytes 1310720 | tf_op jit(solution)/shard_map/all_to_all | solution.py:28
  54.9 0.2 shard_map.95.held_ref
  55.2 19.9 %all-to-all-done.1.got_ref = f32[32,36,128]{2,1,0:T(8,128)S(1)} async-done(((f32[32,36,128]{2,1,0:T(8,128)}), f32[32,36,128]{2,1,0:T(8,128)S(1)}, u32[]{:S(2)}, u32[]{:S(2)}) %all-to-all-start.1) | async-done | bytes 589856 | tf_op jit(solution)/shard_map/all_to_all | solution.py:28
  75.0 0.5 shard_map.96
  75.5 22.4 %all_to_all.26.pack_ref.g_ref = f32[16,72,128]{2,1,0:T(8,128)S(1)} all-to-all(f32[16,72,128]{2,1,0:T(8,128)S(1)} %get-tuple-element.23), channel_id=1, replica_groups=mesh['y'=8,'x'=4,'z'=8,'core'=2] {'z','core'}, dimensions={0} | all-to-all | bytes 1179648 | tf_op jit(solution)/shard_map/all_to_all | solution.py:28
  97.9 4.3 %shard_map.97 = (f32[256,4,128]{2,1,0:T(4,128)}, f32[32,32]{1,0:T(8,128)S(1)}, f32[32,32]{1,0:T(8,128)S(1)}) custom-call(f32[16,72,128]{2,1,0:T(8,128)S(1)} %all_to_all.26.pack_ref.g_ref, f32[16,512]{1,0:T(8,128)S(1)} %get-tuple-element.24.total_ref), custom_call_target="tpu_custom_call" | custom-call | bytes 1048576 | tf_op jit(solution)/shard_map/pallas_call | solution.py:265
  102.3 9.6 %all-to-all-start.3 = ((f32[256,4,128]{2,1,0:T(4,128)}), f32[256,4,128]{2,1,0:T(4,128)S(1)}, u32[]{:S(2)}, u32[]{:S(2)}) async-start(f32[256,4,128]{2,1,0:T(4,128)} %get-tuple-element.25), calls=%async_computation.3 | async-start | bytes 1048576 | tf_op jit(solution)/shard_map/all_to_all | solution.py:28
  111.9 0.1 reshape.35
  112.0 0.1 fusion.2
  112.1 17.9 %all-to-all-done.3 = f32[256,4,128]{2,1,0:T(4,128)S(1)} async-done(((f32[256,4,128]{2,1,0:T(4,128)}), f32[256,4,128]{2,1,0:T(4,128)S(1)}, u32[]{:S(2)}, u32[]{:S(2)}) %all-to-all-start.3) | async-done | bytes 524320 | tf_op jit(solution)/shard_map/all_to_all | solution.py:28
  130.0 0.1 copy.16
  130.0 0.9 copy.14
  130.9 6.3 %all-to-all-start.4 = ((bf16[16,16,512]{2,1,0:T(8,128)(2,1)}), bf16[16,16,512]{2,1,0:T(8,128)(2,1)S(1)}, u32[]{:S(2)}, u32[]{:S(2)}) async-start(bf16[16,16,512]{2,1,0:T(8,128)(2,1)} %copy.14), calls=%async_computation.4 | async-start | bytes 524288 | tf_op jit(solution)/shard_map/all_to_all | solution.py:28
  137.2 0.1 fusion.3
  137.3 2.0 %collective-permute-start = (f32[256,4,128]{2,1,0:T(4,128)S(1)}, f32[256,4,128]{2,1,0:T(4,128)S(1)}, u32[]{:S(2)}, u32[]{:S(2)}) collective-permute-start(f32[256,4,128]{2,1,0:T(4,128)S(1)} %all-to-all-done.3), channel_id=1, source_target_pairs={{0,1},{1,0},{2,3},{3,2},{4,5},{5,4},{6,7},{7,6},{8,9},{9,8},{10,11... | collective-permute-start | bytes 1572872 | tf_op jit(solution)/shard_map/ppermute | solution.py:290
  139.3 0.1 fusion.1
  139.4 0.1 tile.20
  139.5 0.0 copy-start.4
  139.5 0.2 tile.21
  139.7 0.1 tile.9.basis_ref
  139.8 0.1 fusion.weigh_ref
  139.9 9.0 %all-to-all-done.4 = bf16[16,16,512]{2,1,0:T(8,128)(2,1)S(1)} async-done(((bf16[16,16,512]{2,1,0:T(8,128)(2,1)}), bf16[16,16,512]{2,1,0:T(8,128)(2,1)S(1)}, u32[]{:S(2)}, u32[]{:S(2)}) %all-to-all-start.4) | async-done | bytes 262176 | tf_op jit(solution)/shard_map/all_to_all | solution.py:28
  148.9 0.9 convolution_convert_fusion
  149.7 0.0 collective-permute-done
  149.7 4.1 %shard_map.98 = (f32[32,8192]{1,0:T(8,128)}, f32[16,8192]{1,0:T(8,128)}, f32[16,8192]{1,0:T(8,128)}) custom-call(s32[1]{0:T(128)} %bitcast.4.core_ref, f32[8,128,128]{2,1,0:T(8,128)S(1)} %bitcast.24, f32[8,128,128]{2,1,0:T(8,128)S(1)} %bitcast.25, f32[16,128]{1,0:T(8,128)S(1)} %tile.9.basis_ref, f32[128,128]{1,0:T(8,128)S(1)} %fusion.weigh_ref, ...), custom_call_target="tpu_custom_call" | custom-call | flops 1073741824 | bytes 5242880 | tf_op jit(solution)/shard_map/pallas_call | solution.py:293
  (16 shorter events, 0.0 us)
Async XLA Ops:
  0.6 0.7 copy-start.5
  1.3 0.9 copy-start
  2.2 1.2 copy-start.2
  3.5 1.0 copy-start.3
  5.7 37.5 %copy-start.1 = (bf16[128,512]{1,0:T(8,128)(2,1)S(1)}, bf16[128,512]{1,0:T(8,128)(2,1)}, u32[]{:S(2)}) copy-start(bf16[128,512]{1,0:T(8,128)(2,1)} %x_ref.5) | copy-start | bytes 393220
  45.3 29.8 %all-to-all-start.1 = ((f32[32,36,128]{2,1,0:T(8,128)}), f32[32,36,128]{2,1,0:T(8,128)S(1)}, u32[]{:S(2)}, u32[]{:S(2)}) async-start(f32[32,36,128]{2,1,0:T(8,128)} %get-tuple-element.22), calls=%async_computation.1 | async-start | bytes 1310720 | tf_op jit(solution)/shard_map/all_to_all | solution.py:28
  102.2 27.7 %copy-start.7 = (bf16[16,8192]{1,0:T(8,128)(2,1)S(1)}, bf16[16,8192]{1,0:T(8,128)(2,1)}, u32[]{:S(2)}) copy-start(bf16[16,8192]{1,0:T(8,128)(2,1)} %param.8) | copy-start | bytes 786436
  102.3 27.7 %all-to-all-start.3 = ((f32[256,4,128]{2,1,0:T(4,128)}), f32[256,4,128]{2,1,0:T(4,128)S(1)}, u32[]{:S(2)}, u32[]{:S(2)}) async-start(f32[256,4,128]{2,1,0:T(4,128)} %get-tuple-element.25), calls=%async_computation.3 | async-start | bytes 1048576 | tf_op jit(solution)/shard_map/all_to_all | solution.py:28
  130.9 18.0 %all-to-all-start.4 = ((bf16[16,16,512]{2,1,0:T(8,128)(2,1)}), bf16[16,16,512]{2,1,0:T(8,128)(2,1)S(1)}, u32[]{:S(2)}, u32[]{:S(2)}) async-start(bf16[16,16,512]{2,1,0:T(8,128)(2,1)} %copy.14), calls=%async_computation.4 | async-start | bytes 524288 | tf_op jit(solution)/shard_map/all_to_all | solution.py:28
  137.3 12.4 %collective-permute-start = (f32[256,4,128]{2,1,0:T(4,128)S(1)}, f32[256,4,128]{2,1,0:T(4,128)S(1)}, u32[]{:S(2)}, u32[]{:S(2)}) collective-permute-start(f32[256,4,128]{2,1,0:T(4,128)S(1)} %all-to-all-done.3), channel_id=1, source_target_pairs={{0,1},{1,0},{2,3},{3,2},{4,5},{5,4},{6,7},{7,6},{8,9},{9,8},{10,11... | collective-permute-start | bytes 1572872 | tf_op jit(solution)/shard_map/ppermute | solution.py:290
  139.4 10.3 %copy-start.6 = (f32[16,8192]{1,0:T(8,128)S(1)}, f32[16,8192]{1,0:T(8,128)}, u32[]{:S(2)}) copy-start(f32[16,8192]{1,0:T(8,128)} %m_ref.1) | copy-start | bytes 1572868
  139.5 10.2 %copy-start.4 = (f32[1,16,8192]{2,1,0:T(8,128)S(1)}, f32[1,16,8192]{2,1,0:T(8,128)}, u32[]{:S(2)}) copy-start(f32[1,16,8192]{2,1,0:T(8,128)} %param.9) | copy-start | bytes 1572868

commit v4 on v3

--- a/solution.py
+++ b/solution.py
@@ -22,13 +22,14 @@
 
 VMEM = pl.BlockSpec(memory_space=pltpu.VMEM)
 SMEM = pl.BlockSpec(memory_space=pltpu.SMEM)
+HBM = pl.BlockSpec(memory_space=pltpu.HBM)
 
 
 def exchange(parts, axes):
     return lax.all_to_all(parts, axes, 0, 0, tiled=True)
 
 
-def call(kernel, outs, in_specs=None, out_specs=None, flops=0, moved=0, **more):
+def call(kernel, outs, in_specs=None, out_specs=None, flops=0, moved=0, limit=48, **more):
     outs = [jax.ShapeDtypeStruct(*o) for o in outs]
     return functools.partial(
         pl.pallas_call,
@@ -36,7 +37,7 @@
         out_shape=outs,
         out_specs=out_specs or [VMEM] * len(outs),
         cost_estimate=pl.CostEstimate(flops=flops, bytes_accessed=moved, transcendentals=0),
-        compiler_params=pltpu.CompilerParams(vmem_limit_bytes=48 * 2**20),
+        compiler_params=pltpu.CompilerParams(vmem_limit_bytes=limit and limit * 2**20),
         **more,
     )(in_specs=in_specs)
 
@@ -65,18 +66,37 @@
     return dot(pick, kept)
 
 
-def first_kernel(t_ref, x_ref, c_ref, e_ref, q_ref, send_ref, pe_ref):
+def first_kernel(t_ref, x_ref, c_ref, e_ref, q_ref, send_ref, x, c, q, sems):
     n_t, rows, _ = send_ref.shape
     tokens, wide = x_ref.shape
     start = pl.multiple_of(t_ref[0] * wide, wide)
-    y = nt(q_ref[:, pl.ds(start, wide)], x_ref[...].astype(F32))
-    c = c_ref[...].astype(F32)
+    copies = [
+        pltpu.make_async_copy(q_ref.at[:, pl.ds(start, wide)], q, sems.at[0]),
+        pltpu.make_async_copy(x_ref, x, sems.at[1]),
+        pltpu.make_async_copy(c_ref, c, sems.at[2]),
+    ]
     for k in range(n_t):
-        send_ref[k, :, :wide] = e_ref[:, k * wide : (k + 1) * wide]
-        send_ref[k, :, wide : wide + tokens] = c
+        copies.append(
+            pltpu.make_async_copy(
+                e_ref.at[:, pl.ds(k * wide, wide)], send_ref.at[k, :, pl.ds(0, wide)], sems.at[3 + k]
+            )
+        )
+    for copy in copies:
+        copy.start()
+    for copy in copies[:3]:
+        copy.wait()
+    y = nt(q[...], x[...].astype(F32))
+    cot = c[...].astype(F32)
+    for k in range(n_t):
+        send_ref[k, :, wide : wide + tokens] = cot
         for g in range(y.shape[0] // rows):
             at = wide + tokens + g * tokens
             send_ref[k, :, at : at + tokens] = y[g * rows : (g + 1) * rows]
+    for copy in copies[3:]:
+        copy.wait()
+
+
+def project_kernel(e_ref, q_ref, pe_ref):
     pe_ref[...] = nt(e_ref[...], q_ref[...])
 
 
@@ -231,12 +251,24 @@
     error = error_fb[0]
     halves = ff_win // LANES if ff_win >= LANES else 1
 
-    first, p_error = call(
+    (first,) = call(
         first_kernel,
-        [((n_t, rows, wide + tokens + rank // rows * tokens), F32), ((rows, rank), F32)],
-        [SMEM, VMEM, VMEM, VMEM, VMEM],
+        [((n_t, rows, wide + tokens + rank // rows * tokens), F32)],
+        [SMEM] + [HBM] * 4,
         moved=3 * 2**20,
+        limit=None,
+        scratch_shapes=[
+            pltpu.VMEM(tokens_x.shape, BF16),
+            pltpu.VMEM(cotangent.shape, BF16),
+            pltpu.VMEM((rank, wide), F32),
+            pltpu.SemaphoreType.DMA((3 + n_t,)),
+        ],
     )(t, tokens_x, cotangent, error, q_prev)
+    w_parts = weight.reshape(rows, n_t, wide).transpose(1, 0, 2)
+    first, error_late = lax.optimization_barrier((first, error))
+    (p_error,) = call(
+        project_kernel, [((rows, rank), F32)], [VMEM] * 2, flops=2**27, moved=2 * 2**20
+    )(error_late, q_prev)
     first = exchange(first, T)
 
     tall = wide // LANES * rows + SUB
@@ -285,8 +317,8 @@
     weigh = jnp.where(
         iota(square, 0) // rank == iota(square, 1) // rank, jnp.tile(basis_gram, (4, 4)), 0.0
     )
-    weight, mine = lax.optimization_barrier((weight, mine))
-    w_cols = exchange(weight.reshape(rows, n_t, wide).transpose(1, 0, 2), T).reshape(ff_win, wide)
+    w_parts, mine = lax.optimization_barrier((w_parts, mine))
+    w_cols = exchange(w_parts, T).reshape(ff_win, wide)
     other = lax.ppermute(mine, "core", [(0, 1), (1, 0)])
     blocks = (n_z, LANES, LANES)
     limit = CLIPPING * math.sqrt(ff_win * width)
@@ -299,6 +331,7 @@
         scratch_shapes=[pltpu.VMEM((rows, width), F32)],
     )(core, mine.reshape(blocks), other.reshape(blocks), basis4, weigh, error, third, momentum)
 
+    cot_all, q_new = lax.optimization_barrier((cot_all, q_new))
     input_grad = tn(cot_all, w_cols, None).astype(BF16)
     return (input_grad, error_new[None], momentum_new, q_new)
 

time: 154 us -> 150 us (0.974)
  blocking collectives: 59.9 us -> 23.1 us
  waiting for transfers between devices: 46.7 us -> 68.3 us
  starting transfers between devices: 27.5 us -> 39.3 us
  local copies, waits for them, and re-layouts: 5.19 us -> 1.89 us
  Pallas kernels: 12.4 us -> 14.6 us
    all_to_all x2 -> x1, blocking collectives: 59.9 us -> 23.1 us  [exchange(): return lax.all_to_all(parts, axes, 0, 0, tiled=True)]
    all_to_all x3 -> x4, waiting for transfers between devices: 46.7 us -> 68.3 us  [exchange(): return lax.all_to_all(parts, axes, 0, 0, tiled=True)]
    all_to_all x3 -> x4, starting transfers between devices: 25.5 us -> 35.1 us  [exchange(): return lax.all_to_all(parts, axes, 0, 0, tiled=True)]
    unnamed x17 -> x13, local copies, waits for them, and re-layouts: 3.94 us -> 0.65 us
    ppermute x1, starting transfers between devices: 2.01 us -> 4.2 us  [body(): other = lax.ppermute(mine, 'core', [(0, 1), (1, 0)])]
  transfers between devices with their start and end apart: 4 -> 5, of which waited for: 3 -> 4; matrix products, arithmetic and copies ran while one was open for 1% -> 1% of each run, Pallas kernels for 0% -> 3%
where the time goes in v4:
time: 150 us; the launch traced here: 149 us
  waiting for transfers between devices  68.3 us (46%)
  starting transfers between devices  39.3 us (26%)
  blocking collectives  23.1 us (15%)
  Pallas kernels  14.6 us (10%)
  local copies, waits for them, and re-layouts  1.89 us (1%)
    all_to_all x4, waiting for transfers between devices, exchange(): return lax.all_to_all(parts, axes, 0, 0, tiled=True)  68.3 us
    all_to_all x4, starting transfers between devices, exchange(): return lax.all_to_all(parts, axes, 0, 0, tiled=True)  35.1 us
    all_to_all x1, blocking collectives, exchange(): return lax.all_to_all(parts, axes, 0, 0, tiled=True)  23.1 us
    pallas_call x1, Pallas kernels, body(): call(functools.partial(factor_kernel, n_r), [((n_r * n_z, group, LANES),...  4.34 us
    ppermute x1, starting transfers between devices, body(): other = lax.ppermute(mine, 'core', [(0, 1), (1, 0)])  4.2 us
    pallas_call x1, Pallas kernels, body(): call(functools.partial(last_kernel, limit), [((rank, width), F32), ((rows...  4.06 us
  transfers between devices with their start and end apart: 5, of which 4 were waited for; matrix products, arithmetic and copies ran while one was open for 1% of the time, Pallas kernels for 3%

profile of v4, /device:TPU:1, one launch (start us, length us, event | category | flops | bytes accessed | tf_op | source)
XLA Modules:
  0.0 149.4 jit_solution(185082208665283543)
XLA Ops:
  0.6 2.4 %shard_map.93 = f32[16,16,896]{2,1,0:T(8,128)} custom-call(s32[1]{0:T(128)} %bitcast.t_ref, bf16[128,512]{1,0:T(8,128)(2,1)} %x_ref.5, bf16[16,128]{1,0:T(8,128)(2,1)} %c_ref.3, f32[16,8192]{1,0:T(8,128)} %bitcast.22, f32[32,8192]{1,0:T(8,128)} %q_ref.3), custom_call_target="tpu_custom_call" | custom-call | bytes 3145728 | tf_op jit(solution)/shard_map/pallas_call | solution.py:254
  3.1 0.0 copy-start
  3.1 0.0 copy-start.1
  3.1 12.0 %all-to-all-start = ((f32[16,16,896]{2,1,0:T(8,128)}), f32[16,16,896]{2,1,0:T(8,128)S(1)}, u32[]{:S(2)}, u32[]{:S(2)}) async-start(f32[16,16,896]{2,1,0:T(8,128)} %shard_map.93), calls=%async_computation | async-start | bytes 1835008 | tf_op jit(solution)/shard_map/all_to_all | solution.py:29
  15.1 0.0 copy-start.2
  15.1 0.0 copy-start.3
  15.1 0.9 shard_map.94.pe_ref
  16.1 24.3 %all-to-all-done.got_ref = f32[16,16,896]{2,1,0:T(8,128)S(1)} async-done(((f32[16,16,896]{2,1,0:T(8,128)}), f32[16,16,896]{2,1,0:T(8,128)S(1)}, u32[]{:S(2)}, u32[]{:S(2)}) %all-to-all-start) | async-done | bytes 917536 | tf_op jit(solution)/shard_map/all_to_all | solution.py:29
  40.4 2.1 %shard_map.95 = (f32[32,36,128]{2,1,0:T(8,128)}, bf16[256,128]{1,0:T(8,128)(2,1)S(1)}) custom-call(f32[16,16,896]{2,1,0:T(8,128)S(1)} %all-to-all-done.got_ref, bf16[128,512]{1,0:T(8,128)(2,1)S(1)} %copy-done.2, bf16[16,128]{1,0:T(8,128)(2,1)S(1)} %copy-done.3, f32[16,32]{1,0:T(8,128)S(1)} %shard_map.94.pe_ref), custom_call_target="tpu_custom_call" | custom-call | bytes 2097152 | tf_op jit(solution)/shard_map/pallas_call | solution.py:275
  42.5 9.7 %all-to-all-start.1 = ((f32[32,36,128]{2,1,0:T(8,128)}), f32[32,36,128]{2,1,0:T(8,128)S(1)}, u32[]{:S(2)}, u32[]{:S(2)}) async-start(f32[32,36,128]{2,1,0:T(8,128)} %get-tuple-element.24), calls=%async_computation.1 | async-start | bytes 1310720 | tf_op jit(solution)/shard_map/all_to_all | solution.py:29
  52.2 0.2 shard_map.96.held_ref
  52.4 19.6 %all-to-all-done.1.got_ref = f32[32,36,128]{2,1,0:T(8,128)S(1)} async-done(((f32[32,36,128]{2,1,0:T(8,128)}), f32[32,36,128]{2,1,0:T(8,128)S(1)}, u32[]{:S(2)}, u32[]{:S(2)}) %all-to-all-start.1) | async-done | bytes 589856 | tf_op jit(solution)/shard_map/all_to_all | solution.py:29
  71.9 0.5 shard_map.97
  72.5 23.1 %all_to_all.25.pack_ref.g_ref = f32[16,72,128]{2,1,0:T(8,128)S(1)} all-to-all(f32[16,72,128]{2,1,0:T(8,128)S(1)} %get-tuple-element.25), channel_id=1, replica_groups=mesh['y'=8,'x'=4,'z'=8,'core'=2] {'z','core'}, dimensions={0} | all-to-all | bytes 1179648 | tf_op jit(solution)/shard_map/all_to_all | solution.py:29
  95.6 4.3 %shard_map.98 = (f32[256,4,128]{2,1,0:T(4,128)}, f32[32,32]{1,0:T(8,128)S(1)}, f32[32,32]{1,0:T(8,128)S(1)}) custom-call(f32[16,72,128]{2,1,0:T(8,128)S(1)} %all_to_all.25.pack_ref.g_ref, f32[16,512]{1,0:T(8,128)S(1)} %get-tuple-element.26.total_ref), custom_call_target="tpu_custom_call" | custom-call | bytes 1048576 | tf_op jit(solution)/shard_map/pallas_call | solution.py:297
  99.9 9.5 %all-to-all-start.3 = ((f32[256,4,128]{2,1,0:T(4,128)}), f32[256,4,128]{2,1,0:T(4,128)S(1)}, u32[]{:S(2)}, u32[]{:S(2)}) async-start(f32[256,4,128]{2,1,0:T(4,128)} %get-tuple-element.27), calls=%async_computation.3 | async-start | bytes 1048576 | tf_op jit(solution)/shard_map/all_to_all | solution.py:29
  109.4 0.1 copy.16
  109.5 0.1 reshape.34
  109.6 0.1 fusion.2
  109.7 17.8 %all-to-all-done.3 = f32[256,4,128]{2,1,0:T(4,128)S(1)} async-done(((f32[256,4,128]{2,1,0:T(4,128)}), f32[256,4,128]{2,1,0:T(4,128)S(1)}, u32[]{:S(2)}, u32[]{:S(2)}) %all-to-all-start.3) | async-done | bytes 524320 | tf_op jit(solution)/shard_map/all_to_all | solution.py:29
  127.6 4.2 %collective-permute-start = (f32[256,4,128]{2,1,0:T(4,128)S(1)}, f32[256,4,128]{2,1,0:T(4,128)S(1)}, u32[]{:S(2)}, u32[]{:S(2)}) collective-permute-start(f32[256,4,128]{2,1,0:T(4,128)S(1)} %all-to-all-done.3), channel_id=1, source_target_pairs={{0,1},{1,0},{2,3},{3,2},{4,5},{5,4},{6,7},{7,6},{8,9},{9,8},{10,11... | collective-permute-start | bytes 1572872 | tf_op jit(solution)/shard_map/ppermute | solution.py:322
  131.8 0.1 fusion.1
  131.9 0.1 tile.9.basis_ref
  132.0 0.8 copy.15
  132.8 4.0 %all-to-all-start.4 = ((bf16[16,16,512]{2,1,0:T(8,128)(2,1)}), bf16[16,16,512]{2,1,0:T(8,128)(2,1)S(1)}, u32[]{:S(2)}, u32[]{:S(2)}) async-start(bf16[16,16,512]{2,1,0:T(8,128)(2,1)} %copy.15), calls=%async_computation.4 | async-start | bytes 524288 | tf_op jit(solution)/shard_map/all_to_all | solution.py:29
  136.9 0.1 fusion.3
  137.1 0.2 tile.21
  137.2 0.1 fusion.weigh_ref
  137.4 0.5 copy-done.4
  137.9 4.1 %shard_map.99 = (f32[32,8192]{1,0:T(8,128)}, f32[16,8192]{1,0:T(8,128)}, f32[16,8192]{1,0:T(8,128)}) custom-call(s32[1]{0:T(128)} %bitcast.2.core_ref, f32[8,128,128]{2,1,0:T(8,128)S(1)} %bitcast.25, f32[8,128,128]{2,1,0:T(8,128)S(1)} %bitcast.26, f32[16,128]{1,0:T(8,128)S(1)} %tile.9.basis_ref, f32[128,128]{1,0:T(8,128)S(1)} %fusion.weigh_ref, ...), custom_call_target="tpu_custom_call" | custom-call | flops 1073741824 | bytes 5242880 | tf_op jit(solution)/shard_map/pallas_call | solution.py:325
  142.0 6.6 %all-to-all-done.4 = bf16[16,16,512]{2,1,0:T(8,128)(2,1)S(1)} async-done(((bf16[16,16,512]{2,1,0:T(8,128)(2,1)}), bf16[16,16,512]{2,1,0:T(8,128)(2,1)S(1)}, u32[]{:S(2)}, u32[]{:S(2)}) %all-to-all-start.4) | async-done | bytes 262176 | tf_op jit(solution)/shard_map/all_to_all | solution.py:29
  148.6 0.9 convolution_convert_fusion
  (14 shorter events, 0.1 us)
Async XLA Ops:
  3.1 12.0 %copy-start = (f32[32,8192]{1,0:T(8,128)S(1)}, f32[32,8192]{1,0:T(8,128)}, u32[]{:S(2)}) copy-start(f32[32,8192]{1,0:T(8,128)} %q_ref.3) | copy-start | bytes 3145732
  3.1 12.0 %copy-start.1 = (f32[1,16,8192]{2,1,0:T(8,128)S(1)}, f32[1,16,8192]{2,1,0:T(8,128)}, u32[]{:S(2)}) copy-start(f32[1,16,8192]{2,1,0:T(8,128)} %param.9) | copy-start | bytes 1572868
  3.1 37.3 %all-to-all-start = ((f32[16,16,896]{2,1,0:T(8,128)}), f32[16,16,896]{2,1,0:T(8,128)S(1)}, u32[]{:S(2)}, u32[]{:S(2)}) async-start(f32[16,16,896]{2,1,0:T(8,128)} %shard_map.93), calls=%async_computation | async-start | bytes 1835008 | tf_op jit(solution)/shard_map/all_to_all | solution.py:29
  15.1 25.3 %copy-start.2 = (bf16[128,512]{1,0:T(8,128)(2,1)S(1)}, bf16[128,512]{1,0:T(8,128)(2,1)}, u32[]{:S(2)}) copy-start(bf16[128,512]{1,0:T(8,128)(2,1)} %x_ref.5) | copy-start | bytes 393220
  15.1 25.3 %copy-start.3 = (bf16[16,128]{1,0:T(8,128)(2,1)S(1)}, bf16[16,128]{1,0:T(8,128)(2,1)}, u32[]{:S(2)}) copy-start(bf16[16,128]{1,0:T(8,128)(2,1)} %c_ref.3) | copy-start | bytes 12292
  42.5 29.5 %all-to-all-start.1 = ((f32[32,36,128]{2,1,0:T(8,128)}), f32[32,36,128]{2,1,0:T(8,128)S(1)}, u32[]{:S(2)}, u32[]{:S(2)}) async-start(f32[32,36,128]{2,1,0:T(8,128)} %get-tuple-element.24), calls=%async_computation.1 | async-start | bytes 1310720 | tf_op jit(solution)/shard_map/all_to_all | solution.py:29
  99.9 9.5 %copy-start.5 = (bf16[16,8192]{1,0:T(8,128)(2,1)S(1)}, bf16[16,8192]{1,0:T(8,128)(2,1)}, u32[]{:S(2)}) copy-start(bf16[16,8192]{1,0:T(8,128)(2,1)} %param.8) | copy-start | bytes 786436
  99.9 27.6 %all-to-all-start.3 = ((f32[256,4,128]{2,1,0:T(4,128)}), f32[256,4,128]{2,1,0:T(4,128)S(1)}, u32[]{:S(2)}, u32[]{:S(2)}) async-start(f32[256,4,128]{2,1,0:T(4,128)} %get-tuple-element.27), calls=%async_computation.3 | async-start | bytes 1048576 | tf_op jit(solution)/shard_map/all_to_all | solution.py:29
  127.6 9.8 %collective-permute-start = (f32[256,4,128]{2,1,0:T(4,128)S(1)}, f32[256,4,128]{2,1,0:T(4,128)S(1)}, u32[]{:S(2)}, u32[]{:S(2)}) collective-permute-start(f32[256,4,128]{2,1,0:T(4,128)S(1)} %all-to-all-done.3), channel_id=1, source_target_pairs={{0,1},{1,0},{2,3},{3,2},{4,5},{5,4},{6,7},{7,6},{8,9},{9,8},{10,11... | collective-permute-start | bytes 1572872 | tf_op jit(solution)/shard_map/ppermute | solution.py:322
  132.8 15.7 %all-to-all-start.4 = ((bf16[16,16,512]{2,1,0:T(8,128)(2,1)}), bf16[16,16,512]{2,1,0:T(8,128)(2,1)S(1)}, u32[]{:S(2)}, u32[]{:S(2)}) async-start(bf16[16,16,512]{2,1,0:T(8,128)(2,1)} %copy.15), calls=%async_computation.4 | async-start | bytes 524288 | tf_op jit(solution)/shard_map/all_to_all | solution.py:29
  136.9 1.0 copy-start.4

commit v5 on v4

--- a/solution.py
+++ b/solution.py
@@ -66,58 +66,55 @@
     return dot(pick, kept)
 
 
-def first_kernel(t_ref, x_ref, c_ref, e_ref, q_ref, send_ref, x, c, q, sems):
-    n_t, rows, _ = send_ref.shape
-    tokens, wide = x_ref.shape
+def cut_kernel(e_ref, send_ref, sems):
+    n_t, _, wide = send_ref.shape
+    copies = [
+        pltpu.make_async_copy(e_ref.at[:, pl.ds(k * wide, wide)], send_ref.at[k], sems.at[k])
+        for k in range(n_t)
+    ]
+    for copy in copies:
+        copy.start()
+    for copy in copies:
+        copy.wait()
+
+
+def share_kernel(t_ref, x_ref, c_ref, q_ref, send_ref, x, c, q, sems):
+    rows, tokens = c_ref.shape
+    wide = x_ref.shape[1]
     start = pl.multiple_of(t_ref[0] * wide, wide)
     copies = [
         pltpu.make_async_copy(q_ref.at[:, pl.ds(start, wide)], q, sems.at[0]),
         pltpu.make_async_copy(x_ref, x, sems.at[1]),
         pltpu.make_async_copy(c_ref, c, sems.at[2]),
     ]
-    for k in range(n_t):
-        copies.append(
-            pltpu.make_async_copy(
-                e_ref.at[:, pl.ds(k * wide, wide)], send_ref.at[k, :, pl.ds(0, wide)], sems.at[3 + k]
-            )
-        )
     for copy in copies:
         copy.start()
-    for copy in copies[:3]:
+    for copy in copies:
         copy.wait()
-    y = nt(q[...], x[...].astype(F32))
-    cot = c[...].astype(F32)
-    for k in range(n_t):
-        send_ref[k, :, wide : wide + tokens] = cot
-        for g in range(y.shape[0] // rows):
-            at = wide + tokens + g * tokens
-            send_ref[k, :, at : at + tokens] = y[g * rows : (g + 1) * rows]
-    for copy in copies[3:]:
-        copy.wait()
+    send_ref[:rows] = c[...].astype(F32)
+    send_ref[rows:] = nt(q[...], x[...].astype(F32))
 
 
 def project_kernel(e_ref, q_ref, pe_ref):
     pe_ref[...] = nt(e_ref[...], q_ref[...])
 
 
-def merge_kernel(got_ref, x_ref, c_ref, pe_ref, send_ref, cot_ref):
+def merge_kernel(got_ref, all_ref, x_ref, c_ref, pe_ref, send_ref, cot_ref):
     n_t, rows, _ = got_ref.shape
     tokens, wide = x_ref.shape
     n_r = send_ref.shape[0]
     group = LANES // n_r
     ff_win = n_t * rows
-    cot = got_ref[:, :, wide : wide + tokens].reshape(ff_win, tokens).astype(BF16)
+    cot = all_ref[:, :rows, :].reshape(ff_win, tokens).astype(BF16)
     cot_ref[...] = cot
-    y = jnp.sum(got_ref[:, :, wide + tokens :], 0)
-    folds = y.shape[1] // tokens
-    y = jnp.concatenate([y[:, g * tokens : (g + 1) * tokens] for g in range(folds)], 0)
+    y = jnp.sum(all_ref[:, rows:, :], 0)
     rank = y.shape[0]
     y4 = jnp.concatenate([y] * (LANES // rank), 0)
     tile = (iota((rank, LANES), 1) % rank == iota((rank, LANES), 0)).astype(F32)
     p4 = nt(c_ref[...].astype(F32), y4) + dot(pe_ref[...], tile)
     p_pack = fold_rows(p4, rows // 4)
 
-    merged = got_ref[:, :, :wide].reshape(ff_win, wide) + dot(cot, x_ref[...], None)
+    merged = got_ref[...].reshape(ff_win, wide) + dot(cot, x_ref[...], None)
     out, col = iota((wide, wide), 0), iota((wide, wide), 1)
     own = wide // n_r
     r, b, a = out // own, out % own // group, out % group
@@ -138,31 +135,22 @@
         send_ref[k, halves * own :, :] = p_pack[: send_ref.shape[1] - halves * own]
 
 
-def rows_kernel(cot_ref, x_ref, send_ref):
-    n_t = send_ref.shape[0]
-    rows = cot_ref.shape[0] // n_t
+def rows_kernel(cot_ref, x_ref, w_ref, send_ref):
+    n_t, rows, _ = send_ref.shape
+    wide = x_ref.shape[1]
     grad = dot(cot_ref[...], x_ref[...], None)
     for k in range(n_t):
-        for b in range(grad.shape[1] // LANES):
-            send_ref[k, b * rows : (b + 1) * rows, :] = grad[
-                k * rows : (k + 1) * rows, b * LANES : (b + 1) * LANES
-            ]
-
-
-def sum_kernel(got_ref, held_ref, total_ref, pack_ref, send_ref, scratch, sem):
-    n_r = got_ref.shape[0]
-    n_t, tall, _ = send_ref.shape
+        send_ref[k, :, :wide] = grad[k * rows : (k + 1) * rows]
+        send_ref[k, :, wide:] = w_ref[:, k * wide : (k + 1) * wide].astype(F32)
+
+
+def sum_kernel(n_t, got_ref, total_ref, pack_ref):
     own, long = total_ref.shape
     ff_win = long // 2
     rows = ff_win // n_t
     got = jnp.sum(got_ref[...], 0)
     pack = got[got.shape[0] - 4 :]
-    pack = jnp.concatenate([pack, jnp.zeros_like(pack)], 0)
-    pack_ref[...] = pack
-    for k in range(n_t):
-        scratch[k] = pack
-    copy = pltpu.make_async_copy(scratch, send_ref.at[:, pl.ds(tall - SUB, SUB), :], sem)
-    copy.start()
+    pack_ref[...] = jnp.concatenate([pack, jnp.zeros_like(pack)], 0)
     halves = ff_win // LANES if ff_win >= LANES else 1
     width = ff_win // halves
     total = jnp.zeros(total_ref.shape, F32)
@@ -172,15 +160,14 @@
         move = (lane == b * (SUB * n_t) + t * SUB + a).astype(F32)
         total += dot(got[h * own : (h + 1) * own, :width], move)
     total_ref[...] = total
-    copy.wait()
 
 
 def factor_kernel(n_r, pack_ref, total_ref, send_ref, gram_ref, inverse_ref):
-    n_t = pack_ref.shape[0]
+    span = pack_ref.shape[0]
     own = total_ref.shape[0]
     rank = gram_ref.shape[0]
     group = own // 4
-    pack = pack_ref[...].reshape(n_t * SUB, LANES)
+    pack = pack_ref[...]
     gram4 = tn(pack, pack)
     gram = sum(gram4[b * rank : (b + 1) * rank, b * rank : (b + 1) * rank] for b in range(4))
     gram_ref[...] = gram
@@ -197,7 +184,6 @@
     inverse16 = jnp.concatenate([inverse] * 4, 0)
     inverse16 = jnp.concatenate([inverse16] * 4, 1)
     total = total_ref[...]
-    span = SUB * n_t
     product = jnp.zeros((own, LANES), F32)
     for b in range(4):
         part = dot(total[:, b * span : (b + 1) * span], pack)
@@ -232,7 +218,7 @@
                 near = both[LANES + b * rows : LANES + (b + 1) * rows]
                 q_ref[:, at] = both[b * rank : (b + 1) * rank]
                 approx[:, at] = near
-                error_ref[:, at] = e_ref[:, at] + g_ref[t, b * rows : (b + 1) * rows, :] - near
+                error_ref[:, at] = e_ref[:, at] + g_ref[t, :, b * LANES : (b + 1) * LANES] - near
     total = jnp.sum(gram * weigh_ref[...], keepdims=True)
     scale = jnp.minimum(1.0, limit / jnp.sqrt(total))
     momentum_ref[...] = BETA * m_ref[...] + scale * approx[...]
@@ -252,64 +238,66 @@
     halves = ff_win // LANES if ff_win >= LANES else 1
 
     (first,) = call(
-        first_kernel,
-        [((n_t, rows, wide + tokens + rank // rows * tokens), F32)],
-        [SMEM] + [HBM] * 4,
-        moved=3 * 2**20,
+        cut_kernel,
+        [((n_t, rows, wide), F32)],
+        [HBM],
+        moved=2**20,
+        limit=None,
+        scratch_shapes=[pltpu.SemaphoreType.DMA((n_t,))],
+    )(error)
+    (share,) = call(
+        share_kernel,
+        [((rows + rank, tokens), F32)],
+        [SMEM] + [HBM] * 3,
+        flops=2**24,
+        moved=2**19,
         limit=None,
         scratch_shapes=[
             pltpu.VMEM(tokens_x.shape, BF16),
             pltpu.VMEM(cotangent.shape, BF16),
             pltpu.VMEM((rank, wide), F32),
-            pltpu.SemaphoreType.DMA((3 + n_t,)),
+            pltpu.SemaphoreType.DMA((3,)),
         ],
-    )(t, tokens_x, cotangent, error, q_prev)
-    w_parts = weight.reshape(rows, n_t, wide).transpose(1, 0, 2)
+    )(t, tokens_x, cotangent, q_prev)
     first, error_late = lax.optimization_barrier((first, error))
     (p_error,) = call(
         project_kernel, [((rows, rank), F32)], [VMEM] * 2, flops=2**27, moved=2 * 2**20
     )(error_late, q_prev)
     first = exchange(first, T)
-
-    tall = wide // LANES * rows + SUB
+    share = lax.all_gather(share, T)
+
     second, cot_all = call(
         merge_kernel,
         [((n_r, halves * own + 4, LANES), F32), ((ff_win, tokens), BF16)],
-        [VMEM] * 4,
+        [VMEM] * 5,
         moved=2 * 2**20,
-    )(first, tokens_x, cotangent, p_error)
+    )(first, share, tokens_x, cotangent, p_error)
     (third,) = call(
-        rows_kernel, [((n_t, tall, LANES), F32)], [VMEM] * 2, flops=2**25, moved=2**20
-    )(cot_all, tokens_x)
+        rows_kernel, [((n_t, rows, 2 * wide), F32)], [VMEM] * 3, flops=2**25, moved=2**20
+    )(cot_all, tokens_x, weight)
     second = exchange(second, R)
 
-    total_t, p_pack, third = call(
-        sum_kernel,
-        [((own, 2 * ff_win), F32), ((SUB, LANES), F32), (third.shape, F32)],
-        [VMEM, pl.BlockSpec(memory_space=pl.ANY)],
-        [VMEM, VMEM, pl.BlockSpec(memory_space=pl.ANY)],
+    second, third = lax.optimization_barrier((second, third))
+    third = exchange(third, T)
+    total_t, p_pack = call(
+        functools.partial(sum_kernel, n_t),
+        [((own, 2 * ff_win), F32), ((SUB, LANES), F32)],
+        [VMEM],
         moved=2**20,
-        scratch_shapes=[pltpu.VMEM((n_t, SUB, LANES), F32), pltpu.SemaphoreType.DMA(())],
-        input_output_aliases={1: 2},
-    )(second, third)
-    third = exchange(third, T)
+    )(second)
+    p_all = lax.all_gather(p_pack, T, tiled=True)
 
     q_send, gram, inverse = call(
         functools.partial(factor_kernel, n_r),
         [((n_r * n_z, group, LANES), F32), ((rank, rank), F32), ((rank, rank), F32)],
-        [
-            pl.BlockSpec((n_t, SUB, LANES), lambda i: (0, tall // SUB - 1, 0)),
-            pl.BlockSpec((own, 2 * ff_win), lambda i: (0, 0)),
-        ],
-        [
-            pl.BlockSpec((n_r * n_z, group, LANES), lambda i: (0, 0, 0)),
-            pl.BlockSpec((rank, rank), lambda i: (0, 0)),
-            pl.BlockSpec((rank, rank), lambda i: (0, 0)),
-        ],
+        [VMEM] * 2,
+        flops=2**29,
         moved=2**20,
-        grid=(1,),
-    )(third, total_t)
+    )(p_all, total_t)
+    q_send, third = lax.optimization_barrier((q_send, third))
     mine = exchange(q_send, CHIPS)
+    w_cols = third[:, :, wide:].reshape(ff_win, wide).astype(BF16)
+    input_grad = tn(cot_all, w_cols, None).astype(BF16)
     basis_gram = dot(dot(inverse, gram), inverse.T)
     p_rows = p_pack[:4].reshape(4, 4, rank).transpose(1, 0, 2).reshape(rows, rank)
     basis4 = jnp.tile(dot(p_rows, inverse.T), (1, 4))
@@ -317,8 +305,6 @@
     weigh = jnp.where(
         iota(square, 0) // rank == iota(square, 1) // rank, jnp.tile(basis_gram, (4, 4)), 0.0
     )
-    w_parts, mine = lax.optimization_barrier((w_parts, mine))
-    w_cols = exchange(w_parts, T).reshape(ff_win, wide)
     other = lax.ppermute(mine, "core", [(0, 1), (1, 0)])
     blocks = (n_z, LANES, LANES)
     limit = CLIPPING * math.sqrt(ff_win * width)
@@ -331,8 +317,6 @@
         scratch_shapes=[pltpu.VMEM((rows, width), F32)],
     )(core, mine.reshape(blocks), other.reshape(blocks), basis4, weigh, error, third, momentum)
 
-    cot_all, q_new = lax.optimization_barrier((cot_all, q_new))
-    input_grad = tn(cot_all, w_cols, None).astype(BF16)
     return (input_grad, error_new[None], momentum_new, q_new)
 
 

time: 150 us -> 164 us (1.093)
  blocking collectives: 23.1 us -> 60.4 us
  waiting for transfers between devices: 68.3 us -> 36 us
  starting transfers between devices: 39.3 us -> 46.7 us
  Pallas kernels: 14.6 us -> 17.1 us
    all_gather x0 -> x2, blocking collectives: none -> 60.4 us  [the longest x1 36.5 us: body(): p_all = lax.all_gather(p_pack, T, tiled=True)]
    all_to_all x4, waiting for transfers between devices: 68.3 us -> 36 us  [exchange(): return lax.all_to_all(parts, axes, 0, 0, tiled=True)]
    all_to_all x1 -> x0, blocking collectives: 23.1 us -> none  [exchange(): return lax.all_to_all(parts, axes, 0, 0, tiled=True)]
    all_to_all x4, starting transfers between devices: 35.1 us -> 42.8 us  [exchange(): return lax.all_to_all(parts, axes, 0, 0, tiled=True)]
    pallas_call x3 -> x4, Pallas kernels: 3.13 us -> 5.6 us  [the longest x1 1.98 us: body(): call(share_kernel, [((rows + rank, tokens), F32)], [SMEM] + [HBM] * 3, fl...]
  transfers between devices with their start and end apart: 5 -> 5, of which waited for: 4 -> 2; matrix products, arithmetic and copies ran while one was open for 1% -> 1% of each run, Pallas kernels for 3% -> 5%
where the time goes in v5:
time: 164 us; the launch traced here: 163 us
  blocking collectives  60.4 us (37%)
  starting transfers between devices  46.7 us (28%)
  waiting for transfers between devices  36 us (22%)
  Pallas kernels  17.1 us (10%)
    all_to_all x4, starting transfers between devices, exchange(): return lax.all_to_all(parts, axes, 0, 0, tiled=True)  42.8 us
    all_gather x1, blocking collectives, body(): p_all = lax.all_gather(p_pack, T, tiled=True)  36.5 us
    all_to_all x4, waiting for transfers between devices, exchange(): return lax.all_to_all(parts, axes, 0, 0, tiled=True)  36 us
    all_gather x1, blocking collectives, body(): share = lax.all_gather(share, T)  23.9 us
    pallas_call x1, Pallas kernels, body(): call(functools.partial(factor_kernel, n_r), [((n_r * n_z, group, LANES),...  4.34 us
    pallas_call x1, Pallas kernels, body(): call(functools.partial(last_kernel, limit), [((rank, width), F32), ((rows...  4.07 us
    ppermute x1, starting transfers between devices, body(): other = lax.ppermute(mine, 'core', [(0, 1), (1, 0)])  3.88 us
  transfers between devices with their start and end apart: 5, of which 2 were waited for; matrix products, arithmetic and copies ran while one was open for 1% of the time, Pallas kernels for 5%

profile of v5, /device:TPU:1, one launch (start us, length us, event | category | flops | bytes accessed | tf_op | source)
XLA Modules:
  0.0 162.9 jit_solution(3199423522645882959)
XLA Ops:
  0.6 1.9 %shard_map.93 = f32[16,16,512]{2,1,0:T(8,128)} custom-call(f32[16,8192]{1,0:T(8,128)} %bitcast.19), custom_call_target="tpu_custom_call" | custom-call | bytes 1048576 | tf_op jit(solution)/shard_map/pallas_call | solution.py:240
  2.6 0.0 copy-start
  2.6 12.0 %all-to-all-start = ((f32[16,16,512]{2,1,0:T(8,128)}), f32[16,16,512]{2,1,0:T(8,128)S(1)}, u32[]{:S(2)}, u32[]{:S(2)}) async-start(f32[16,16,512]{2,1,0:T(8,128)} %shard_map.93), calls=%async_computation | async-start | bytes 1048576 | tf_op jit(solution)/shard_map/all_to_all | solution.py:29
  14.6 2.0 %shard_map.94 = f32[48,128]{1,0:T(8,128)} custom-call(s32[1]{0:T(128)} %bitcast.1.t_ref, bf16[128,512]{1,0:T(8,128)(2,1)} %x_ref.5, bf16[16,128]{1,0:T(8,128)(2,1)} %c_ref.3, f32[32,8192]{1,0:T(8,128)} %q_ref.3), custom_call_target="tpu_custom_call" | custom-call | flops 16777216 | bytes 524288 | tf_op jit(solution)/shard_map/pallas_call | solution.py:248
  16.6 0.0 copy-start.6
  16.6 0.9 shard_map.95.pe_ref
  17.5 0.0 copy-start.4
  17.6 23.9 %all-gather = f32[768,128]{1,0:T(8,128)S(1)} all-gather(f32[48,128]{1,0:T(8,128)S(1)} %copy-done.6), channel_id=2, replica_groups=mesh['y'=8,'x'=4,'z'=8,'core'=2] {'z','core'}, dimensions={0}, use_global_device_ids=true | all-gather | bytes 417792 | tf_op jit(solution)/shard_map/all_gather | solution.py:267
  41.5 2.1 %shard_map.96 = (f32[32,36,128]{2,1,0:T(8,128)}, bf16[256,128]{1,0:T(8,128)(2,1)S(1)}) custom-call(f32[16,16,512]{2,1,0:T(8,128)S(1)} %all-to-all-done.got_ref, f32[16,48,128]{2,1,0:T(8,128)S(1)} %bitcast.22, bf16[128,512]{1,0:T(8,128)(2,1)S(1)} %copy-done.2, bf16[16,128]{1,0:T(8,128)(2,1)S(1)} %copy-done.4, f32[16,32]{1,0:T(8,128)S(1)} %shard_map.95.pe_ref), custom_call_target="tpu_custom_call" | custom-call | bytes 2097152 | tf_op jit(solution)/shard_map/pallas_call | solution.py:269
  43.6 9.8 %all-to-all-start.1 = ((f32[32,36,128]{2,1,0:T(8,128)}), f32[32,36,128]{2,1,0:T(8,128)S(1)}, u32[]{:S(2)}, u32[]{:S(2)}) async-start(f32[32,36,128]{2,1,0:T(8,128)} %get-tuple-element.23), calls=%async_computation.1 | async-start | bytes 1310720 | tf_op jit(solution)/shard_map/all_to_all | solution.py:29
  53.4 1.2 shard_map.97
  54.6 17.8 %all-to-all-done.1.got_ref = f32[32,36,128]{2,1,0:T(8,128)S(1)} async-done(((f32[32,36,128]{2,1,0:T(8,128)}), f32[32,36,128]{2,1,0:T(8,128)S(1)}, u32[]{:S(2)}, u32[]{:S(2)}) %all-to-all-start.1) | async-done | bytes 589856 | tf_op jit(solution)/shard_map/all_to_all | solution.py:29
  72.4 8.2 %all-to-all-start.2 = ((f32[16,16,1024]{2,1,0:T(8,128)}), f32[16,16,1024]{2,1,0:T(8,128)S(1)}, u32[]{:S(2)}, u32[]{:S(2)}) async-start(f32[16,16,1024]{2,1,0:T(8,128)} %shard_map.97), calls=%async_computation.2 | async-start | bytes 2097152 | tf_op jit(solution)/shard_map/all_to_all | solution.py:29
  80.6 0.5 shard_map.98
  81.1 36.5 %all_gather.11.pack_ref = f32[128,128]{1,0:T(8,128)S(1)} all-gather(f32[8,128]{1,0:T(8,128)S(1)} %get-tuple-element.25), channel_id=1, replica_groups=mesh['y'=8,'x'=4,'z'=8,'core'=2] {'z','core'}, dimensions={0}, use_global_device_ids=true | all-gather | bytes 69632 | tf_op jit(solution)/shard_map/all_gather | solution.py:288
  117.5 4.3 %shard_map.99 = (f32[256,4,128]{2,1,0:T(4,128)}, f32[32,32]{1,0:T(8,128)S(1)}, f32[32,32]{1,0:T(8,128)S(1)}) custom-call(f32[128,128]{1,0:T(8,128)S(1)} %all_gather.11.pack_ref, f32[16,512]{1,0:T(8,128)S(1)} %get-tuple-element.26.total_ref), custom_call_target="tpu_custom_call" | custom-call | flops 536870912 | bytes 1048576 | tf_op jit(solution)/shard_map/pallas_call | solution.py:290
  121.9 12.8 %all-to-all-start.3 = ((f32[256,4,128]{2,1,0:T(4,128)}), f32[256,4,128]{2,1,0:T(4,128)S(1)}, u32[]{:S(2)}, u32[]{:S(2)}) async-start(f32[256,4,128]{2,1,0:T(4,128)} %get-tuple-element.30), calls=%async_computation.3 | async-start | bytes 1048576 | tf_op jit(solution)/shard_map/all_to_all | solution.py:29
  134.8 0.1 reshape.29
  134.9 0.1 fusion.2
  135.0 0.2 fusion.3
  135.2 18.2 %all-to-all-done.3 = f32[256,4,128]{2,1,0:T(4,128)S(1)} async-done(((f32[256,4,128]{2,1,0:T(4,128)}), f32[256,4,128]{2,1,0:T(4,128)S(1)}, u32[]{:S(2)}, u32[]{:S(2)}) %all-to-all-start.3) | async-done | bytes 524320 | tf_op jit(solution)/shard_map/all_to_all | solution.py:29
  153.3 3.9 %collective-permute-start = (f32[256,4,128]{2,1,0:T(4,128)S(1)}, f32[256,4,128]{2,1,0:T(4,128)S(1)}, u32[]{:S(2)}, u32[]{:S(2)}) collective-permute-start(f32[256,4,128]{2,1,0:T(4,128)S(1)} %all-to-all-done.3), channel_id=1, source_target_pairs={{0,1},{1,0},{2,3},{3,2},{4,5},{5,4},{6,7},{7,6},{8,9},{9,8},{10,11... | collective-permute-start | bytes 1572872 | tf_op jit(solution)/shard_map/ppermute | solution.py:308
  157.2 0.1 fusion.1
  157.3 0.1 tile.20
  157.4 0.2 tile.21
  157.6 0.1 tile.9.basis_ref
  157.7 0.1 fusion.weigh_ref
  157.8 0.0 copy-start.5
  157.8 0.9 convolution_convert_fusion
  158.7 0.0 collective-permute-done
  158.7 0.1 copy-done.5
  158.8 4.1 %shard_map.100 = (f32[32,8192]{1,0:T(8,128)}, f32[16,8192]{1,0:T(8,128)}, f32[16,8192]{1,0:T(8,128)}) custom-call(s32[1]{0:T(128)} %bitcast.4.core_ref, f32[8,128,128]{2,1,0:T(8,128)S(1)} %bitcast.23, f32[8,128,128]{2,1,0:T(8,128)S(1)} %bitcast.24, f32[16,128]{1,0:T(8,128)S(1)} %tile.9.basis_ref, f32[128,128]{1,0:T(8,128)S(1)} %fusion.weigh_ref, ...), custom_call_target="tpu_custom_call" | custom-call | flops 1073741824 | bytes 5242880 | tf_op jit(solution)/shard_map/pallas_call | solution.py:311
  (17 shorter events, 0.1 us)
Async XLA Ops:
  2.6 14.0 %copy-start = (f32[32,8192]{1,0:T(8,128)S(1)}, f32[32,8192]{1,0:T(8,128)}, u32[]{:S(2)}) copy-start(f32[32,8192]{1,0:T(8,128)} %q_ref.3) | copy-start | bytes 3145732
  2.6 38.9 %all-to-all-start = ((f32[16,16,512]{2,1,0:T(8,128)}), f32[16,16,512]{2,1,0:T(8,128)S(1)}, u32[]{:S(2)}, u32[]{:S(2)}) async-start(f32[16,16,512]{2,1,0:T(8,128)} %shard_map.93), calls=%async_computation | async-start | bytes 1048576 | tf_op jit(solution)/shard_map/all_to_all | solution.py:29
  14.6 2.0 %copy-start.1 = (f32[1,16,8192]{2,1,0:T(8,128)S(1)}, f32[1,16,8192]{2,1,0:T(8,128)}, u32[]{:S(2)}) copy-start(f32[1,16,8192]{2,1,0:T(8,128)} %param.9) | copy-start | bytes 1572868
  16.6 1.0 copy-start.6
  17.5 23.9 %copy-start.2 = (bf16[128,512]{1,0:T(8,128)(2,1)S(1)}, bf16[128,512]{1,0:T(8,128)(2,1)}, u32[]{:S(2)}) copy-start(bf16[128,512]{1,0:T(8,128)(2,1)} %x_ref.5) | copy-start | bytes 393220
  17.5 23.9 %copy-start.4 = (bf16[16,128]{1,0:T(8,128)(2,1)S(1)}, bf16[16,128]{1,0:T(8,128)(2,1)}, u32[]{:S(2)}) copy-start(bf16[16,128]{1,0:T(8,128)(2,1)} %c_ref.3) | copy-start | bytes 12292
  43.6 9.8 %copy-start.3 = (bf16[16,8192]{1,0:T(8,128)(2,1)S(1)}, bf16[16,8192]{1,0:T(8,128)(2,1)}, u32[]{:S(2)}) copy-start(bf16[16,8192]{1,0:T(8,128)(2,1)} %w_ref.1) | copy-start | bytes 786436
  43.6 28.8 %all-to-all-start.1 = ((f32[32,36,128]{2,1,0:T(8,128)}), f32[32,36,128]{2,1,0:T(8,128)S(1)}, u32[]{:S(2)}, u32[]{:S(2)}) async-start(f32[32,36,128]{2,1,0:T(8,128)} %get-tuple-element.23), calls=%async_computation.1 | async-start | bytes 1310720 | tf_op jit(solution)/shard_map/all_to_all | solution.py:29
  72.4 49.5 %all-to-all-start.2 = ((f32[16,16,1024]{2,1,0:T(8,128)}), f32[16,16,1024]{2,1,0:T(8,128)S(1)}, u32[]{:S(2)}, u32[]{:S(2)}) async-start(f32[16,16,1024]{2,1,0:T(8,128)} %shard_map.97), calls=%async_computation.2 | async-start | bytes 2097152 | tf_op jit(solution)/shard_map/all_to_all | solution.py:29
  121.9 31.4 %all-to-all-start.3 = ((f32[256,4,128]{2,1,0:T(4,128)}), f32[256,4,128]{2,1,0:T(4,128)S(1)}, u32[]{:S(2)}, u32[]{:S(2)}) async-start(f32[256,4,128]{2,1,0:T(4,128)} %get-tuple-element.30), calls=%async_computation.3 | async-start | bytes 1048576 | tf_op jit(solution)/shard_map/all_to_all | solution.py:29
  153.3 5.4 %collective-permute-start = (f32[256,4,128]{2,1,0:T(4,128)S(1)}, f32[256,4,128]{2,1,0:T(4,128)S(1)}, u32[]{:S(2)}, u32[]{:S(2)}) collective-permute-start(f32[256,4,128]{2,1,0:T(4,128)S(1)} %all-to-all-done.3), channel_id=1, source_target_pairs={{0,1},{1,0},{2,3},{3,2},{4,5},{5,4},{6,7},{7,6},{8,9},{9,8},{10,11... | collective-permute-start | bytes 1572872 | tf_op jit(solution)/shard_map/ppermute | solution.py:308
  157.8 1.0 copy-start.5

commit v6 on v4

--- a/solution.py
+++ b/solution.py
@@ -138,31 +138,24 @@
         send_ref[k, halves * own :, :] = p_pack[: send_ref.shape[1] - halves * own]
 
 
-def rows_kernel(cot_ref, x_ref, send_ref):
-    n_t = send_ref.shape[0]
-    rows = cot_ref.shape[0] // n_t
-    grad = dot(cot_ref[...], x_ref[...], None)
+def rows_kernel(t_ref, c_ref, cot_ref, got_ref, g_ref, dx_ref, w):
+    n_t = got_ref.shape[0]
+    rows, tokens = c_ref.shape
+    wide = got_ref.shape[2]
+    at = pl.ds(pl.multiple_of(tokens + t_ref[0] * rows, rows), rows)
     for k in range(n_t):
-        for b in range(grad.shape[1] // LANES):
-            send_ref[k, b * rows : (b + 1) * rows, :] = grad[
-                k * rows : (k + 1) * rows, b * LANES : (b + 1) * LANES
-            ]
-
-
-def sum_kernel(got_ref, held_ref, total_ref, pack_ref, send_ref, scratch, sem):
-    n_r = got_ref.shape[0]
-    n_t, tall, _ = send_ref.shape
+        g_ref[:, k * wide : (k + 1) * wide] = dot(c_ref[...], got_ref[k, :tokens, :], None)
+        w[k * rows : (k + 1) * rows] = got_ref[k, at, :]
+    dx_ref[...] = tn(cot_ref[...], w[...], None).astype(BF16)
+
+
+def sum_kernel(n_t, got_ref, total_ref, pack_ref):
     own, long = total_ref.shape
     ff_win = long // 2
     rows = ff_win // n_t
     got = jnp.sum(got_ref[...], 0)
     pack = got[got.shape[0] - 4 :]
-    pack = jnp.concatenate([pack, jnp.zeros_like(pack)], 0)
-    pack_ref[...] = pack
-    for k in range(n_t):
-        scratch[k] = pack
-    copy = pltpu.make_async_copy(scratch, send_ref.at[:, pl.ds(tall - SUB, SUB), :], sem)
-    copy.start()
+    pack_ref[...] = jnp.concatenate([pack, jnp.zeros_like(pack)], 0)
     halves = ff_win // LANES if ff_win >= LANES else 1
     width = ff_win // halves
     total = jnp.zeros(total_ref.shape, F32)
@@ -172,15 +165,14 @@
         move = (lane == b * (SUB * n_t) + t * SUB + a).astype(F32)
         total += dot(got[h * own : (h + 1) * own, :width], move)
     total_ref[...] = total
-    copy.wait()
 
 
 def factor_kernel(n_r, pack_ref, total_ref, send_ref, gram_ref, inverse_ref):
-    n_t = pack_ref.shape[0]
+    span = pack_ref.shape[0]
     own = total_ref.shape[0]
     rank = gram_ref.shape[0]
     group = own // 4
-    pack = pack_ref[...].reshape(n_t * SUB, LANES)
+    pack = pack_ref[...]
     gram4 = tn(pack, pack)
     gram = sum(gram4[b * rank : (b + 1) * rank, b * rank : (b + 1) * rank] for b in range(4))
     gram_ref[...] = gram
@@ -197,7 +189,6 @@
     inverse16 = jnp.concatenate([inverse] * 4, 0)
     inverse16 = jnp.concatenate([inverse16] * 4, 1)
     total = total_ref[...]
-    span = SUB * n_t
     product = jnp.zeros((own, LANES), F32)
     for b in range(4):
         part = dot(total[:, b * span : (b + 1) * span], pack)
@@ -232,7 +223,7 @@
                 near = both[LANES + b * rows : LANES + (b + 1) * rows]
                 q_ref[:, at] = both[b * rank : (b + 1) * rank]
                 approx[:, at] = near
-                error_ref[:, at] = e_ref[:, at] + g_ref[t, b * rows : (b + 1) * rows, :] - near
+                error_ref[:, at] = e_ref[:, at] + g_ref[:, at] - near
     total = jnp.sum(gram * weigh_ref[...], keepdims=True)
     scale = jnp.minimum(1.0, limit / jnp.sqrt(total))
     momentum_ref[...] = BETA * m_ref[...] + scale * approx[...]
@@ -271,45 +262,41 @@
     )(error_late, q_prev)
     first = exchange(first, T)
 
-    tall = wide // LANES * rows + SUB
+    bulk = jnp.concatenate([tokens_x, w_parts.reshape(rows * n_t, wide)], 0)
+    first, bulk = lax.optimization_barrier((first, bulk))
+    bulk = lax.all_gather(bulk, T)
     second, cot_all = call(
         merge_kernel,
         [((n_r, halves * own + 4, LANES), F32), ((ff_win, tokens), BF16)],
         [VMEM] * 4,
         moved=2 * 2**20,
     )(first, tokens_x, cotangent, p_error)
-    (third,) = call(
-        rows_kernel, [((n_t, tall, LANES), F32)], [VMEM] * 2, flops=2**25, moved=2**20
-    )(cot_all, tokens_x)
     second = exchange(second, R)
-
-    total_t, p_pack, third = call(
-        sum_kernel,
-        [((own, 2 * ff_win), F32), ((SUB, LANES), F32), (third.shape, F32)],
-        [VMEM, pl.BlockSpec(memory_space=pl.ANY)],
-        [VMEM, VMEM, pl.BlockSpec(memory_space=pl.ANY)],
+    total_t, p_pack = call(
+        functools.partial(sum_kernel, n_t),
+        [((own, 2 * ff_win), F32), ((SUB, LANES), F32)],
+        [VMEM],
         moved=2**20,
-        scratch_shapes=[pltpu.VMEM((n_t, SUB, LANES), F32), pltpu.SemaphoreType.DMA(())],
-        input_output_aliases={1: 2},
-    )(second, third)
-    third = exchange(third, T)
+    )(second)
+    p_all = exchange(jnp.broadcast_to(p_pack[None], (n_t, SUB, LANES)), T)
 
     q_send, gram, inverse = call(
         functools.partial(factor_kernel, n_r),
         [((n_r * n_z, group, LANES), F32), ((rank, rank), F32), ((rank, rank), F32)],
-        [
-            pl.BlockSpec((n_t, SUB, LANES), lambda i: (0, tall // SUB - 1, 0)),
-            pl.BlockSpec((own, 2 * ff_win), lambda i: (0, 0)),
-        ],
-        [
-            pl.BlockSpec((n_r * n_z, group, LANES), lambda i: (0, 0, 0)),
-            pl.BlockSpec((rank, rank), lambda i: (0, 0)),
-            pl.BlockSpec((rank, rank), lambda i: (0, 0)),
-        ],
+        [VMEM] * 2,
+        flops=2**29,
         moved=2**20,
-        grid=(1,),
-    )(third, total_t)
+    )(p_all.reshape(n_t * SUB, LANES), total_t)
+    q_send, bulk = lax.optimization_barrier((q_send, bulk))
     mine = exchange(q_send, CHIPS)
+    grad_rows, input_grad = call(
+        rows_kernel,
+        [((rows, width), F32), ((tokens, wide), BF16)],
+        [SMEM] + [VMEM] * 3,
+        flops=2**28,
+        moved=8 * 2**20,
+        scratch_shapes=[pltpu.VMEM((ff_win, wide), BF16)],
+    )(t, cotangent, cot_all, bulk)
     basis_gram = dot(dot(inverse, gram), inverse.T)
     p_rows = p_pack[:4].reshape(4, 4, rank).transpose(1, 0, 2).reshape(rows, rank)
     basis4 = jnp.tile(dot(p_rows, inverse.T), (1, 4))
@@ -317,8 +304,6 @@
     weigh = jnp.where(
         iota(square, 0) // rank == iota(square, 1) // rank, jnp.tile(basis_gram, (4, 4)), 0.0
     )
-    w_parts, mine = lax.optimization_barrier((w_parts, mine))
-    w_cols = exchange(w_parts, T).reshape(ff_win, wide)
     other = lax.ppermute(mine, "core", [(0, 1), (1, 0)])
     blocks = (n_z, LANES, LANES)
     limit = CLIPPING * math.sqrt(ff_win * width)
@@ -329,10 +314,8 @@
         flops=2**30,
         moved=5 * 2**20,
         scratch_shapes=[pltpu.VMEM((rows, width), F32)],
-    )(core, mine.reshape(blocks), other.reshape(blocks), basis4, weigh, error, third, momentum)
-
-    cot_all, q_new = lax.optimization_barrier((cot_all, q_new))
-    input_grad = tn(cot_all, w_cols, None).astype(BF16)
+    )(core, mine.reshape(blocks), other.reshape(blocks), basis4, weigh, error, grad_rows, momentum)
+
     return (input_grad, error_new[None], momentum_new, q_new)
 
 

time: 150 us -> 150 us (level)
  waiting for transfers between devices: 68.3 us -> 40.6 us
  blocking collectives: 23.1 us -> 42.1 us
  between operations: 0.82 us -> 14.2 us
  starting transfers between devices: 39.3 us -> 30.8 us
  Pallas kernels: 14.6 us -> 17.6 us
  other arithmetic: 0.13 us -> 1.81 us
    all_to_all x4 -> x2, waiting for transfers between devices: 68.3 us -> 40.6 us  [exchange(): return lax.all_to_all(parts, axes, 0, 0, tiled=True)]
    all_to_all x1 -> x2, blocking collectives: 23.1 us -> 42.1 us  [exchange(): return lax.all_to_all(parts, axes, 0, 0, tiled=True)]
    all_to_all x4 -> x2, starting transfers between devices: 35.1 us -> 26.8 us  [exchange(): return lax.all_to_all(parts, axes, 0, 0, tiled=True)]
    pallas_call x2, Pallas kernels: 0.7 us -> 4.4 us  [the longest x1 3.91 us: body(): call(rows_kernel, [((rows, width), F32), ((tokens, wide), BF16)], [SMEM]...]
    concatenate x0 -> x1, other arithmetic: none -> 1.68 us  [body(): bulk = jnp.concatenate([tokens_x, w_parts.reshape(rows * n_t, wide)], 0)]
  transfers between devices with their start and end apart: 5 -> 4, of which waited for: 4 -> 2; matrix products, arithmetic and copies ran while one was open for 1% -> 3% of each run, Pallas kernels for 3% -> 7%
where the time goes in v6:
time: 150 us; the launch traced here: 149 us
  blocking collectives  42.1 us (28%)
  waiting for transfers between devices  40.6 us (27%)
  starting transfers between devices  30.8 us (21%)
  Pallas kernels  17.6 us (12%)
  between operations  14.2 us (9%)
  other arithmetic  1.81 us (1%)
  local copies, waits for them, and re-layouts  1.62 us (1%)
    all_to_all x2, blocking collectives, exchange(): return lax.all_to_all(parts, axes, 0, 0, tiled=True)  42.1 us
    all_to_all x2, waiting for transfers between devices, exchange(): return lax.all_to_all(parts, axes, 0, 0, tiled=True)  40.6 us
    all_to_all x2, starting transfers between devices, exchange(): return lax.all_to_all(parts, axes, 0, 0, tiled=True)  26.8 us
    pallas_call x1, Pallas kernels, body(): call(functools.partial(factor_kernel, n_r), [((n_r * n_z, group, LANES),...  4.34 us
    pallas_call x1, Pallas kernels, body(): call(functools.partial(last_kernel, limit), [((rank, width), F32), ((rows...  4.09 us
    ppermute x1, starting transfers between devices, body(): other = lax.ppermute(mine, 'core', [(0, 1), (1, 0)])  3.98 us
    pallas_call x1, Pallas kernels, body(): call(rows_kernel, [((rows, width), F32), ((tokens, wide), BF16)], [SMEM]...  3.91 us
  transfers between devices with their start and end apart: 4, of which 2 were waited for; matrix products, arithmetic and copies ran while one was open for 3% of the time, Pallas kernels for 7%

profile of v6, /device:TPU:1, one launch (start us, length us, event | category | flops | bytes accessed | tf_op | source)
XLA Modules:
  0.0 149.2 jit_solution(12361857753664783993)
XLA Ops:
  7.2 0.0 copy-start.2
  7.2 0.0 copy-start.1
  7.2 0.0 copy-start
  7.2 2.5 %shard_map.93 = f32[16,16,896]{2,1,0:T(8,128)} custom-call(s32[1]{0:T(128)} %bitcast.t_ref, bf16[128,512]{1,0:T(8,128)(2,1)} %x_ref.3, bf16[16,128]{1,0:T(8,128)(2,1)} %c_ref.5, f32[16,8192]{1,0:T(8,128)} %bitcast.22, f32[32,8192]{1,0:T(8,128)} %q_ref.3), custom_call_target="tpu_custom_call" | custom-call | bytes 3145728 | tf_op jit(solution)/shard_map/pallas_call | solution.py:245
  9.8 11.8 %all-to-all-start = ((f32[16,16,896]{2,1,0:T(8,128)}), f32[16,16,896]{2,1,0:T(8,128)S(1)}, u32[]{:S(2)}, u32[]{:S(2)}) async-start(f32[16,16,896]{2,1,0:T(8,128)} %shard_map.93), calls=%async_computation | async-start | bytes 1835008 | tf_op jit(solution)/shard_map/all_to_all | solution.py:29
  21.6 0.0 all-gather.3.cloned.1.call-start
  21.7 1.0 copy.13
  22.7 0.2 copy.11
  22.8 1.7 %pad_maximum_fusion = bf16[384,512]{1,0:T(8,128)(2,1)} fusion(bf16[256,512]{1,0:T(8,128)(2,1)S(1)} %bitcast.29, bf16[128,512]{1,0:T(8,128)(2,1)} %x_ref.3), kind=kLoop, calls=%fused_computation | loop fusion | flops 786432 | bytes 786432 | tf_op jit(solution)/shard_map/concatenate | solution.py:265
  24.5 22.4 %all-to-all-done.got_ref = f32[16,16,896]{2,1,0:T(8,128)S(1)} async-done(((f32[16,16,896]{2,1,0:T(8,128)}), f32[16,16,896]{2,1,0:T(8,128)S(1)}, u32[]{:S(2)}, u32[]{:S(2)}) %all-to-all-start) | async-done | bytes 917536 | tf_op jit(solution)/shard_map/all_to_all | solution.py:29
  46.9 0.0 all-gather.3.cloned.1.call-update
  47.0 1.0 shard_map.94.pe_ref
  47.9 0.0 copy-done.2
  47.9 1.3 shard_map.95
  49.2 0.0 copy-start.4
  49.2 29.3 %all_to_all.20.got_ref = f32[32,36,128]{2,1,0:T(8,128)S(1)} all-to-all(f32[32,36,128]{2,1,0:T(8,128)S(1)} %get-tuple-element.26), channel_id=1, replica_groups=mesh['y'=8,'x'=4,'z'=8,'core'=2] {'y','x'}, dimensions={0} | all-to-all | bytes 1179648 | tf_op jit(solution)/shard_map/all_to_all | solution.py:29
  78.5 0.5 shard_map.96
  79.0 12.8 %all_to_all.21 = f32[16,8,128]{2,1,0:T(8,128)S(1)} all-to-all(f32[16,8,128]{2,1,0:T(8,128)S(1)} %broadcast_in_dim.20), channel_id=1, replica_groups=mesh['y'=8,'x'=4,'z'=8,'core'=2] {'z','core'}, dimensions={0} | all-to-all | bytes 131072 | tf_op jit(solution)/shard_map/all_to_all | solution.py:29
  91.9 4.3 %shard_map.97 = (f32[256,4,128]{2,1,0:T(4,128)}, f32[32,32]{1,0:T(8,128)S(1)}, f32[32,32]{1,0:T(8,128)S(1)}) custom-call(f32[128,128]{1,0:T(8,128)S(1)} %bitcast.26, f32[16,512]{1,0:T(8,128)S(1)} %get-tuple-element.28.total_ref), custom_call_target="tpu_custom_call" | custom-call | flops 536870912 | bytes 1048576 | tf_op jit(solution)/shard_map/pallas_call | solution.py:283
  96.2 14.9 %all-to-all-start.3 = ((f32[256,4,128]{2,1,0:T(4,128)}), f32[256,4,128]{2,1,0:T(4,128)S(1)}, u32[]{:S(2)}, u32[]{:S(2)}) async-start(f32[256,4,128]{2,1,0:T(4,128)} %get-tuple-element.33), calls=%async_computation.3 | async-start | bytes 1048576 | tf_op jit(solution)/shard_map/all_to_all | solution.py:29
  111.2 0.1 reshape.40
  111.3 0.1 fusion.2
  111.4 18.2 %all-to-all-done.3 = f32[256,4,128]{2,1,0:T(4,128)S(1)} async-done(((f32[256,4,128]{2,1,0:T(4,128)}), f32[256,4,128]{2,1,0:T(4,128)S(1)}, u32[]{:S(2)}, u32[]{:S(2)}) %all-to-all-start.3) | async-done | bytes 524320 | tf_op jit(solution)/shard_map/all_to_all | solution.py:29
  129.6 4.0 %collective-permute-start = (f32[256,4,128]{2,1,0:T(4,128)S(1)}, f32[256,4,128]{2,1,0:T(4,128)S(1)}, u32[]{:S(2)}, u32[]{:S(2)}) collective-permute-start(f32[256,4,128]{2,1,0:T(4,128)S(1)} %all-to-all-done.3), channel_id=1, source_target_pairs={{0,1},{1,0},{2,3},{3,2},{4,5},{5,4},{6,7},{7,6},{8,9},{9,8},{10,11... | collective-permute-start | bytes 1572872 | tf_op jit(solution)/shard_map/ppermute | solution.py:307
  133.6 0.1 fusion.1
  133.8 0.1 tile.9.basis_ref
  133.9 0.1 fusion.3
  134.1 0.2 tile.21
  134.2 0.1 fusion.weigh_ref
  134.3 3.9 %shard_map.98 = (f32[16,8192]{1,0:T(8,128)S(1)}, bf16[128,512]{1,0:T(8,128)(2,1)}) custom-call(s32[1]{0:T(128)} %bitcast.t_ref, bf16[16,128]{1,0:T(8,128)(2,1)S(1)} %copy-done.3, bf16[256,128]{1,0:T(8,128)(2,1)S(1)} %get-tuple-element.25.cot_ref, bf16[16,384,512]{2,1,0:T(8,128)(2,1)} %bitcast.28), custom_call_target="tpu_custom_call" | custom-call | flops 268435456 | bytes 8388608 | tf_op jit(solution)/shard_map/pallas_call | solution.py:292
  138.3 0.0 collective-permute-done
  138.3 4.1 %shard_map.99 = (f32[32,8192]{1,0:T(8,128)}, f32[16,8192]{1,0:T(8,128)}, f32[16,8192]{1,0:T(8,128)}) custom-call(s32[1]{0:T(128)} %bitcast.6.core_ref, f32[8,128,128]{2,1,0:T(8,128)S(1)} %bitcast.25, f32[8,128,128]{2,1,0:T(8,128)S(1)} %bitcast.27, f32[16,128]{1,0:T(8,128)S(1)} %tile.9.basis_ref, f32[128,128]{1,0:T(8,128)S(1)} %fusion.weigh_ref, ...), custom_call_target="tpu_custom_call" | custom-call | flops 1073741824 | bytes 5242880 | tf_op jit(solution)/shard_map/pallas_call | solution.py:310
  (13 shorter events, 0.1 us)
Async XLA Ops:
  7.2 40.7 %copy-start.3 = (bf16[16,128]{1,0:T(8,128)(2,1)S(1)}, bf16[16,128]{1,0:T(8,128)(2,1)}, u32[]{:S(2)}) copy-start(bf16[16,128]{1,0:T(8,128)(2,1)} %c_ref.5) | copy-start | bytes 12292
  7.2 40.7 %copy-start.2 = (bf16[128,512]{1,0:T(8,128)(2,1)S(1)}, bf16[128,512]{1,0:T(8,128)(2,1)}, u32[]{:S(2)}) copy-start(bf16[128,512]{1,0:T(8,128)(2,1)} %x_ref.3) | copy-start | bytes 393220
  7.2 39.7 %copy-start.1 = (f32[1,16,8192]{2,1,0:T(8,128)S(1)}, f32[1,16,8192]{2,1,0:T(8,128)}, u32[]{:S(2)}) copy-start(f32[1,16,8192]{2,1,0:T(8,128)} %param.9) | copy-start | bytes 1572868
  7.2 39.7 %copy-start = (f32[32,8192]{1,0:T(8,128)S(1)}, f32[32,8192]{1,0:T(8,128)}, u32[]{:S(2)}) copy-start(f32[32,8192]{1,0:T(8,128)} %q_ref.3) | copy-start | bytes 3145732
  9.8 37.1 %all-to-all-start = ((f32[16,16,896]{2,1,0:T(8,128)}), f32[16,16,896]{2,1,0:T(8,128)S(1)}, u32[]{:S(2)}, u32[]{:S(2)}) async-start(f32[16,16,896]{2,1,0:T(8,128)} %shard_map.93), calls=%async_computation | async-start | bytes 1835008 | tf_op jit(solution)/shard_map/all_to_all | solution.py:29
  21.6 74.6 %all-gather.3.cloned.1.call-start = ((), (), s32[]{:S(2)}) async-start(), calls=%async_computation.4 | async-start | bytes 6684672 | tf_op jit(solution)/shard_map/all_gather | solution.py:267
  49.2 89.1 %copy-start.4 = (f32[16,8192]{1,0:T(8,128)S(1)}, f32[16,8192]{1,0:T(8,128)}, u32[]{:S(2)}) copy-start(f32[16,8192]{1,0:T(8,128)} %m_ref.1) | copy-start | bytes 1572868
  96.2 33.4 %all-to-all-start.3 = ((f32[256,4,128]{2,1,0:T(4,128)}), f32[256,4,128]{2,1,0:T(4,128)S(1)}, u32[]{:S(2)}, u32[]{:S(2)}) async-start(f32[256,4,128]{2,1,0:T(4,128)} %get-tuple-element.33), calls=%async_computation.3 | async-start | bytes 1048576 | tf_op jit(solution)/shard_map/all_to_all | solution.py:29
  129.6 8.6 %collective-permute-start = (f32[256,4,128]{2,1,0:T(4,128)S(1)}, f32[256,4,128]{2,1,0:T(4,128)S(1)}, u32[]{:S(2)}, u32[]{:S(2)}) collective-permute-start(f32[256,4,128]{2,1,0:T(4,128)S(1)} %all-to-all-done.3), channel_id=1, source_target_pairs={{0,1},{1,0},{2,3},{3,2},{4,5},{5,4},{6,7},{7,6},{8,9},{9,8},{10,11... | collective-permute-start | bytes 1572872 | tf_op jit(solution)/shard_map/ppermute | solution.py:307
Sparse Core Ops, SparseCore 0:
  47.1 48.4 all-gather.2

commit v7 on v6

--- a/solution.py
+++ b/solution.py
@@ -198,12 +198,10 @@
     send_ref[...] = jnp.broadcast_to(q_pack[None], send_ref.shape)
 
 
-def last_kernel(limit, core_ref, mine_ref, other_ref, basis_ref, weigh_ref, e_ref, g_ref, m_ref, q_ref, error_ref, momentum_ref, approx):
-    n_z = mine_ref.shape[0]
+def place_blocks(near_core, blocks_ref, basis_ref, e_ref, g_ref, q_hbm, error_hbm, q, error, sems, approx_ref, gram):
+    n_z = blocks_ref.shape[0]
     rows = e_ref.shape[0]
-    rank = q_ref.shape[0]
-    core = core_ref[0]
-    wide = 4 * LANES
+    rank = q.shape[1]
     square = (LANES, LANES)
     basis4 = basis_ref[...]
     stack = jnp.concatenate(
@@ -211,22 +209,50 @@
         + [jnp.where(iota(basis4.shape, 1) // rank == b, basis4, 0.0) for b in range(4)],
         0,
     )
-    gram = jnp.zeros(square, F32)
+    copies = []
     for z in range(n_z):
-        for ref, c in ((mine_ref, core), (other_ref, 1 - core)):
-            block = ref[z]
-            gram += tn(block, block)
-            both = nt(stack, block)
-            t = 2 * z + c
-            for b in range(4):
-                at = pl.ds(pl.multiple_of(t * wide + b * LANES, LANES), LANES)
-                near = both[LANES + b * rows : LANES + (b + 1) * rows]
-                q_ref[:, at] = both[b * rank : (b + 1) * rank]
-                approx[:, at] = near
-                error_ref[:, at] = e_ref[:, at] + g_ref[:, at] - near
+        block = blocks_ref[z]
+        gram += tn(block, block)
+        both = nt(stack, block)
+        start = pl.multiple_of((2 * z + near_core) * 4 * LANES, 4 * LANES)
+        for b in range(4):
+            near = both[LANES + b * rows : LANES + (b + 1) * rows]
+            at = pl.ds(pl.multiple_of(start + b * LANES, LANES), LANES)
+            to = slice(b * LANES, (b + 1) * LANES)
+            q[z, :, to] = both[b * rank : (b + 1) * rank]
+            approx_ref[z, :, to] = near
+            error[z, :, to] = e_ref[:, at] + g_ref[:, at] - near
+        span = pl.ds(start, 4 * LANES)
+        copies.append(pltpu.make_async_copy(q.at[z], q_hbm.at[:, span], sems.at[0, z]))
+        copies.append(pltpu.make_async_copy(error.at[z], error_hbm.at[:, span], sems.at[1, z]))
+        copies[-2].start()
+        copies[-1].start()
+    return gram, copies
+
+
+def near_kernel(core_ref, mine_ref, basis_ref, e_ref, g_ref, q_hbm, error_hbm, approx_ref, gram_ref, q, error, sems):
+    gram, copies = place_blocks(
+        core_ref[0], mine_ref, basis_ref, e_ref, g_ref, q_hbm, error_hbm, q, error, sems, approx_ref,
+        jnp.zeros((LANES, LANES), F32),
+    )
+    gram_ref[...] = gram
+    for copy in copies:
+        copy.wait()
+
+
+def far_kernel(limit, core_ref, other_ref, basis_ref, e_ref, g_ref, gram_ref, approx_ref, weigh_ref, m_ref, q_old, error_old, q_hbm, error_hbm, momentum_ref, q, error, sems, far):
+    core = core_ref[0]
+    gram, copies = place_blocks(
+        1 - core, other_ref, basis_ref, e_ref, g_ref, q_hbm, error_hbm, q, error, sems, far, gram_ref[...]
+    )
     total = jnp.sum(gram * weigh_ref[...], keepdims=True)
     scale = jnp.minimum(1.0, limit / jnp.sqrt(total))
-    momentum_ref[...] = BETA * m_ref[...] + scale * approx[...]
+    for z in range(other_ref.shape[0]):
+        for ref, c in ((approx_ref, core), (far, 1 - core)):
+            at = pl.ds(pl.multiple_of((2 * z + c) * 4 * LANES, 4 * LANES), 4 * LANES)
+            momentum_ref[:, at] = BETA * m_ref[:, at] + scale * ref[z]
+    for copy in copies:
+        copy.wait()
 
 
 def body(tokens_x, cotangent, weight, error_fb, momentum, q_prev):
@@ -263,7 +289,7 @@
     first = exchange(first, T)
 
     bulk = jnp.concatenate([tokens_x, w_parts.reshape(rows * n_t, wide)], 0)
-    first, bulk = lax.optimization_barrier((first, bulk))
+    first, bulk, p_error = lax.optimization_barrier((first, bulk, p_error))
     bulk = lax.all_gather(bulk, T)
     second, cot_all = call(
         merge_kernel,
@@ -287,7 +313,6 @@
         flops=2**29,
         moved=2**20,
     )(p_all.reshape(n_t * SUB, LANES), total_t)
-    q_send, bulk = lax.optimization_barrier((q_send, bulk))
     mine = exchange(q_send, CHIPS)
     grad_rows, input_grad = call(
         rows_kernel,
@@ -297,6 +322,7 @@
         moved=8 * 2**20,
         scratch_shapes=[pltpu.VMEM((ff_win, wide), BF16)],
     )(t, cotangent, cot_all, bulk)
+    mine, grad_rows = lax.optimization_barrier((mine, grad_rows))
     basis_gram = dot(dot(inverse, gram), inverse.T)
     p_rows = p_pack[:4].reshape(4, 4, rank).transpose(1, 0, 2).reshape(rows, rank)
     basis4 = jnp.tile(dot(p_rows, inverse.T), (1, 4))
@@ -307,15 +333,31 @@
     other = lax.ppermute(mine, "core", [(0, 1), (1, 0)])
     blocks = (n_z, LANES, LANES)
     limit = CLIPPING * math.sqrt(ff_win * width)
+    scratch = [
+        pltpu.VMEM((n_z, rank, wide), F32),
+        pltpu.VMEM((n_z, rows, wide), F32),
+        pltpu.SemaphoreType.DMA((2, n_z)),
+    ]
+    whole = [((rank, width), F32), ((rows, width), F32)]
+    q_new, error_new, approx, q_gram = call(
+        near_kernel,
+        [*whole, ((n_z, rows, wide), F32), ((LANES, LANES), F32)],
+        [SMEM] + [VMEM] * 4,
+        [HBM, HBM, VMEM, VMEM],
+        flops=2**30,
+        moved=3 * 2**20,
+        scratch_shapes=scratch,
+    )(core, mine.reshape(blocks), basis4, error, grad_rows)
     q_new, error_new, momentum_new = call(
-        functools.partial(last_kernel, limit),
-        [((rank, width), F32), ((rows, width), F32), ((rows, width), F32)],
-        [SMEM] + [VMEM] * 7,
+        functools.partial(far_kernel, limit),
+        [*whole, ((rows, width), F32)],
+        [SMEM] + [VMEM] * 8 + [HBM, HBM],
+        [HBM, HBM, VMEM],
         flops=2**30,
-        moved=5 * 2**20,
-        scratch_shapes=[pltpu.VMEM((rows, width), F32)],
-    )(core, mine.reshape(blocks), other.reshape(blocks), basis4, weigh, error, grad_rows, momentum)
-
+        moved=4 * 2**20,
+        scratch_shapes=[*scratch, pltpu.VMEM((n_z, rows, wide), F32)],
+        input_output_aliases={9: 0, 10: 1},
+    )(core, other.reshape(blocks), basis4, error, grad_rows, q_gram, approx, weigh, momentum, q_new, error_new)
     return (input_grad, error_new[None], momentum_new, q_new)
 
 

time: 150 us -> 140 us (0.933)
  waiting for transfers between devices: 40.6 us -> 33.5 us
  starting transfers between devices: 30.8 us -> 26 us
  local copies, waits for them, and re-layouts: 1.62 us -> 3.87 us
    all_to_all x2, waiting for transfers between devices: 40.6 us -> 33.5 us  [exchange(): return lax.all_to_all(parts, axes, 0, 0, tiled=True)]
    all_to_all x2, starting transfers between devices: 26.8 us -> 21.2 us  [exchange(): return lax.all_to_all(parts, axes, 0, 0, tiled=True)]
    unnamed x11 -> x13, local copies, waits for them, and re-layouts: 1.06 us -> 3.31 us
    pallas_call x1 -> x2, Pallas kernels: 4.09 us -> 5.33 us  [the longest x1 3.1 us: body(): call(functools.partial(far_kernel, limit), [*whole, ((rows, width), F32)]...]
  transfers between devices with their start and end apart: 4 -> 4, of which waited for: 2 -> 2; matrix products, arithmetic and copies ran while one was open for 3% -> 2% of each run, Pallas kernels for 7% -> 9%
where the time goes in v7:
time: 140 us
  blocking collectives  42.1 us (30%)
  waiting for transfers between devices  33.5 us (24%)
  starting transfers between devices  26 us (19%)
  Pallas kernels  18.8 us (13%)
  between operations  14.2 us (10%)
  local copies, waits for them, and re-layouts  3.87 us (3%)
    all_to_all x2, blocking collectives, exchange(): return lax.all_to_all(parts, axes, 0, 0, tiled=True)  42.1 us
    all_to_all x2, waiting for transfers between devices, exchange(): return lax.all_to_all(parts, axes, 0, 0, tiled=True)  33.5 us
    all_to_all x2, starting transfers between devices, exchange(): return lax.all_to_all(parts, axes, 0, 0, tiled=True)  21.2 us
    ppermute x1, starting transfers between devices, body(): other = lax.ppermute(mine, 'core', [(0, 1), (1, 0)])  4.77 us
    pallas_call x1, Pallas kernels, body(): call(functools.partial(factor_kernel, n_r), [((n_r * n_z, group, LANES),...  4.34 us
    pallas_call x1, Pallas kernels, body(): call(rows_kernel, [((rows, width), F32), ((tokens, wide), BF16)], [SMEM]...  3.91 us
    unnamed x13, local copies, waits for them, and re-layouts  3.31 us
    pallas_call x1, Pallas kernels, body(): call(functools.partial(far_kernel, limit), [*whole, ((rows, width), F32)]...  3.1 us
  transfers between devices with their start and end apart: 4, of which 2 were waited for; matrix products, arithmetic and copies ran while one was open for 2% of the time, Pallas kernels for 9%

profile of v7, /device:TPU:1, one launch (start us, length us, event | category | flops | bytes accessed | tf_op | source)
XLA Modules:
  0.0 139.9 jit_solution(11788325490634259511)
XLA Ops:
  7.2 2.5 %shard_map.93 = f32[16,16,896]{2,1,0:T(8,128)} custom-call(s32[1]{0:T(128)} %bitcast.t_ref, bf16[128,512]{1,0:T(8,128)(2,1)} %x_ref.3, bf16[16,128]{1,0:T(8,128)(2,1)} %c_ref.5, f32[16,8192]{1,0:T(8,128)} %bitcast.22, f32[32,8192]{1,0:T(8,128)} %q_ref.3), custom_call_target="tpu_custom_call" | custom-call | bytes 3145728 | tf_op jit(solution)/shard_map/pallas_call | solution.py:271
  9.7 11.8 %all-to-all-start = ((f32[16,16,896]{2,1,0:T(8,128)}), f32[16,16,896]{2,1,0:T(8,128)S(1)}, u32[]{:S(2)}, u32[]{:S(2)}) async-start(f32[16,16,896]{2,1,0:T(8,128)} %shard_map.93), calls=%async_computation | async-start | bytes 1835008 | tf_op jit(solution)/shard_map/all_to_all | solution.py:29
  21.5 0.0 all-gather.3.cloned.1.call-start
  21.6 1.0 copy.15
  22.6 0.2 copy.13
  22.8 0.0 copy-start
  22.8 1.0 copy-done
  23.8 1.2 copy-done.2
  25.0 0.9 shard_map.94.pe_ref
  26.0 0.8 pad_maximum_fusion
  26.8 20.1 %all-to-all-done.got_ref = f32[16,16,896]{2,1,0:T(8,128)S(1)} async-done(((f32[16,16,896]{2,1,0:T(8,128)}), f32[16,16,896]{2,1,0:T(8,128)S(1)}, u32[]{:S(2)}, u32[]{:S(2)}) %all-to-all-start) | async-done | bytes 917536 | tf_op jit(solution)/shard_map/all_to_all | solution.py:29
  46.8 0.0 all-gather.3.cloned.1.call-update
  46.8 1.3 shard_map.95
  48.1 0.0 copy-start.1
  48.1 29.4 %all_to_all.20.got_ref = f32[32,36,128]{2,1,0:T(8,128)S(1)} all-to-all(f32[32,36,128]{2,1,0:T(8,128)S(1)} %get-tuple-element.34), channel_id=1, replica_groups=mesh['y'=8,'x'=4,'z'=8,'core'=2] {'y','x'}, dimensions={0} | all-to-all | bytes 1179648 | tf_op jit(solution)/shard_map/all_to_all | solution.py:29
  77.5 0.5 shard_map.97
  78.0 12.7 %all_to_all.21 = f32[16,8,128]{2,1,0:T(8,128)S(1)} all-to-all(f32[16,8,128]{2,1,0:T(8,128)S(1)} %broadcast_in_dim.21), channel_id=1, replica_groups=mesh['y'=8,'x'=4,'z'=8,'core'=2] {'z','core'}, dimensions={0} | all-to-all | bytes 131072 | tf_op jit(solution)/shard_map/all_to_all | solution.py:29
  90.8 4.3 %shard_map.98 = (f32[256,4,128]{2,1,0:T(4,128)}, f32[32,32]{1,0:T(8,128)S(1)}, f32[32,32]{1,0:T(8,128)S(1)}) custom-call(f32[128,128]{1,0:T(8,128)S(1)} %bitcast.28, f32[16,512]{1,0:T(8,128)S(1)} %get-tuple-element.36.total_ref), custom_call_target="tpu_custom_call" | custom-call | flops 536870912 | bytes 1048576 | tf_op jit(solution)/shard_map/pallas_call | solution.py:309
  95.1 9.4 %all-to-all-start.3 = ((f32[256,4,128]{2,1,0:T(4,128)}), f32[256,4,128]{2,1,0:T(4,128)S(1)}, u32[]{:S(2)}, u32[]{:S(2)}) async-start(f32[256,4,128]{2,1,0:T(4,128)} %get-tuple-element.37), calls=%async_computation.3 | async-start | bytes 1048576 | tf_op jit(solution)/shard_map/all_to_all | solution.py:29
  104.5 0.1 reshape.39
  104.6 0.1 fusion.2
  104.8 0.2 fusion.3
  105.0 0.2 tile.21
  105.1 0.0 all-gather.3.cloned.1.call-done
  105.2 3.9 %shard_map.96 = (f32[16,8192]{1,0:T(8,128)S(1)}, bf16[128,512]{1,0:T(8,128)(2,1)}) custom-call(s32[1]{0:T(128)} %bitcast.t_ref, bf16[16,128]{1,0:T(8,128)(2,1)S(1)} %copy-done.5, bf16[256,128]{1,0:T(8,128)(2,1)S(1)} %get-tuple-element.31.cot_ref, bf16[16,384,512]{2,1,0:T(8,128)(2,1)} %bitcast.29), custom_call_target="tpu_custom_call" | custom-call | flops 268435456 | bytes 8388608 | tf_op jit(solution)/shard_map/pallas_call | solution.py:317
  109.1 13.4 %all-to-all-done.3 = f32[256,4,128]{2,1,0:T(4,128)S(1)} async-done(((f32[256,4,128]{2,1,0:T(4,128)}), f32[256,4,128]{2,1,0:T(4,128)S(1)}, u32[]{:S(2)}, u32[]{:S(2)}) %all-to-all-start.3) | async-done | bytes 524320 | tf_op jit(solution)/shard_map/all_to_all | solution.py:29
  122.5 4.8 %collective-permute-start = (f32[256,4,128]{2,1,0:T(4,128)S(1)}, f32[256,4,128]{2,1,0:T(4,128)S(1)}, u32[]{:S(2)}, u32[]{:S(2)}) collective-permute-start(f32[256,4,128]{2,1,0:T(4,128)S(1)} %all-to-all-done.3), channel_id=1, source_target_pairs={{0,1},{1,0},{2,3},{3,2},{4,5},{5,4},{6,7},{7,6},{8,9},{9,8},{10,11... | collective-permute-start | bytes 1572872 | tf_op jit(solution)/shard_map/ppermute | solution.py:333
  127.3 0.1 fusion.1
  127.4 0.1 tile.9.basis_ref
  127.5 0.1 fusion.weigh_ref
  127.7 2.2 %shard_map.99 = (f32[32,8192]{1,0:T(8,128)}, f32[16,8192]{1,0:T(8,128)}, f32[8,16,512]{2,1,0:T(8,128)S(1)}, f32[128,128]{1,0:T(8,128)S(1)}) custom-call(s32[1]{0:T(128)} %bitcast.5.core_ref, f32[8,128,128]{2,1,0:T(8,128)S(1)} %bitcast.27, f32[16,128]{1,0:T(8,128)S(1)} %tile.9.basis_ref, f32[16,8192]{1,0:T(8,128)S(1)} %bitcast.24, ...), custom_call_target="tpu_custom_call" | custom-call | flops 1073741824 | bytes 3145728 | tf_op jit(solution)/shard_map/pallas_call | solution.py:342
  129.9 3.1 %shard_map.100 = (f32[32,8192]{1,0:T(8,128)}, f32[16,8192]{1,0:T(8,128)}, f32[16,8192]{1,0:T(8,128)}) custom-call(s32[1]{0:T(128)} %bitcast.5.core_ref, f32[8,128,128]{2,1,0:T(8,128)S(1)} %bitcast.26, f32[16,128]{1,0:T(8,128)S(1)} %tile.9.basis_ref, f32[16,8192]{1,0:T(8,128)S(1)} %bitcast.25, ...), custom_call_target="tpu_custom_call", output_to_operand_aliasing={{0}: (9, {}), {1}: (10, {})} | custom-call | flops 1073741824 | bytes 4194304 | tf_op jit(solution)/shard_map/pallas_call | solution.py:351
  (16 shorter events, 0.1 us)
Async XLA Ops:
  7.2 18.8 %copy-start.3 = (bf16[128,512]{1,0:T(8,128)(2,1)S(1)}, bf16[128,512]{1,0:T(8,128)(2,1)}, u32[]{:S(2)}) copy-start(bf16[128,512]{1,0:T(8,128)(2,1)} %x_ref.3) | copy-start | bytes 393220
  7.2 39.7 %copy-start.5 = (bf16[16,128]{1,0:T(8,128)(2,1)S(1)}, bf16[16,128]{1,0:T(8,128)(2,1)}, u32[]{:S(2)}) copy-start(bf16[16,128]{1,0:T(8,128)(2,1)} %c_ref.5) | copy-start | bytes 12292
  9.7 37.1 %all-to-all-start = ((f32[16,16,896]{2,1,0:T(8,128)}), f32[16,16,896]{2,1,0:T(8,128)S(1)}, u32[]{:S(2)}, u32[]{:S(2)}) async-start(f32[16,16,896]{2,1,0:T(8,128)} %shard_map.93), calls=%async_computation | async-start | bytes 1835008 | tf_op jit(solution)/shard_map/all_to_all | solution.py:29
  21.5 83.6 %all-gather.3.cloned.1.call-start = ((), (), s32[]{:S(2)}) async-start(), calls=%async_computation.4 | async-start | bytes 6684672 | tf_op jit(solution)/shard_map/all_gather | solution.py:293
  22.8 1.0 copy-start
  23.8 1.2 copy-start.2
  48.1 79.5 %copy-start.1 = (f32[1,16,8192]{2,1,0:T(8,128)S(1)}, f32[1,16,8192]{2,1,0:T(8,128)}, u32[]{:S(2)}) copy-start(f32[1,16,8192]{2,1,0:T(8,128)} %param.9) | copy-start | bytes 1572868
  95.1 34.8 %copy-start.4 = (f32[16,8192]{1,0:T(8,128)S(1)}, f32[16,8192]{1,0:T(8,128)}, u32[]{:S(2)}) copy-start(f32[16,8192]{1,0:T(8,128)} %m_ref.1) | copy-start | bytes 1572868
  95.1 27.4 %all-to-all-start.3 = ((f32[256,4,128]{2,1,0:T(4,128)}), f32[256,4,128]{2,1,0:T(4,128)S(1)}, u32[]{:S(2)}, u32[]{:S(2)}) async-start(f32[256,4,128]{2,1,0:T(4,128)} %get-tuple-element.37), calls=%async_computation.3 | async-start | bytes 1048576 | tf_op jit(solution)/shard_map/all_to_all | solution.py:29
  122.5 7.4 %collective-permute-start = (f32[256,4,128]{2,1,0:T(4,128)S(1)}, f32[256,4,128]{2,1,0:T(4,128)S(1)}, u32[]{:S(2)}, u32[]{:S(2)}) collective-permute-start(f32[256,4,128]{2,1,0:T(4,128)S(1)} %all-to-all-done.3), channel_id=1, source_target_pairs={{0,1},{1,0},{2,3},{3,2},{4,5},{5,4},{6,7},{7,6},{8,9},{9,8},{10,11... | collective-permute-start | bytes 1572872 | tf_op jit(solution)/shard_map/ppermute | solution.py:333
Sparse Core Ops, SparseCore 0:
  47.0 48.2 all-gather.2

commit v8 on v7

--- a/solution.py
+++ b/solution.py
@@ -56,6 +56,11 @@
 
 def dot(a, b, precision=HIGHEST):
     return jnp.dot(a, b, precision=precision, preferred_element_type=F32)
+
+
+def lane_halves(ff_win):
+    halves = max(ff_win // LANES, 1)
+    return halves, ff_win // halves
 
 
 def fold_rows(tiled, group):
@@ -100,7 +105,7 @@
     pe_ref[...] = nt(e_ref[...], q_ref[...])
 
 
-def merge_kernel(got_ref, x_ref, c_ref, pe_ref, send_ref, cot_ref):
+def merge_kernel(got_ref, x_ref, c_ref, pe_ref, send_ref, cot_ref, turned_ref):
     n_t, rows, _ = got_ref.shape
     tokens, wide = x_ref.shape
     n_r = send_ref.shape[0]
@@ -128,14 +133,15 @@
         piece = rest.astype(BF16)
         turned += nt(turn, piece, None)
         rest -= piece.astype(F32)
-    halves = ff_win // LANES if ff_win >= LANES else 1
-    width = ff_win // halves
+    turned_ref[...] = turned
+    halves, width = lane_halves(ff_win)
     for k in range(n_r):
         for h in range(halves):
-            send_ref[k, h * own : (h + 1) * own, :width] = turned[
-                k * own : (k + 1) * own, h * width : (h + 1) * width
-            ]
-        send_ref[k, halves * own :, :] = p_pack[: send_ref.shape[1] - halves * own]
+            for g in range(own // 4):
+                send_ref[k, h * (own // 4) + g, :, :width] = turned_ref[
+                    k * own + 4 * g : k * own + 4 * g + 4, h * width : (h + 1) * width
+                ]
+        send_ref[k, halves * (own // 4)] = p_pack[:4]
 
 
 def rows_kernel(t_ref, c_ref, cot_ref, got_ref, g_ref, dx_ref, w):
@@ -149,40 +155,47 @@
     dx_ref[...] = tn(cot_ref[...], w[...], None).astype(BF16)
 
 
-def sum_kernel(n_t, got_ref, total_ref, pack_ref):
+def sum_kernel(n_t, got_ref, total_ref, pack_ref, scratch):
     own, long = total_ref.shape
     ff_win = long // 2
     rows = ff_win // n_t
+    halves, width = lane_halves(ff_win)
     got = jnp.sum(got_ref[...], 0)
-    pack = got[got.shape[0] - 4 :]
-    pack_ref[...] = jnp.concatenate([pack, jnp.zeros_like(pack)], 0)
-    halves = ff_win // LANES if ff_win >= LANES else 1
-    width = ff_win // halves
+    pack_ref[...] = jnp.broadcast_to(got[-1][None], pack_ref.shape)
     total = jnp.zeros(total_ref.shape, F32)
     for h in range(halves):
+        for g in range(own // 4):
+            scratch[h, 4 * g : 4 * g + 4, :] = got[h * (own // 4) + g]
         unit, lane = iota((width, long), 0) + h * width, iota((width, long), 1)
         t, b, a = unit // rows, unit % rows // 4, unit % 4
         move = (lane == b * (SUB * n_t) + t * SUB + a).astype(F32)
-        total += dot(got[h * own : (h + 1) * own, :width], move)
+        total += dot(scratch[h, :, :width], move)
     total_ref[...] = total
 
 
-def factor_kernel(n_r, pack_ref, total_ref, send_ref, gram_ref, inverse_ref):
-    span = pack_ref.shape[0]
+def factor_kernel(n_r, pack_ref, total_ref, send_ref, gram_ref, inverse_ref, held):
+    span = held.shape[0]
     own = total_ref.shape[0]
     rank = gram_ref.shape[0]
     group = own // 4
-    pack = pack_ref[...]
+    held[...] = jnp.zeros(held.shape, F32)
+    for k in range(pack_ref.shape[0]):
+        held[k * SUB : k * SUB + 4] = pack_ref[k]
+    pack = held[...]
     gram4 = tn(pack, pack)
     gram = sum(gram4[b * rank : (b + 1) * rank, b * rank : (b + 1) * rank] for b in range(4))
     gram_ref[...] = gram
     row, lane = iota((rank, LANES), 0), iota((rank, LANES), 1)
     work = jnp.concatenate([gram, jnp.zeros((rank, LANES - rank), F32)], 1)
     work = jnp.where(lane == row + rank, 1.0, work)
-    for j in range(rank):
-        pivot = work[j : j + 1, :]
-        factor = work[:, j : j + 1] / work[j : j + 1, j : j + 1]
-        work = jnp.where(row > j, work - factor * pivot, work)
+    for first in range(0, rank, 4):
+        columns = [jnp.broadcast_to(work[:, first + m : first + m + 1], work.shape) for m in range(4)]
+        for m in range(4):
+            j = first + m
+            factor = jnp.where(row > j, columns[m] * (1.0 / columns[m][j : j + 1, :]), 0.0)
+            work -= factor * work[j : j + 1, :]
+            for n in range(m + 1, 4):
+                columns[n] -= factor * columns[n][j : j + 1, :]
     diagonal = jnp.sum(jnp.where(lane == row, work, 0.0), 1, keepdims=True)
     inverse = (work * lax.rsqrt(diagonal))[:, rank : 2 * rank]
     inverse_ref[...] = inverse
@@ -210,10 +223,10 @@
         0,
     )
     copies = []
+    blocks = blocks_ref[...].reshape(n_z * LANES, LANES)
+    every = nt(stack, blocks)
     for z in range(n_z):
-        block = blocks_ref[z]
-        gram += tn(block, block)
-        both = nt(stack, block)
+        both = every[:, z * LANES : (z + 1) * LANES]
         start = pl.multiple_of((2 * z + near_core) * 4 * LANES, 4 * LANES)
         for b in range(4):
             near = both[LANES + b * rows : LANES + (b + 1) * rows]
@@ -227,7 +240,7 @@
         copies.append(pltpu.make_async_copy(error.at[z], error_hbm.at[:, span], sems.at[1, z]))
         copies[-2].start()
         copies[-1].start()
-    return gram, copies
+    return gram + tn(blocks, blocks), copies
 
 
 def near_kernel(core_ref, mine_ref, basis_ref, e_ref, g_ref, q_hbm, error_hbm, approx_ref, gram_ref, q, error, sems):
@@ -265,8 +278,8 @@
     ff_win = rows * n_t
     own = wide // n_r
     group = own // 4
+    halves, _ = lane_halves(ff_win)
     error = error_fb[0]
-    halves = ff_win // LANES if ff_win >= LANES else 1
 
     (first,) = call(
         first_kernel,
@@ -293,18 +306,20 @@
     bulk = lax.all_gather(bulk, T)
     second, cot_all = call(
         merge_kernel,
-        [((n_r, halves * own + 4, LANES), F32), ((ff_win, tokens), BF16)],
+        [((n_r, halves * own // 4 + 1, 4, LANES), F32), ((ff_win, tokens), BF16)],
         [VMEM] * 4,
         moved=2 * 2**20,
+        scratch_shapes=[pltpu.VMEM((wide, ff_win), F32)],
     )(first, tokens_x, cotangent, p_error)
     second = exchange(second, R)
     total_t, p_pack = call(
         functools.partial(sum_kernel, n_t),
-        [((own, 2 * ff_win), F32), ((SUB, LANES), F32)],
+        [((own, 2 * ff_win), F32), ((n_t, 4, LANES), F32)],
         [VMEM],
         moved=2**20,
+        scratch_shapes=[pltpu.VMEM((halves, own, LANES), F32)],
     )(second)
-    p_all = exchange(jnp.broadcast_to(p_pack[None], (n_t, SUB, LANES)), T)
+    p_all = exchange(p_pack, T)
 
     q_send, gram, inverse = call(
         functools.partial(factor_kernel, n_r),
@@ -312,7 +327,8 @@
         [VMEM] * 2,
         flops=2**29,
         moved=2**20,
-    )(p_all.reshape(n_t * SUB, LANES), total_t)
+        scratch_shapes=[pltpu.VMEM((n_t * SUB, LANES), F32)],
+    )(p_all, total_t)
     mine = exchange(q_send, CHIPS)
     grad_rows, input_grad = call(
         rows_kernel,
@@ -324,7 +340,7 @@
     )(t, cotangent, cot_all, bulk)
     mine, grad_rows = lax.optimization_barrier((mine, grad_rows))
     basis_gram = dot(dot(inverse, gram), inverse.T)
-    p_rows = p_pack[:4].reshape(4, 4, rank).transpose(1, 0, 2).reshape(rows, rank)
+    p_rows = p_pack[0].reshape(4, 4, rank).transpose(1, 0, 2).reshape(rows, rank)
     basis4 = jnp.tile(dot(p_rows, inverse.T), (1, 4))
     square = (LANES, LANES)
     weigh = jnp.where(

time: 140 us -> 136 us (0.971)
  blocking collectives: 42.1 us -> 40 us
  Pallas kernels: 18.8 us -> 16.8 us
    all_to_all x2, blocking collectives: 42.1 us -> 40 us  [exchange(): return lax.all_to_all(parts, axes, 0, 0, tiled=True)]
  transfers between devices with their start and end apart: 4 -> 4, of which waited for: 2 -> 2; matrix products, arithmetic and copies ran while one was open for 2% -> 2% of each run, Pallas kernels for 9% -> 8%
where the time goes in v8:
time: 136 us
  blocking collectives  40 us (29%)
  waiting for transfers between devices  34.2 us (25%)
  starting transfers between devices  25.1 us (18%)
  Pallas kernels  16.8 us (12%)
  between operations  14.2 us (10%)
  local copies, waits for them, and re-layouts  3.86 us (3%)
    all_to_all x2, blocking collectives, exchange(): return lax.all_to_all(parts, axes, 0, 0, tiled=True)  40 us
    all_to_all x2, waiting for transfers between devices, exchange(): return lax.all_to_all(parts, axes, 0, 0, tiled=True)  34.1 us
    all_to_all x2, starting transfers between devices, exchange(): return lax.all_to_all(parts, axes, 0, 0, tiled=True)  21.1 us
    ppermute x1, starting transfers between devices, body(): other = lax.ppermute(mine, 'core', [(0, 1), (1, 0)])  3.93 us
    pallas_call x1, Pallas kernels, body(): call(rows_kernel, [((rows, width), F32), ((tokens, wide), BF16)], [SMEM]...  3.91 us
    unnamed x13, local copies, waits for them, and re-layouts  3.31 us
    pallas_call x1, Pallas kernels, body(): call(functools.partial(factor_kernel, n_r), [((n_r * n_z, group, LANES),...  3.06 us
    pallas_call x1, Pallas kernels, body(): call(functools.partial(far_kernel, limit), [*whole, ((rows, width), F32)]...  2.86 us
  transfers between devices with their start and end apart: 4, of which 2 were waited for; matrix products, arithmetic and copies ran while one was open for 2% of the time, Pallas kernels for 8%

profile of v8, /device:TPU:1, one launch (start us, length us, event | category | flops | bytes accessed | tf_op | source)
XLA Modules:
  0.0 135.6 jit_solution(11215349858543149960)
XLA Ops:
  7.2 2.5 %shard_map.93 = f32[16,16,896]{2,1,0:T(8,128)} custom-call(s32[1]{0:T(128)} %bitcast.t_ref, bf16[128,512]{1,0:T(8,128)(2,1)} %x_ref.3, bf16[16,128]{1,0:T(8,128)(2,1)} %c_ref.5, f32[16,8192]{1,0:T(8,128)} %bitcast.21, f32[32,8192]{1,0:T(8,128)} %q_ref.3), custom_call_target="tpu_custom_call" | custom-call | bytes 3145728 | tf_op jit(solution)/shard_map/pallas_call | solution.py:284
  9.7 11.8 %all-to-all-start = ((f32[16,16,896]{2,1,0:T(8,128)}), f32[16,16,896]{2,1,0:T(8,128)S(1)}, u32[]{:S(2)}, u32[]{:S(2)}) async-start(f32[16,16,896]{2,1,0:T(8,128)} %shard_map.93), calls=%async_computation | async-start | bytes 1835008 | tf_op jit(solution)/shard_map/all_to_all | solution.py:29
  21.5 0.0 all-gather.3.cloned.1.call-start
  21.5 1.0 copy.15
  22.6 0.2 copy.13
  22.7 0.0 copy-start
  22.8 1.0 copy-done
  23.8 1.2 copy-done.2
  25.0 0.9 shard_map.94.pe_ref
  26.0 0.8 pad_maximum_fusion
  26.7 20.1 %all-to-all-done.got_ref = f32[16,16,896]{2,1,0:T(8,128)S(1)} async-done(((f32[16,16,896]{2,1,0:T(8,128)}), f32[16,16,896]{2,1,0:T(8,128)S(1)}, u32[]{:S(2)}, u32[]{:S(2)}) %all-to-all-start) | async-done | bytes 917536 | tf_op jit(solution)/shard_map/all_to_all | solution.py:29
  46.8 0.0 all-gather.3.cloned.1.call-update
  46.8 1.3 shard_map.95
  48.2 0.0 copy-start.1
  48.2 28.0 %all_to_all.20.got_ref = f32[32,9,4,128]{3,2,1,0:T(4,128)S(1)} all-to-all(f32[32,9,4,128]{3,2,1,0:T(4,128)S(1)} %get-tuple-element.34), channel_id=1, replica_groups=mesh['y'=8,'x'=4,'z'=8,'core'=2] {'y','x'}, dimensions={0} | all-to-all | bytes 1179648 | tf_op jit(solution)/shard_map/all_to_all | solution.py:29
  76.2 0.6 shard_map.97
  76.8 12.0 %all_to_all.21.pack_ref = f32[16,4,128]{2,1,0:T(4,128)S(1)} all-to-all(f32[16,4,128]{2,1,0:T(4,128)S(1)} %get-tuple-element.35), channel_id=1, replica_groups=mesh['y'=8,'x'=4,'z'=8,'core'=2] {'z','core'}, dimensions={0} | all-to-all | bytes 65536 | tf_op jit(solution)/shard_map/all_to_all | solution.py:29
  88.8 3.1 %shard_map.98 = (f32[256,4,128]{2,1,0:T(4,128)}, f32[32,32]{1,0:T(8,128)S(1)}, f32[32,32]{1,0:T(8,128)S(1)}) custom-call(f32[16,4,128]{2,1,0:T(4,128)S(1)} %all_to_all.21.pack_ref, f32[16,512]{1,0:T(8,128)S(1)} %get-tuple-element.36.total_ref), custom_call_target="tpu_custom_call" | custom-call | flops 536870912 | bytes 1048576 | tf_op jit(solution)/shard_map/pallas_call | solution.py:324
  91.8 9.3 %all-to-all-start.3 = ((f32[256,4,128]{2,1,0:T(4,128)}), f32[256,4,128]{2,1,0:T(4,128)S(1)}, u32[]{:S(2)}, u32[]{:S(2)}) async-start(f32[256,4,128]{2,1,0:T(4,128)} %get-tuple-element.37), calls=%async_computation.3 | async-start | bytes 1048576 | tf_op jit(solution)/shard_map/all_to_all | solution.py:29
  101.2 0.1 reshape_squeeze.3
  101.3 0.1 fusion.1
  101.4 0.1 tile.9.basis_ref
  101.5 0.1 fusion.2
  101.7 0.0 all-gather.3.cloned.1.call-done
  101.7 3.9 %shard_map.96 = (f32[16,8192]{1,0:T(8,128)S(1)}, bf16[128,512]{1,0:T(8,128)(2,1)}) custom-call(s32[1]{0:T(128)} %bitcast.t_ref, bf16[16,128]{1,0:T(8,128)(2,1)S(1)} %copy-done.5, bf16[256,128]{1,0:T(8,128)(2,1)S(1)} %get-tuple-element.31.cot_ref, bf16[16,384,512]{2,1,0:T(8,128)(2,1)} %bitcast.27), custom_call_target="tpu_custom_call" | custom-call | flops 268435456 | bytes 8388608 | tf_op jit(solution)/shard_map/pallas_call | solution.py:333
  105.6 14.1 %all-to-all-done.3 = f32[256,4,128]{2,1,0:T(4,128)S(1)} async-done(((f32[256,4,128]{2,1,0:T(4,128)}), f32[256,4,128]{2,1,0:T(4,128)S(1)}, u32[]{:S(2)}, u32[]{:S(2)}) %all-to-all-start.3) | async-done | bytes 524320 | tf_op jit(solution)/shard_map/all_to_all | solution.py:29
  119.7 3.9 %collective-permute-start = (f32[256,4,128]{2,1,0:T(4,128)S(1)}, f32[256,4,128]{2,1,0:T(4,128)S(1)}, u32[]{:S(2)}, u32[]{:S(2)}) collective-permute-start(f32[256,4,128]{2,1,0:T(4,128)S(1)} %all-to-all-done.3), channel_id=1, source_target_pairs={{0,1},{1,0},{2,3},{3,2},{4,5},{5,4},{6,7},{7,6},{8,9},{9,8},{10,11... | collective-permute-start | bytes 1572872 | tf_op jit(solution)/shard_map/ppermute | solution.py:349
  123.6 0.1 fusion.3
  123.8 0.2 tile.21
  124.0 0.1 fusion.weigh_ref
  124.1 1.7 %shard_map.99 = (f32[32,8192]{1,0:T(8,128)}, f32[16,8192]{1,0:T(8,128)}, f32[8,16,512]{2,1,0:T(8,128)S(1)}, f32[128,128]{1,0:T(8,128)S(1)}) custom-call(s32[1]{0:T(128)} %bitcast.5.core_ref, f32[8,128,128]{2,1,0:T(8,128)S(1)} %bitcast.26, f32[16,128]{1,0:T(8,128)S(1)} %tile.9.basis_ref, f32[16,8192]{1,0:T(8,128)S(1)} %bitcast.23, ...), custom_call_target="tpu_custom_call" | custom-call | flops 1073741824 | bytes 3145728 | tf_op jit(solution)/shard_map/pallas_call | solution.py:358
  125.8 2.9 %shard_map.100 = (f32[32,8192]{1,0:T(8,128)}, f32[16,8192]{1,0:T(8,128)}, f32[16,8192]{1,0:T(8,128)}) custom-call(s32[1]{0:T(128)} %bitcast.5.core_ref, f32[8,128,128]{2,1,0:T(8,128)S(1)} %bitcast.25, f32[16,128]{1,0:T(8,128)S(1)} %tile.9.basis_ref, f32[16,8192]{1,0:T(8,128)S(1)} %bitcast.24, ...), custom_call_target="tpu_custom_call", output_to_operand_aliasing={{0}: (9, {}), {1}: (10, {})} | custom-call | flops 1073741824 | bytes 4194304 | tf_op jit(solution)/shard_map/pallas_call | solution.py:367
  (15 shorter events, 0.1 us)
Async XLA Ops:
  7.2 39.7 %copy-start.5 = (bf16[16,128]{1,0:T(8,128)(2,1)S(1)}, bf16[16,128]{1,0:T(8,128)(2,1)}, u32[]{:S(2)}) copy-start(bf16[16,128]{1,0:T(8,128)(2,1)} %c_ref.5) | copy-start | bytes 12292
  7.2 18.8 %copy-start.3 = (bf16[128,512]{1,0:T(8,128)(2,1)S(1)}, bf16[128,512]{1,0:T(8,128)(2,1)}, u32[]{:S(2)}) copy-start(bf16[128,512]{1,0:T(8,128)(2,1)} %x_ref.3) | copy-start | bytes 393220
  9.7 37.1 %all-to-all-start = ((f32[16,16,896]{2,1,0:T(8,128)}), f32[16,16,896]{2,1,0:T(8,128)S(1)}, u32[]{:S(2)}, u32[]{:S(2)}) async-start(f32[16,16,896]{2,1,0:T(8,128)} %shard_map.93), calls=%async_computation | async-start | bytes 1835008 | tf_op jit(solution)/shard_map/all_to_all | solution.py:29
  21.5 80.2 %all-gather.3.cloned.1.call-start = ((), (), s32[]{:S(2)}) async-start(), calls=%async_computation.4 | async-start | bytes 6684672 | tf_op jit(solution)/shard_map/all_gather | solution.py:306
  22.7 1.0 copy-start
  23.8 1.2 copy-start.2
  48.2 75.9 %copy-start.1 = (f32[1,16,8192]{2,1,0:T(8,128)S(1)}, f32[1,16,8192]{2,1,0:T(8,128)}, u32[]{:S(2)}) copy-start(f32[1,16,8192]{2,1,0:T(8,128)} %param.9) | copy-start | bytes 1572868
  91.8 34.0 %copy-start.4 = (f32[16,8192]{1,0:T(8,128)S(1)}, f32[16,8192]{1,0:T(8,128)}, u32[]{:S(2)}) copy-start(f32[16,8192]{1,0:T(8,128)} %m_ref.1) | copy-start | bytes 1572868
  91.8 27.8 %all-to-all-start.3 = ((f32[256,4,128]{2,1,0:T(4,128)}), f32[256,4,128]{2,1,0:T(4,128)S(1)}, u32[]{:S(2)}, u32[]{:S(2)}) async-start(f32[256,4,128]{2,1,0:T(4,128)} %get-tuple-element.37), calls=%async_computation.3 | async-start | bytes 1048576 | tf_op jit(solution)/shard_map/all_to_all | solution.py:29
  119.7 6.2 %collective-permute-start = (f32[256,4,128]{2,1,0:T(4,128)S(1)}, f32[256,4,128]{2,1,0:T(4,128)S(1)}, u32[]{:S(2)}, u32[]{:S(2)}) collective-permute-start(f32[256,4,128]{2,1,0:T(4,128)S(1)} %all-to-all-done.3), channel_id=1, source_target_pairs={{0,1},{1,0},{2,3},{3,2},{4,5},{5,4},{6,7},{7,6},{8,9},{9,8},{10,11... | collective-permute-start | bytes 1572872 | tf_op jit(solution)/shard_map/ppermute | solution.py:349
Sparse Core Ops, SparseCore 0:
  46.9 47.5 all-gather.2

commit v9 on v8

--- a/solution.py
+++ b/solution.py
@@ -71,77 +71,109 @@
     return dot(pick, kept)
 
 
-def first_kernel(t_ref, x_ref, c_ref, e_ref, q_ref, send_ref, x, c, q, sems):
+def fetch(pairs, sems):
+    copies = [pltpu.make_async_copy(src, dst, sems.at[i]) for i, (src, dst) in enumerate(pairs)]
+    for copy in copies:
+        copy.start()
+    return copies
+
+
+def first_kernel(t_ref, x_ref, c_ref, q_ref, send_ref, x, c, q, sems):
     n_t, rows, _ = send_ref.shape
     tokens, wide = x_ref.shape
     start = pl.multiple_of(t_ref[0] * wide, wide)
-    copies = [
-        pltpu.make_async_copy(q_ref.at[:, pl.ds(start, wide)], q, sems.at[0]),
-        pltpu.make_async_copy(x_ref, x, sems.at[1]),
-        pltpu.make_async_copy(c_ref, c, sems.at[2]),
-    ]
-    for k in range(n_t):
-        copies.append(
-            pltpu.make_async_copy(
-                e_ref.at[:, pl.ds(k * wide, wide)], send_ref.at[k, :, pl.ds(0, wide)], sems.at[3 + k]
-            )
-        )
-    for copy in copies:
-        copy.start()
-    for copy in copies[:3]:
+    for copy in fetch([(q_ref.at[:, pl.ds(start, wide)], q), (x_ref, x), (c_ref, c)], sems):
         copy.wait()
     y = nt(q[...], x[...].astype(F32))
     cot = c[...].astype(F32)
     for k in range(n_t):
-        send_ref[k, :, wide : wide + tokens] = cot
+        send_ref[k, :, :tokens] = cot
         for g in range(y.shape[0] // rows):
-            at = wide + tokens + g * tokens
+            at = tokens + g * tokens
             send_ref[k, :, at : at + tokens] = y[g * rows : (g + 1) * rows]
-    for copy in copies[3:]:
+
+
+def tiles_kernel(x_ref, e_ref, *refs):
+    outs, e, sem = refs[:-2], refs[-2], refs[-1]
+    n_t = outs[0].shape[0]
+    copy = pltpu.make_async_copy(e_ref, e, sem)
+    copy.start()
+    copy.wait()
+    for d, out in enumerate(outs):
+        b = lax.rem(x_ref[0] + d, 4)
+        for k in range(n_t):
+            out[k] = e[:, pl.ds(pl.multiple_of((4 * k + b) * LANES, LANES), LANES)]
+
+
+def project_kernel(group, x_ref, e_ref, q_ref, xt_ref, pe_ref, x, e, q, sems):
+    copies = fetch([(x_ref, x), (e_ref, e), (q_ref, q)], sems)
+    wide = x_ref.shape[1]
+    own = 4 * group
+    out, col = iota((wide, wide), 0), iota((wide, wide), 1)
+    r, b, a = out // own, out % own // group, out % group
+    turn = (col == b * LANES + r * group + a).astype(BF16)
+    copies[0].wait()
+    xt_ref[...] = nt(turn, x[...], None).astype(BF16)
+    copies[1].wait()
+    copies[2].wait()
+    pe_ref[...] = nt(e[...], q[...])
+
+
+def turn_kernel(a_ref, b_ref, c_ref, d_ref, x_ref, p_ref, out_ref, xt_ref, pe_ref):
+    xt_ref[...] = x_ref[...]
+    pe_ref[...] = p_ref[...]
+    rest = (a_ref[...] + b_ref[...]) + (c_ref[...] + d_ref[...])
+    rest = rest.reshape(out_ref.shape[1], LANES)
+    same = (iota((LANES, LANES), 0) == iota((LANES, LANES), 1)).astype(BF16)
+    turned = jnp.zeros(out_ref.shape, F32)
+    for _ in range(3):
+        piece = rest.astype(BF16)
+        turned += nt(same, piece, None)
+        rest -= piece.astype(F32)
+    out_ref[...] = turned
+
+
+def pack_kernel(x_ref, w_ref, out_ref, sems):
+    tokens, wide = x_ref.shape
+    rows = w_ref.shape[0]
+    pairs = [(x_ref, out_ref.at[pl.ds(0, tokens)])]
+    for k in range(w_ref.shape[1] // wide):
+        pairs.append((w_ref.at[:, pl.ds(k * wide, wide)], out_ref.at[pl.ds(tokens + k * rows, rows)]))
+    for copy in fetch(pairs, sems):
         copy.wait()
 
 
-def project_kernel(e_ref, q_ref, pe_ref):
-    pe_ref[...] = nt(e_ref[...], q_ref[...])
-
-
-def merge_kernel(got_ref, x_ref, c_ref, pe_ref, send_ref, cot_ref, turned_ref):
+def merge_kernel(t_ref, got_ref, xt_ref, pe_ref, et_ref, send_ref, cot_ref, turned_ref):
     n_t, rows, _ = got_ref.shape
-    tokens, wide = x_ref.shape
+    wide, tokens = xt_ref.shape
     n_r = send_ref.shape[0]
     group = LANES // n_r
     ff_win = n_t * rows
-    cot = got_ref[:, :, wide : wide + tokens].reshape(ff_win, tokens).astype(BF16)
+    cot = got_ref[:, :, :tokens].reshape(ff_win, tokens).astype(BF16)
     cot_ref[...] = cot
-    y = jnp.sum(got_ref[:, :, wide + tokens :], 0)
+    y = jnp.sum(got_ref[:, :, tokens:], 0)
     folds = y.shape[1] // tokens
     y = jnp.concatenate([y[:, g * tokens : (g + 1) * tokens] for g in range(folds)], 0)
     rank = y.shape[0]
     y4 = jnp.concatenate([y] * (LANES // rank), 0)
     tile = (iota((rank, LANES), 1) % rank == iota((rank, LANES), 0)).astype(F32)
-    p4 = nt(c_ref[...].astype(F32), y4) + dot(pe_ref[...], tile)
+    p4 = nt(got_ref[t_ref[0], :, :tokens], y4) + dot(pe_ref[...], tile)
     p_pack = fold_rows(p4, rows // 4)
 
-    merged = got_ref[:, :, :wide].reshape(ff_win, wide) + dot(cot, x_ref[...], None)
-    out, col = iota((wide, wide), 0), iota((wide, wide), 1)
     own = wide // n_r
-    r, b, a = out // own, out % own // group, out % group
-    turn = (col == b * LANES + r * group + a).astype(BF16)
-    turned = jnp.zeros((wide, ff_win), F32)
-    rest = merged
-    for _ in range(3):
-        piece = rest.astype(BF16)
-        turned += nt(turn, piece, None)
-        rest -= piece.astype(F32)
-    turned_ref[...] = turned
+    turned_ref[...] = nt(xt_ref[...], cot, None)
     halves, width = lane_halves(ff_win)
+    at = halves * (own // 4)
     for k in range(n_r):
         for h in range(halves):
+            lanes = slice(h * width, (h + 1) * width)
             for g in range(own // 4):
-                send_ref[k, h * (own // 4) + g, :, :width] = turned_ref[
-                    k * own + 4 * g : k * own + 4 * g + 4, h * width : (h + 1) * width
-                ]
-        send_ref[k, halves * (own // 4)] = p_pack[:4]
+                row = k * own + 4 * g
+                send_ref[k, h * (own // 4) + g, :, :width] = turned_ref[row : row + 4, lanes]
+            for g in range(group // 4):
+                row = k * group + 4 * g
+                send_ref[k, at + 1 + h * (group // 4) + g, :, :width] = et_ref[row : row + 4, lanes]
+        send_ref[k, at] = p_pack[:4]
 
 
 def rows_kernel(t_ref, c_ref, cot_ref, got_ref, g_ref, dx_ref, w):
@@ -155,13 +187,17 @@
     dx_ref[...] = tn(cot_ref[...], w[...], None).astype(BF16)
 
 
-def sum_kernel(n_t, got_ref, total_ref, pack_ref, scratch):
+def sum_kernel(got_ref, total_ref, send_ref, scratch, error):
+    n_r = got_ref.shape[0]
+    n_t = send_ref.shape[0]
     own, long = total_ref.shape
     ff_win = long // 2
     rows = ff_win // n_t
+    group = own // 4
     halves, width = lane_halves(ff_win)
-    got = jnp.sum(got_ref[...], 0)
-    pack_ref[...] = jnp.broadcast_to(got[-1][None], pack_ref.shape)
+    at = halves * (own // 4)
+    got = jnp.sum(got_ref[:, : at + 1], 0)
+    p_pack = got[at]
     total = jnp.zeros(total_ref.shape, F32)
     for h in range(halves):
         for g in range(own // 4):
@@ -172,15 +208,50 @@
         total += dot(scratch[h, :, :width], move)
     total_ref[...] = total
 
-
-def factor_kernel(n_r, pack_ref, total_ref, send_ref, gram_ref, inverse_ref, held):
+    p8 = jnp.concatenate([p_pack, jnp.zeros_like(p_pack)], 0)
+    spread = (iota((rows, SUB), 0) % 4 == iota((rows, SUB), 1)).astype(F32)
+    p16 = dot(spread, p8)
+    p16 = jnp.where(iota(p16.shape, 0) // 4 == iota(p16.shape, 1) // 32, p16, 0.0)
+    square = (LANES, LANES)
+    p16 = dot(p16, (iota(square, 0) % 32 == iota(square, 1) % 32).astype(F32))
+    p_all = jnp.concatenate([p16] * n_t, 0)
+    for b in range(4):
+        part = sum(got_ref[r, at + 1 :] for r in range(b, n_r, 4))
+        for h in range(halves):
+            for g in range(group // 4):
+                row = b * group + 4 * g
+                error[row : row + 4, h * width : (h + 1) * width] = part[h * (group // 4) + g][:, :width]
+    pieces = []
+    for q in range(n_t // 4):
+        mask = iota(p_all.shape, 0) // rows == 4 * q + iota(p_all.shape, 1) // 32
+        out = dot(error[...], jnp.where(mask, p_all, 0.0))
+        rolled = [out] + [pltpu.roll(out, 32 * d, 1) for d in range(1, 4)]
+        row, lane = iota(out.shape, 0) // group, iota(out.shape, 1) // 32
+        for s in range(4):
+            kept = jnp.zeros(out.shape, F32)
+            for b in range(4):
+                kept = jnp.where((row == b) & (lane == b), rolled[(b - s) % 4], kept)
+            pieces.append(kept)
+    every = jnp.concatenate(pieces, 0)
+    tall = max(group, SUB)
+    pick_row, pick_col = iota((n_t * tall, n_t * own), 0), iota((n_t * tall, n_t * own), 1)
+    pick = (pick_row // tall == pick_col // own) & (pick_row % tall == pick_col % group)
+    folded = dot(pick.astype(F32), every)
+    for k in range(n_t):
+        send_ref[k, 0] = p_pack
+        for g in range(group // 4):
+            send_ref[k, 1 + g] = folded[k * tall + 4 * g : k * tall + 4 * g + 4]
+
+
+def factor_kernel(n_r, pack_ref, total_ref, send_ref, gram_ref, inverse_ref, held, wide):
+    wide[...] = jnp.zeros(wide.shape, F32)
     span = held.shape[0]
     own = total_ref.shape[0]
     rank = gram_ref.shape[0]
     group = own // 4
     held[...] = jnp.zeros(held.shape, F32)
     for k in range(pack_ref.shape[0]):
-        held[k * SUB : k * SUB + 4] = pack_ref[k]
+        held[k * SUB : k * SUB + 4] = pack_ref[k, 0]
     pack = held[...]
     gram4 = tn(pack, pack)
     gram = sum(gram4[b * rank : (b + 1) * rank, b * rank : (b + 1) * rank] for b in range(4))
@@ -206,6 +277,13 @@
     for b in range(4):
         part = dot(total[:, b * span : (b + 1) * span], pack)
         product = jnp.where(iota(part.shape, 1) // rank == b, part, product)
+    from_error = jnp.sum(pack_ref[:, 1:], 0)
+    for g in range(group // 4):
+        wide[4 * g : 4 * g + 4] = from_error[g]
+    tall = wide.shape[0]
+    spread = (iota((own, tall), 0) % group == iota((own, tall), 1)).astype(F32)
+    from_error = dot(spread, wide[...])
+    product += jnp.where(iota(product.shape, 0) // group == iota(product.shape, 1) // rank, from_error, 0.0)
     q4 = nt(product, inverse16) / n_r
     q_pack = fold_rows(q4, group)[:group]
     send_ref[...] = jnp.broadcast_to(q_pack[None], send_ref.shape)
@@ -283,43 +361,79 @@
 
     (first,) = call(
         first_kernel,
-        [((n_t, rows, wide + tokens + rank // rows * tokens), F32)],
-        [SMEM] + [HBM] * 4,
-        moved=3 * 2**20,
+        [((n_t, rows, tokens + rank // rows * tokens), F32)],
+        [SMEM] + [HBM] * 3,
+        moved=2**20,
         limit=None,
         scratch_shapes=[
             pltpu.VMEM(tokens_x.shape, BF16),
             pltpu.VMEM(cotangent.shape, BF16),
             pltpu.VMEM((rank, wide), F32),
-            pltpu.SemaphoreType.DMA((3 + n_t,)),
+            pltpu.SemaphoreType.DMA((3,)),
         ],
-    )(t, tokens_x, cotangent, error, q_prev)
-    w_parts = weight.reshape(rows, n_t, wide).transpose(1, 0, 2)
-    first, error_late = lax.optimization_barrier((first, error))
-    (p_error,) = call(
-        project_kernel, [((rows, rank), F32)], [VMEM] * 2, flops=2**27, moved=2 * 2**20
-    )(error_late, q_prev)
+    )(t, tokens_x, cotangent, q_prev)
+    first, error_late, x_late = lax.optimization_barrier((first, error, tokens_x))
+    tiles = call(
+        tiles_kernel,
+        [((n_t, rows, LANES), F32)] * 4,
+        [SMEM, HBM],
+        moved=2**20,
+        limit=None,
+        scratch_shapes=[pltpu.VMEM(error.shape, F32), pltpu.SemaphoreType.DMA(())],
+    )(lax.axis_index("x")[None], error_late)
+    tiles = [tiles[0]] + [
+        lax.ppermute(tiles[d], "x", [(i, (i + d) % 4) for i in range(4)]) for d in range(1, 4)
+    ]
+    x_t, p_error = call(
+        functools.partial(project_kernel, group),
+        [((wide, tokens), BF16), ((rows, rank), F32)],
+        [HBM] * 3,
+        flops=2**27,
+        moved=2 * 2**20,
+        limit=None,
+        scratch_shapes=[
+            pltpu.VMEM(tokens_x.shape, BF16),
+            pltpu.VMEM(error.shape, F32),
+            pltpu.VMEM(q_prev.shape, F32),
+            pltpu.SemaphoreType.DMA((3,)),
+        ],
+    )(x_late, error_late, q_prev)
+    error_t, x_t, p_error = call(
+        turn_kernel,
+        [((LANES, ff_win), F32), ((wide, tokens), BF16), ((rows, rank), F32)],
+        [VMEM] * 6,
+        moved=2**20,
+    )(*tiles, x_t, p_error)
+    (bulk,) = call(
+        pack_kernel,
+        [((tokens + rows * n_t, wide), BF16)],
+        [HBM] * 2,
+        [HBM],
+        moved=2**20,
+        limit=None,
+        scratch_shapes=[pltpu.SemaphoreType.DMA((1 + n_t,))],
+    )(x_late, weight)
     first = exchange(first, T)
-
-    bulk = jnp.concatenate([tokens_x, w_parts.reshape(rows * n_t, wide)], 0)
-    first, bulk, p_error = lax.optimization_barrier((first, bulk, p_error))
+    first, error_t, x_t, p_error, bulk = lax.optimization_barrier((first, error_t, x_t, p_error, bulk))
     bulk = lax.all_gather(bulk, T)
+    blocks_g, blocks_e = halves * own // 4, halves * group // 4
     second, cot_all = call(
         merge_kernel,
-        [((n_r, halves * own // 4 + 1, 4, LANES), F32), ((ff_win, tokens), BF16)],
-        [VMEM] * 4,
+        [((n_r, blocks_g + 1 + blocks_e, 4, LANES), F32), ((ff_win, tokens), BF16)],
+        [SMEM] + [VMEM] * 4,
         moved=2 * 2**20,
         scratch_shapes=[pltpu.VMEM((wide, ff_win), F32)],
-    )(first, tokens_x, cotangent, p_error)
+    )(t, first, x_t, p_error, error_t)
     second = exchange(second, R)
-    total_t, p_pack = call(
-        functools.partial(sum_kernel, n_t),
-        [((own, 2 * ff_win), F32), ((n_t, 4, LANES), F32)],
+    total_t, third = call(
+        sum_kernel,
+        [((own, 2 * ff_win), F32), ((n_t, 1 + group // 4, 4, LANES), F32)],
         [VMEM],
         moved=2**20,
-        scratch_shapes=[pltpu.VMEM((halves, own, LANES), F32)],
+        scratch_shapes=[pltpu.VMEM((halves, own, LANES), F32), pltpu.VMEM((own, ff_win), F32)],
     )(second)
-    p_all = exchange(p_pack, T)
+    p_pack = third[0, 0]
+    third = exchange(third, T)
 
     q_send, gram, inverse = call(
         functools.partial(factor_kernel, n_r),
@@ -327,8 +441,8 @@
         [VMEM] * 2,
         flops=2**29,
         moved=2**20,
-        scratch_shapes=[pltpu.VMEM((n_t * SUB, LANES), F32)],
-    )(p_all, total_t)
+        scratch_shapes=[pltpu.VMEM((n_t * SUB, LANES), F32), pltpu.VMEM((max(group, SUB), LANES), F32)],
+    )(third, total_t)
     mine = exchange(q_send, CHIPS)
     grad_rows, input_grad = call(
         rows_kernel,
@@ -338,14 +452,14 @@
         moved=8 * 2**20,
         scratch_shapes=[pltpu.VMEM((ff_win, wide), BF16)],
     )(t, cotangent, cot_all, bulk)
-    mine, grad_rows = lax.optimization_barrier((mine, grad_rows))
     basis_gram = dot(dot(inverse, gram), inverse.T)
-    p_rows = p_pack[0].reshape(4, 4, rank).transpose(1, 0, 2).reshape(rows, rank)
+    p_rows = p_pack.reshape(4, 4, rank).transpose(1, 0, 2).reshape(rows, rank)
     basis4 = jnp.tile(dot(p_rows, inverse.T), (1, 4))
     square = (LANES, LANES)
     weigh = jnp.where(
         iota(square, 0) // rank == iota(square, 1) // rank, jnp.tile(basis_gram, (4, 4)), 0.0
     )
+    mine, grad_rows, weigh, basis4 = lax.optimization_barrier((mine, grad_rows, weigh, basis4))
     other = lax.ppermute(mine, "core", [(0, 1), (1, 0)])
     blocks = (n_z, LANES, LANES)
     limit = CLIPPING * math.sqrt(ff_win * width)
@@ -379,7 +493,7 @@
 
 def solution(mesh):
     n_r, n_t = mesh.devices.shape
-    x = 4 if n_r > 4 else 2
+    x = 4
     split = Mesh(mesh.devices.reshape(n_r // x, x, n_t // 2, 2), (*R, *T))
     placed = (P(R, T), P(T, R), P(T, None), P(R, T, None), P(T, None), P())
     return jax.shard_map(

time: 136 us -> 147 us (1.081)
  waiting for transfers between devices: 34.2 us -> 13.4 us
  Pallas kernels: 16.8 us -> 34.3 us
  starting transfers between devices: 25.1 us -> 36.3 us
  blocking collectives: 40 us -> 44.9 us
    all_to_all x2, waiting for transfers between devices: 34.1 us -> 13.3 us  [exchange(): return lax.all_to_all(parts, axes, 0, 0, tiled=True)]
    pallas_call x4 -> x7, Pallas kernels: 5.28 us -> 22.8 us  [the longest x1 13.2 us: body(): call(pack_kernel, [((tokens + rows * n_t, wide), BF16)], [HBM] * 2, [HBM]...]
    ppermute x0 -> x3, starting transfers between devices: none -> 10.6 us  [body(): lax.ppermute(tiles[d], 'x', [(i, (i + d) % 4) for i in range(4)])]
    all_to_all x2, blocking collectives: 40 us -> 44.9 us  [exchange(): return lax.all_to_all(parts, axes, 0, 0, tiled=True)]
    unnamed x13 -> x12, local copies, waits for them, and re-layouts: 3.31 us -> 2.52 us
  transfers between devices with their start and end apart: 4 -> 7, of which waited for: 2 -> 1; matrix products, arithmetic and copies ran while one was open for 2% -> 1% of each run, Pallas kernels for 8% -> 20%
where the time goes in v9:
time: 147 us
  blocking collectives  44.9 us (31%)
  starting transfers between devices  36.3 us (25%)
  Pallas kernels  34.3 us (23%)
  between operations  14.3 us (10%)
  waiting for transfers between devices  13.4 us (9%)
  local copies, waits for them, and re-layouts  2.92 us (2%)
    all_to_all x2, blocking collectives, exchange(): return lax.all_to_all(parts, axes, 0, 0, tiled=True)  44.9 us
    all_to_all x2, starting transfers between devices, exchange(): return lax.all_to_all(parts, axes, 0, 0, tiled=True)  21.6 us
    all_to_all x2, waiting for transfers between devices, exchange(): return lax.all_to_all(parts, axes, 0, 0, tiled=True)  13.3 us
    pallas_call x1, Pallas kernels, body(): call(pack_kernel, [((tokens + rows * n_t, wide), BF16)], [HBM] * 2, [HBM]...  13.2 us
    ppermute x3, starting transfers between devices, body(): lax.ppermute(tiles[d], 'x', [(i, (i + d) % 4) for i in range(4)])  10.6 us
    ppermute x1, starting transfers between devices, body(): other = lax.ppermute(mine, 'core', [(0, 1), (1, 0)])  4.18 us
    pallas_call x1, Pallas kernels, body(): call(rows_kernel, [((rows, width), F32), ((tokens, wide), BF16)], [SMEM]...  3.91 us
    pallas_call x1, Pallas kernels, body(): call(functools.partial(project_kernel, group), [((wide, tokens), BF16), (...  3.18 us
  transfers between devices with their start and end apart: 7, of which 1 were waited for; matrix products, arithmetic and copies ran while one was open for 1% of the time, Pallas kernels for 20%

profile of v9, /device:TPU:1, one launch (start us, length us, event | category | flops | bytes accessed | tf_op | source)
XLA Modules:
  0.0 146.7 jit_solution(9297370179662273316)
XLA Ops:
  7.2 2.1 %shard_map.93 = f32[16,16,384]{2,1,0:T(8,128)} custom-call(s32[1]{0:T(128)} %bitcast.t_ref, bf16[128,512]{1,0:T(8,128)(2,1)} %x_ref.3, bf16[16,128]{1,0:T(8,128)(2,1)} %c_ref.3, f32[32,8192]{1,0:T(8,128)} %q_ref.3), custom_call_target="tpu_custom_call" | custom-call | bytes 1048576 | tf_op jit(solution)/shard_map/pallas_call | solution.py:362
  9.3 11.8 %all-to-all-start = ((f32[16,16,384]{2,1,0:T(8,128)}), f32[16,16,384]{2,1,0:T(8,128)S(1)}, u32[]{:S(2)}, u32[]{:S(2)}) async-start(f32[16,16,384]{2,1,0:T(8,128)} %shard_map.93), calls=%async_computation | async-start | bytes 786432 | tf_op jit(solution)/shard_map/all_to_all | solution.py:29
  21.1 0.0 all-gather.3.cloned.1.call-start
  21.2 1.9 %shard_map.94 = (f32[16,16,128]{2,1,0:T(8,128)}, f32[16,16,128]{2,1,0:T(8,128)}, f32[16,16,128]{2,1,0:T(8,128)}, f32[16,16,128]{2,1,0:T(8,128)}) custom-call(s32[1]{0:T(128)} %bitcast.2.x_ref, f32[16,8192]{1,0:T(8,128)} %bitcast.17), custom_call_target="tpu_custom_call" | custom-call | bytes 1048576 | tf_op jit(solution)/shard_map/pallas_call | solution.py:376
  23.1 3.1 %collective-permute-start = (f32[16,16,128]{2,1,0:T(8,128)}, f32[16,16,128]{2,1,0:T(8,128)S(1)}, u32[]{:S(2)}, u32[]{:S(2)}) collective-permute-start(f32[16,16,128]{2,1,0:T(8,128)} %get-tuple-element.44), channel_id=1, source_target_pairs={{0,16},{16,32},{32,48},{48,0},{1,17},{17,33},{33,49},{49,1},{2,18}... | collective-permute-start | bytes 393224 | tf_op jit(solution)/shard_map/ppermute | solution.py:385
  26.2 4.4 %collective-permute-start.1 = (f32[16,16,128]{2,1,0:T(8,128)}, f32[16,16,128]{2,1,0:T(8,128)S(1)}, u32[]{:S(2)}, u32[]{:S(2)}) collective-permute-start(f32[16,16,128]{2,1,0:T(8,128)} %get-tuple-element.45), channel_id=1, source_target_pairs={{0,32},{16,48},{32,0},{48,16},{1,33},{17,49},{33,1},{49,17},{2,34}... | collective-permute-start | bytes 393224 | tf_op jit(solution)/shard_map/ppermute | solution.py:385
  30.6 3.1 %collective-permute-start.2 = (f32[16,16,128]{2,1,0:T(8,128)}, f32[16,16,128]{2,1,0:T(8,128)S(1)}, u32[]{:S(2)}, u32[]{:S(2)}) collective-permute-start(f32[16,16,128]{2,1,0:T(8,128)} %get-tuple-element.46), channel_id=1, source_target_pairs={{0,48},{16,0},{32,16},{48,32},{1,49},{17,1},{33,17},{49,33},{2,50}... | collective-permute-start | bytes 393224 | tf_op jit(solution)/shard_map/ppermute | solution.py:385
  33.7 13.2 %shard_map.97 = bf16[384,512]{1,0:T(8,128)(2,1)} custom-call(bf16[128,512]{1,0:T(8,128)(2,1)} %x_ref.3, bf16[16,8192]{1,0:T(8,128)(2,1)} %w_ref.1), custom_call_target="tpu_custom_call" | custom-call | bytes 1048576 | tf_op jit(solution)/shard_map/pallas_call | solution.py:407
  46.8 3.2 %shard_map.95 = (bf16[512,128]{1,0:T(8,128)(2,1)}, f32[16,32]{1,0:T(8,128)}) custom-call(bf16[128,512]{1,0:T(8,128)(2,1)} %x_ref.3, f32[16,8192]{1,0:T(8,128)} %bitcast.18, f32[32,8192]{1,0:T(8,128)} %q_ref.3), custom_call_target="tpu_custom_call" | custom-call | flops 134217728 | bytes 2097152 | tf_op jit(solution)/shard_map/pallas_call | solution.py:387
  50.1 0.9 copy-done.2
  51.0 0.9 copy-done.3
  51.9 0.7 copy-done.5
  52.6 0.2 shard_map.96
  52.8 0.7 shard_map.98
  53.5 27.2 %all_to_all.20.got_ref = f32[32,11,4,128]{3,2,1,0:T(4,128)S(1)} all-to-all(f32[32,11,4,128]{3,2,1,0:T(4,128)S(1)} %get-tuple-element.60), channel_id=1, replica_groups=mesh['y'=8,'x'=4,'z'=8,'core'=2] {'y','x'}, dimensions={0} | all-to-all | bytes 1441792 | tf_op jit(solution)/shard_map/all_to_all | solution.py:29
  80.7 1.5 %shard_map.100 = (f32[16,512]{1,0:T(8,128)S(1)}, f32[16,2,4,128]{3,2,1,0:T(4,128)S(1)}) custom-call(f32[32,11,4,128]{3,2,1,0:T(4,128)S(1)} %all_to_all.20.got_ref), custom_call_target="tpu_custom_call" | custom-call | bytes 1048576 | tf_op jit(solution)/shard_map/pallas_call | solution.py:428
  82.2 17.7 %all_to_all.21.pack_ref = f32[16,2,4,128]{3,2,1,0:T(4,128)S(1)} all-to-all(f32[16,2,4,128]{3,2,1,0:T(4,128)S(1)} %get-tuple-element.61), channel_id=1, replica_groups=mesh['y'=8,'x'=4,'z'=8,'core'=2] {'z','core'}, dimensions={0} | all-to-all | bytes 131072 | tf_op jit(solution)/shard_map/all_to_all | solution.py:29
  100.0 3.1 %shard_map.101 = (f32[256,4,128]{2,1,0:T(4,128)}, f32[32,32]{1,0:T(8,128)S(1)}, f32[32,32]{1,0:T(8,128)S(1)}) custom-call(f32[16,2,4,128]{3,2,1,0:T(4,128)S(1)} %all_to_all.21.pack_ref, f32[16,512]{1,0:T(8,128)S(1)} %get-tuple-element.62.total_ref), custom_call_target="tpu_custom_call" | custom-call | flops 536870912 | bytes 1048576 | tf_op jit(solution)/shard_map/pallas_call | solution.py:438
  103.0 9.7 %all-to-all-start.3 = ((f32[256,4,128]{2,1,0:T(4,128)}), f32[256,4,128]{2,1,0:T(4,128)S(1)}, u32[]{:S(2)}, u32[]{:S(2)}) async-start(f32[256,4,128]{2,1,0:T(4,128)} %get-tuple-element.63), calls=%async_computation.3 | async-start | bytes 1048576 | tf_op jit(solution)/shard_map/all_to_all | solution.py:29
  112.8 0.1 reshape_squeeze.3
  112.9 0.1 fusion.3
  113.0 0.1 tile.21.basis_ref
  113.1 0.1 fusion.1
  113.3 0.2 fusion.2
  113.5 0.2 tile.9
  113.6 0.1 fusion.weigh_ref
  113.8 0.0 all-gather.3.cloned.1.call-done
  113.8 3.9 %shard_map.99 = (f32[16,8192]{1,0:T(8,128)S(1)}, bf16[128,512]{1,0:T(8,128)(2,1)}) custom-call(s32[1]{0:T(128)} %bitcast.t_ref, bf16[16,128]{1,0:T(8,128)(2,1)S(1)} %copy-done.4, bf16[256,128]{1,0:T(8,128)(2,1)S(1)} %get-tuple-element.57.cot_ref, bf16[16,384,512]{2,1,0:T(8,128)(2,1)} %bitcast.23), custom_call_target="tpu_custom_call" | custom-call | flops 268435456 | bytes 8388608 | tf_op jit(solution)/shard_map/pallas_call | solution.py:447
  117.7 13.3 %all-to-all-done.3 = f32[256,4,128]{2,1,0:T(4,128)S(1)} async-done(((f32[256,4,128]{2,1,0:T(4,128)}), f32[256,4,128]{2,1,0:T(4,128)S(1)}, u32[]{:S(2)}, u32[]{:S(2)}) %all-to-all-start.3) | async-done | bytes 524320 | tf_op jit(solution)/shard_map/all_to_all | solution.py:29
  131.1 4.2 %collective-permute-start.3 = (f32[256,4,128]{2,1,0:T(4,128)S(1)}, f32[256,4,128]{2,1,0:T(4,128)S(1)}, u32[]{:S(2)}, u32[]{:S(2)}) collective-permute-start(f32[256,4,128]{2,1,0:T(4,128)S(1)} %all-to-all-done.3), channel_id=1, source_target_pairs={{0,1},{1,0},{2,3},{3,2},{4,5},{5,4},{6,7},{7,6},{8,9},{9,8},{10,11... | collective-permute-start | bytes 1572872 | tf_op jit(solution)/shard_map/ppermute | solution.py:463
  135.3 1.7 %shard_map.102 = (f32[32,8192]{1,0:T(8,128)}, f32[16,8192]{1,0:T(8,128)}, f32[8,16,512]{2,1,0:T(8,128)S(1)}, f32[128,128]{1,0:T(8,128)S(1)}) custom-call(s32[1]{0:T(128)} %bitcast.4.core_ref, f32[8,128,128]{2,1,0:T(8,128)S(1)} %bitcast.22, f32[16,128]{1,0:T(8,128)S(1)} %tile.21.basis_ref, f32[16,8192]{1,0:T(8,128)S(1)} %bitcast.19, ...), custom_call_target="tpu_custom_call" | custom-call | flops 1073741824 | bytes 3145728 | tf_op jit(solution)/shard_map/pallas_call | solution.py:472
  137.0 2.8 %shard_map.103 = (f32[32,8192]{1,0:T(8,128)}, f32[16,8192]{1,0:T(8,128)}, f32[16,8192]{1,0:T(8,128)}) custom-call(s32[1]{0:T(128)} %bitcast.4.core_ref, f32[8,128,128]{2,1,0:T(8,128)S(1)} %bitcast.21, f32[16,128]{1,0:T(8,128)S(1)} %tile.21.basis_ref, f32[16,8192]{1,0:T(8,128)S(1)} %bitcast.20, ...), custom_call_target="tpu_custom_call", output_to_operand_aliasing={{0}: (9, {}), {1}: (10, {})} | custom-call | flops 1073741824 | bytes 4194304 | tf_op jit(solution)/shard_map/pallas_call | solution.py:481
  (21 shorter events, 0.1 us)
Async XLA Ops:
  9.3 104.5 %copy-start.4 = (bf16[16,128]{1,0:T(8,128)(2,1)S(1)}, bf16[16,128]{1,0:T(8,128)(2,1)}, u32[]{:S(2)}) copy-start(bf16[16,128]{1,0:T(8,128)(2,1)} %c_ref.3) | copy-start | bytes 12292
  9.3 43.5 %all-to-all-start = ((f32[16,16,384]{2,1,0:T(8,128)}), f32[16,16,384]{2,1,0:T(8,128)S(1)}, u32[]{:S(2)}, u32[]{:S(2)}) async-start(f32[16,16,384]{2,1,0:T(8,128)} %shard_map.93), calls=%async_computation | async-start | bytes 786432 | tf_op jit(solution)/shard_map/all_to_all | solution.py:29
  21.1 92.7 %all-gather.3.cloned.1.call-start = ((), (), s32[]{:S(2)}) async-start(), calls=%async_computation.4 | async-start | bytes 6684672 | tf_op jit(solution)/shard_map/all_gather | solution.py:418
  23.1 27.0 %collective-permute-start = (f32[16,16,128]{2,1,0:T(8,128)}, f32[16,16,128]{2,1,0:T(8,128)S(1)}, u32[]{:S(2)}, u32[]{:S(2)}) collective-permute-start(f32[16,16,128]{2,1,0:T(8,128)} %get-tuple-element.44), channel_id=1, source_target_pairs={{0,16},{16,32},{32,48},{48,0},{1,17},{17,33},{33,49},{49,1},{2,18}... | collective-permute-start | bytes 393224 | tf_op jit(solution)/shard_map/ppermute | solution.py:385
  26.2 23.8 %collective-permute-start.1 = (f32[16,16,128]{2,1,0:T(8,128)}, f32[16,16,128]{2,1,0:T(8,128)S(1)}, u32[]{:S(2)}, u32[]{:S(2)}) collective-permute-start(f32[16,16,128]{2,1,0:T(8,128)} %get-tuple-element.45), channel_id=1, source_target_pairs={{0,32},{16,48},{32,0},{48,16},{1,33},{17,49},{33,1},{49,17},{2,34}... | collective-permute-start | bytes 393224 | tf_op jit(solution)/shard_map/ppermute | solution.py:385
  30.6 19.5 %collective-permute-start.2 = (f32[16,16,128]{2,1,0:T(8,128)}, f32[16,16,128]{2,1,0:T(8,128)S(1)}, u32[]{:S(2)}, u32[]{:S(2)}) collective-permute-start(f32[16,16,128]{2,1,0:T(8,128)} %get-tuple-element.46), channel_id=1, source_target_pairs={{0,48},{16,0},{32,16},{48,32},{1,49},{17,1},{33,17},{49,33},{2,50}... | collective-permute-start | bytes 393224 | tf_op jit(solution)/shard_map/ppermute | solution.py:385
  50.1 0.9 copy-start.2
  51.0 0.9 copy-start.3
  51.9 0.7 copy-start.5
  53.5 81.7 %copy-start = (f32[1,16,8192]{2,1,0:T(8,128)S(1)}, f32[1,16,8192]{2,1,0:T(8,128)}, u32[]{:S(2)}) copy-start(f32[1,16,8192]{2,1,0:T(8,128)} %param.9) | copy-start | bytes 1572868
  103.0 34.0 %copy-start.1 = (f32[16,8192]{1,0:T(8,128)S(1)}, f32[16,8192]{1,0:T(8,128)}, u32[]{:S(2)}) copy-start(f32[16,8192]{1,0:T(8,128)} %m_ref.1) | copy-start | bytes 1572868
  103.0 28.0 %all-to-all-start.3 = ((f32[256,4,128]{2,1,0:T(4,128)}), f32[256,4,128]{2,1,0:T(4,128)S(1)}, u32[]{:S(2)}, u32[]{:S(2)}) async-start(f32[256,4,128]{2,1,0:T(4,128)} %get-tuple-element.63), calls=%async_computation.3 | async-start | bytes 1048576 | tf_op jit(solution)/shard_map/all_to_all | solution.py:29
  131.1 5.9 %collective-permute-start.3 = (f32[256,4,128]{2,1,0:T(4,128)S(1)}, f32[256,4,128]{2,1,0:T(4,128)S(1)}, u32[]{:S(2)}, u32[]{:S(2)}) collective-permute-start(f32[256,4,128]{2,1,0:T(4,128)S(1)} %all-to-all-done.3), channel_id=1, source_target_pairs={{0,1},{1,0},{2,3},{3,2},{4,5},{5,4},{6,7},{7,6},{8,9},{9,8},{10,11... | collective-permute-start | bytes 1572872 | tf_op jit(solution)/shard_map/ppermute | solution.py:463
Sparse Core Ops, SparseCore 0:
  53.0 50.5 all-gather.2

commit v10 on v9

--- a/solution.py
+++ b/solution.py
@@ -93,35 +93,30 @@
             send_ref[k, :, at : at + tokens] = y[g * rows : (g + 1) * rows]
 
 
-def tiles_kernel(x_ref, e_ref, *refs):
-    outs, e, sem = refs[:-2], refs[-2], refs[-1]
+def tiles_kernel(x_ref, e_ref, q_ref, *refs):
+    outs, pe_ref, (e, q, sems) = refs[:4], refs[4], refs[5:]
     n_t = outs[0].shape[0]
-    copy = pltpu.make_async_copy(e_ref, e, sem)
-    copy.start()
-    copy.wait()
+    copies = fetch([(e_ref, e), (q_ref, q)], sems)
+    copies[0].wait()
     for d, out in enumerate(outs):
         b = lax.rem(x_ref[0] + d, 4)
         for k in range(n_t):
             out[k] = e[:, pl.ds(pl.multiple_of((4 * k + b) * LANES, LANES), LANES)]
-
-
-def project_kernel(group, x_ref, e_ref, q_ref, xt_ref, pe_ref, x, e, q, sems):
-    copies = fetch([(x_ref, x), (e_ref, e), (q_ref, q)], sems)
-    wide = x_ref.shape[1]
-    own = 4 * group
-    out, col = iota((wide, wide), 0), iota((wide, wide), 1)
-    r, b, a = out // own, out % own // group, out % group
-    turn = (col == b * LANES + r * group + a).astype(BF16)
-    copies[0].wait()
-    xt_ref[...] = nt(turn, x[...], None).astype(BF16)
     copies[1].wait()
-    copies[2].wait()
     pe_ref[...] = nt(e[...], q[...])
 
 
-def turn_kernel(a_ref, b_ref, c_ref, d_ref, x_ref, p_ref, out_ref, xt_ref, pe_ref):
-    xt_ref[...] = x_ref[...]
+def pack_kernel(x_ref, w_ref, out_ref):
+    tokens, wide = x_ref.shape
+    rows = w_ref.shape[0]
+    out_ref[:tokens] = x_ref[...]
+    for k in range(w_ref.shape[1] // wide):
+        out_ref[tokens + k * rows : tokens + (k + 1) * rows] = w_ref[:, k * wide : (k + 1) * wide]
+
+
+def turn_kernel(a_ref, b_ref, c_ref, d_ref, p_ref, x_ref, out_ref, pe_ref, near_ref):
     pe_ref[...] = p_ref[...]
+    near_ref[...] = x_ref[...]
     rest = (a_ref[...] + b_ref[...]) + (c_ref[...] + d_ref[...])
     rest = rest.reshape(out_ref.shape[1], LANES)
     same = (iota((LANES, LANES), 0) == iota((LANES, LANES), 1)).astype(BF16)
@@ -133,19 +128,9 @@
     out_ref[...] = turned
 
 
-def pack_kernel(x_ref, w_ref, out_ref, sems):
+def merge_kernel(t_ref, got_ref, x_ref, pe_ref, et_ref, send_ref, cot_ref, turned_ref):
+    n_t, rows, _ = got_ref.shape
     tokens, wide = x_ref.shape
-    rows = w_ref.shape[0]
-    pairs = [(x_ref, out_ref.at[pl.ds(0, tokens)])]
-    for k in range(w_ref.shape[1] // wide):
-        pairs.append((w_ref.at[:, pl.ds(k * wide, wide)], out_ref.at[pl.ds(tokens + k * rows, rows)]))
-    for copy in fetch(pairs, sems):
-        copy.wait()
-
-
-def merge_kernel(t_ref, got_ref, xt_ref, pe_ref, et_ref, send_ref, cot_ref, turned_ref):
-    n_t, rows, _ = got_ref.shape
-    wide, tokens = xt_ref.shape
     n_r = send_ref.shape[0]
     group = LANES // n_r
     ff_win = n_t * rows
@@ -161,14 +146,16 @@
     p_pack = fold_rows(p4, rows // 4)
 
     own = wide // n_r
-    turned_ref[...] = nt(xt_ref[...], cot, None)
+    turned_ref[...] = lax.dot_general(
+        x_ref[...], cot, (((0,), (1,)), ((), ())), preferred_element_type=F32
+    )
     halves, width = lane_halves(ff_win)
     at = halves * (own // 4)
     for k in range(n_r):
         for h in range(halves):
             lanes = slice(h * width, (h + 1) * width)
             for g in range(own // 4):
-                row = k * own + 4 * g
+                row = 4 * g // group * LANES + k * group + 4 * g % group
                 send_ref[k, h * (own // 4) + g, :, :width] = turned_ref[row : row + 4, lanes]
             for g in range(group // 4):
                 row = k * group + 4 * g
@@ -373,48 +360,33 @@
         ],
     )(t, tokens_x, cotangent, q_prev)
     first, error_late, x_late = lax.optimization_barrier((first, error, tokens_x))
-    tiles = call(
+    *tiles, p_error = call(
         tiles_kernel,
-        [((n_t, rows, LANES), F32)] * 4,
-        [SMEM, HBM],
-        moved=2**20,
+        [((n_t, rows, LANES), F32)] * 4 + [((rows, rank), F32)],
+        [SMEM, HBM, HBM],
+        flops=2**27,
+        moved=3 * 2**20,
         limit=None,
-        scratch_shapes=[pltpu.VMEM(error.shape, F32), pltpu.SemaphoreType.DMA(())],
-    )(lax.axis_index("x")[None], error_late)
+        scratch_shapes=[
+            pltpu.VMEM(error.shape, F32),
+            pltpu.VMEM(q_prev.shape, F32),
+            pltpu.SemaphoreType.DMA((2,)),
+        ],
+    )(lax.axis_index("x")[None], error_late, q_prev)
     tiles = [tiles[0]] + [
         lax.ppermute(tiles[d], "x", [(i, (i + d) % 4) for i in range(4)]) for d in range(1, 4)
     ]
-    x_t, p_error = call(
-        functools.partial(project_kernel, group),
-        [((wide, tokens), BF16), ((rows, rank), F32)],
-        [HBM] * 3,
-        flops=2**27,
-        moved=2 * 2**20,
-        limit=None,
-        scratch_shapes=[
-            pltpu.VMEM(tokens_x.shape, BF16),
-            pltpu.VMEM(error.shape, F32),
-            pltpu.VMEM(q_prev.shape, F32),
-            pltpu.SemaphoreType.DMA((3,)),
-        ],
-    )(x_late, error_late, q_prev)
-    error_t, x_t, p_error = call(
+    error_t, p_error, x_near = call(
         turn_kernel,
-        [((LANES, ff_win), F32), ((wide, tokens), BF16), ((rows, rank), F32)],
+        [((LANES, ff_win), F32), ((rows, rank), F32), (tokens_x.shape, BF16)],
         [VMEM] * 6,
         moved=2**20,
-    )(*tiles, x_t, p_error)
+    )(*tiles, p_error, x_late)
     (bulk,) = call(
-        pack_kernel,
-        [((tokens + rows * n_t, wide), BF16)],
-        [HBM] * 2,
-        [HBM],
-        moved=2**20,
-        limit=None,
-        scratch_shapes=[pltpu.SemaphoreType.DMA((1 + n_t,))],
+        pack_kernel, [((tokens + rows * n_t, wide), BF16)], [VMEM] * 2, moved=2**20
     )(x_late, weight)
     first = exchange(first, T)
-    first, error_t, x_t, p_error, bulk = lax.optimization_barrier((first, error_t, x_t, p_error, bulk))
+    first, error_t, p_error, x_near, bulk = lax.optimization_barrier((first, error_t, p_error, x_near, bulk))
     bulk = lax.all_gather(bulk, T)
     blocks_g, blocks_e = halves * own // 4, halves * group // 4
     second, cot_all = call(
@@ -423,7 +395,7 @@
         [SMEM] + [VMEM] * 4,
         moved=2 * 2**20,
         scratch_shapes=[pltpu.VMEM((wide, ff_win), F32)],
-    )(t, first, x_t, p_error, error_t)
+    )(t, first, x_near, p_error, error_t)
     second = exchange(second, R)
     total_t, third = call(
         sum_kernel,

time: 147 us -> 137 us (0.932)
  Pallas kernels: 34.3 us -> 19.8 us
  local copies, waits for them, and re-layouts: 2.92 us -> 4.77 us
  blocking collectives: 44.9 us -> 46.7 us
    pallas_call x4 -> x3, Pallas kernels: 18.5 us -> 3.96 us  [the longest x1 2.96 us: body(): call(tiles_kernel, [((n_t, rows, LANES), F32)] * 4 + [((rows, rank), F32)...]
    unnamed x12 -> x16, local copies, waits for them, and re-layouts: 2.52 us -> 4.37 us
    all_to_all x2, blocking collectives: 44.9 us -> 46.7 us  [exchange(): return lax.all_to_all(parts, axes, 0, 0, tiled=True)]
  transfers between devices with their start and end apart: 7 -> 7, of which waited for: 1 -> 2; matrix products, arithmetic and copies ran while one was open for 1% -> 1% of each run, Pallas kernels for 20% -> 11%
where the time goes in v10:
time: 137 us; the launch traced here: 136 us
  blocking collectives  46.7 us (34%)
  starting transfers between devices  36.3 us (26%)
  Pallas kernels  19.8 us (14%)
  between operations  14.3 us (10%)
  waiting for transfers between devices  14 us (10%)
  local copies, waits for them, and re-layouts  4.77 us (3%)
    all_to_all x2, blocking collectives, exchange(): return lax.all_to_all(parts, axes, 0, 0, tiled=True)  46.7 us
    all_to_all x2, starting transfers between devices, exchange(): return lax.all_to_all(parts, axes, 0, 0, tiled=True)  21.2 us
    all_to_all x2, waiting for transfers between devices, exchange(): return lax.all_to_all(parts, axes, 0, 0, tiled=True)  13.1 us
    ppermute x3, starting transfers between devices, body(): lax.ppermute(tiles[d], 'x', [(i, (i + d) % 4) for i in range(4)])  10.6 us
    ppermute x1, starting transfers between devices, body(): other = lax.ppermute(mine, 'core', [(0, 1), (1, 0)])  4.54 us
    unnamed x16, local copies, waits for them, and re-layouts  4.37 us
    pallas_call x1, Pallas kernels, body(): call(rows_kernel, [((rows, width), F32), ((tokens, wide), BF16)], [SMEM]...  3.91 us
    pallas_call x1, Pallas kernels, body(): call(functools.partial(factor_kernel, n_r), [((n_r * n_z, group, LANES),...  3.08 us
  transfers between devices with their start and end apart: 7, of which 2 were waited for; matrix products, arithmetic and copies ran while one was open for 1% of the time, Pallas kernels for 11%

profile of v10, /device:TPU:1, one launch (start us, length us, event | category | flops | bytes accessed | tf_op | source)
XLA Modules:
  0.0 136.4 jit_solution(9270863452100160681)
XLA Ops:
  7.2 2.1 %shard_map.93 = f32[16,16,384]{2,1,0:T(8,128)} custom-call(s32[1]{0:T(128)} %bitcast.t_ref, bf16[128,512]{1,0:T(8,128)(2,1)} %x_ref.3, bf16[16,128]{1,0:T(8,128)(2,1)} %c_ref.3, f32[32,8192]{1,0:T(8,128)} %q_ref.3), custom_call_target="tpu_custom_call" | custom-call | bytes 1048576 | tf_op jit(solution)/shard_map/pallas_call | solution.py:349
  9.3 11.8 %all-to-all-start = ((f32[16,16,384]{2,1,0:T(8,128)}), f32[16,16,384]{2,1,0:T(8,128)S(1)}, u32[]{:S(2)}, u32[]{:S(2)}) async-start(f32[16,16,384]{2,1,0:T(8,128)} %shard_map.93), calls=%async_computation | async-start | bytes 786432 | tf_op jit(solution)/shard_map/all_to_all | solution.py:29
  21.2 3.0 %shard_map.94 = (f32[16,16,128]{2,1,0:T(8,128)}, f32[16,16,128]{2,1,0:T(8,128)}, f32[16,16,128]{2,1,0:T(8,128)}, f32[16,16,128]{2,1,0:T(8,128)}, f32[16,32]{1,0:T(8,128)}) custom-call(s32[1]{0:T(128)} %bitcast.2.x_ref, f32[16,8192]{1,0:T(8,128)} %bitcast.17, f32[32,8192]{1,0:T(8,128)} %q_ref.3), custom_call_target="tpu_custom_call" | custom-call | flops 134217728 | bytes 3145728 | tf_op jit(solution)/shard_map/pallas_call | solution.py:363
  24.1 3.1 %collective-permute-start = (f32[16,16,128]{2,1,0:T(8,128)}, f32[16,16,128]{2,1,0:T(8,128)S(1)}, u32[]{:S(2)}, u32[]{:S(2)}) collective-permute-start(f32[16,16,128]{2,1,0:T(8,128)} %get-tuple-element.43), channel_id=1, source_target_pairs={{0,16},{16,32},{32,48},{48,0},{1,17},{17,33},{33,49},{49,1},{2,18}... | collective-permute-start | bytes 393224 | tf_op jit(solution)/shard_map/ppermute | solution.py:377
  27.3 4.4 %collective-permute-start.1 = (f32[16,16,128]{2,1,0:T(8,128)}, f32[16,16,128]{2,1,0:T(8,128)S(1)}, u32[]{:S(2)}, u32[]{:S(2)}) collective-permute-start(f32[16,16,128]{2,1,0:T(8,128)} %get-tuple-element.44), channel_id=1, source_target_pairs={{0,32},{16,48},{32,0},{48,16},{1,33},{17,49},{33,1},{49,17},{2,34}... | collective-permute-start | bytes 393224 | tf_op jit(solution)/shard_map/ppermute | solution.py:377
  31.6 3.1 %collective-permute-start.2 = (f32[16,16,128]{2,1,0:T(8,128)}, f32[16,16,128]{2,1,0:T(8,128)S(1)}, u32[]{:S(2)}, u32[]{:S(2)}) collective-permute-start(f32[16,16,128]{2,1,0:T(8,128)} %get-tuple-element.45), channel_id=1, source_target_pairs={{0,48},{16,0},{32,16},{48,32},{1,49},{17,1},{33,17},{49,33},{2,50}... | collective-permute-start | bytes 393224 | tf_op jit(solution)/shard_map/ppermute | solution.py:377
  34.7 0.9 copy-done.1
  35.6 0.9 copy-done.4
  36.6 0.8 shard_map.96
  37.3 0.8 collective-permute-done.2.d_ref
  38.2 0.9 copy-done.2
  39.1 0.9 copy-done.5
  40.0 0.7 copy-done.7
  40.7 0.2 shard_map.95
  40.9 0.7 shard_map.97
  41.6 28.2 %all_to_all.20.got_ref = f32[32,11,4,128]{3,2,1,0:T(4,128)S(1)} all-to-all(f32[32,11,4,128]{3,2,1,0:T(4,128)S(1)} %get-tuple-element.58), channel_id=1, replica_groups=mesh['y'=8,'x'=4,'z'=8,'core'=2] {'y','x'}, dimensions={0} | all-to-all | bytes 1441792 | tf_op jit(solution)/shard_map/all_to_all | solution.py:29
  69.9 1.5 %shard_map.99 = (f32[16,512]{1,0:T(8,128)S(1)}, f32[16,2,4,128]{3,2,1,0:T(4,128)S(1)}) custom-call(f32[32,11,4,128]{3,2,1,0:T(4,128)S(1)} %all_to_all.20.got_ref), custom_call_target="tpu_custom_call" | custom-call | bytes 1048576 | tf_op jit(solution)/shard_map/pallas_call | solution.py:400
  71.4 18.5 %all_to_all.21.pack_ref = f32[16,2,4,128]{3,2,1,0:T(4,128)S(1)} all-to-all(f32[16,2,4,128]{3,2,1,0:T(4,128)S(1)} %get-tuple-element.59), channel_id=1, replica_groups=mesh['y'=8,'x'=4,'z'=8,'core'=2] {'z','core'}, dimensions={0} | all-to-all | bytes 131072 | tf_op jit(solution)/shard_map/all_to_all | solution.py:29
  89.9 3.1 %shard_map.100 = (f32[256,4,128]{2,1,0:T(4,128)}, f32[32,32]{1,0:T(8,128)S(1)}, f32[32,32]{1,0:T(8,128)S(1)}) custom-call(f32[16,2,4,128]{3,2,1,0:T(4,128)S(1)} %all_to_all.21.pack_ref, f32[16,512]{1,0:T(8,128)S(1)} %get-tuple-element.60.total_ref), custom_call_target="tpu_custom_call" | custom-call | flops 536870912 | bytes 1048576 | tf_op jit(solution)/shard_map/pallas_call | solution.py:410
  93.0 9.3 %all-to-all-start.3 = ((f32[256,4,128]{2,1,0:T(4,128)}), f32[256,4,128]{2,1,0:T(4,128)S(1)}, u32[]{:S(2)}, u32[]{:S(2)}) async-start(f32[256,4,128]{2,1,0:T(4,128)} %get-tuple-element.61), calls=%async_computation.3 | async-start | bytes 1048576 | tf_op jit(solution)/shard_map/all_to_all | solution.py:29
  102.3 0.1 reshape_squeeze.3
  102.4 0.1 fusion.3
  102.6 0.1 tile.21.basis_ref
  102.7 0.1 fusion.1
  102.8 0.2 fusion.2
  103.0 0.2 tile.9
  103.2 0.1 fusion.weigh_ref
  103.3 3.9 %shard_map.98 = (f32[16,8192]{1,0:T(8,128)S(1)}, bf16[128,512]{1,0:T(8,128)(2,1)}) custom-call(s32[1]{0:T(128)} %bitcast.t_ref, bf16[16,128]{1,0:T(8,128)(2,1)S(1)} %copy-done.6, bf16[256,128]{1,0:T(8,128)(2,1)S(1)} %get-tuple-element.55.cot_ref, bf16[16,384,512]{2,1,0:T(8,128)(2,1)} %bitcast.22), custom_call_target="tpu_custom_call" | custom-call | flops 268435456 | bytes 8388608 | tf_op jit(solution)/shard_map/pallas_call | solution.py:419
  107.2 13.1 %all-to-all-done.3 = f32[256,4,128]{2,1,0:T(4,128)S(1)} async-done(((f32[256,4,128]{2,1,0:T(4,128)}), f32[256,4,128]{2,1,0:T(4,128)S(1)}, u32[]{:S(2)}, u32[]{:S(2)}) %all-to-all-start.3) | async-done | bytes 524320 | tf_op jit(solution)/shard_map/all_to_all | solution.py:29
  120.4 4.5 %collective-permute-start.3 = (f32[256,4,128]{2,1,0:T(4,128)S(1)}, f32[256,4,128]{2,1,0:T(4,128)S(1)}, u32[]{:S(2)}, u32[]{:S(2)}) collective-permute-start(f32[256,4,128]{2,1,0:T(4,128)S(1)} %all-to-all-done.3), channel_id=1, source_target_pairs={{0,1},{1,0},{2,3},{3,2},{4,5},{5,4},{6,7},{7,6},{8,9},{9,8},{10,11... | collective-permute-start | bytes 1572872 | tf_op jit(solution)/shard_map/ppermute | solution.py:435
  124.9 1.7 %shard_map.101 = (f32[32,8192]{1,0:T(8,128)}, f32[16,8192]{1,0:T(8,128)}, f32[8,16,512]{2,1,0:T(8,128)S(1)}, f32[128,128]{1,0:T(8,128)S(1)}) custom-call(s32[1]{0:T(128)} %bitcast.4.core_ref, f32[8,128,128]{2,1,0:T(8,128)S(1)} %bitcast.21, f32[16,128]{1,0:T(8,128)S(1)} %tile.21.basis_ref, f32[16,8192]{1,0:T(8,128)S(1)} %bitcast.18, ...), custom_call_target="tpu_custom_call" | custom-call | flops 1073741824 | bytes 3145728 | tf_op jit(solution)/shard_map/pallas_call | solution.py:444
  126.7 2.9 %shard_map.102 = (f32[32,8192]{1,0:T(8,128)}, f32[16,8192]{1,0:T(8,128)}, f32[16,8192]{1,0:T(8,128)}) custom-call(s32[1]{0:T(128)} %bitcast.4.core_ref, f32[8,128,128]{2,1,0:T(8,128)S(1)} %bitcast.20, f32[16,128]{1,0:T(8,128)S(1)} %tile.21.basis_ref, f32[16,8192]{1,0:T(8,128)S(1)} %bitcast.19, ...), custom_call_target="tpu_custom_call", output_to_operand_aliasing={{0}: (9, {}), {1}: (10, {})} | custom-call | flops 1073741824 | bytes 4194304 | tf_op jit(solution)/shard_map/pallas_call | solution.py:453
  (24 shorter events, 0.2 us)
Async XLA Ops:
  7.2 96.2 %copy-start.6 = (bf16[16,128]{1,0:T(8,128)(2,1)S(1)}, bf16[16,128]{1,0:T(8,128)(2,1)}, u32[]{:S(2)}) copy-start(bf16[16,128]{1,0:T(8,128)(2,1)} %c_ref.3) | copy-start | bytes 12292
  9.3 31.6 %all-to-all-start = ((f32[16,16,384]{2,1,0:T(8,128)}), f32[16,16,384]{2,1,0:T(8,128)S(1)}, u32[]{:S(2)}, u32[]{:S(2)}) async-start(f32[16,16,384]{2,1,0:T(8,128)} %shard_map.93), calls=%async_computation | async-start | bytes 786432 | tf_op jit(solution)/shard_map/all_to_all | solution.py:29
  21.1 82.2 %all-gather.3.cloned.1.call-start = ((), (), s32[]{:S(2)}) async-start(), calls=%async_computation.4 | async-start | bytes 6684672 | tf_op jit(solution)/shard_map/all_gather | solution.py:390
  24.1 13.2 %collective-permute-start = (f32[16,16,128]{2,1,0:T(8,128)}, f32[16,16,128]{2,1,0:T(8,128)S(1)}, u32[]{:S(2)}, u32[]{:S(2)}) collective-permute-start(f32[16,16,128]{2,1,0:T(8,128)} %get-tuple-element.43), channel_id=1, source_target_pairs={{0,16},{16,32},{32,48},{48,0},{1,17},{17,33},{33,49},{49,1},{2,18}... | collective-permute-start | bytes 393224 | tf_op jit(solution)/shard_map/ppermute | solution.py:377
  27.3 10.1 %collective-permute-start.1 = (f32[16,16,128]{2,1,0:T(8,128)}, f32[16,16,128]{2,1,0:T(8,128)S(1)}, u32[]{:S(2)}, u32[]{:S(2)}) collective-permute-start(f32[16,16,128]{2,1,0:T(8,128)} %get-tuple-element.44), channel_id=1, source_target_pairs={{0,32},{16,48},{32,0},{48,16},{1,33},{17,49},{33,1},{49,17},{2,34}... | collective-permute-start | bytes 393224 | tf_op jit(solution)/shard_map/ppermute | solution.py:377
  31.6 6.5 %collective-permute-start.2 = (f32[16,16,128]{2,1,0:T(8,128)}, f32[16,16,128]{2,1,0:T(8,128)S(1)}, u32[]{:S(2)}, u32[]{:S(2)}) collective-permute-start(f32[16,16,128]{2,1,0:T(8,128)} %get-tuple-element.45), channel_id=1, source_target_pairs={{0,48},{16,0},{32,16},{48,32},{1,49},{17,1},{33,17},{49,33},{2,50}... | collective-permute-start | bytes 393224 | tf_op jit(solution)/shard_map/ppermute | solution.py:377
  34.7 0.9 copy-start.1
  35.6 0.9 copy-start.4
  38.2 0.9 copy-start.2
  39.1 0.9 copy-start.5
  40.0 0.7 copy-start.7
  41.6 83.3 %copy-start = (f32[1,16,8192]{2,1,0:T(8,128)S(1)}, f32[1,16,8192]{2,1,0:T(8,128)}, u32[]{:S(2)}) copy-start(f32[1,16,8192]{2,1,0:T(8,128)} %param.9) | copy-start | bytes 1572868
  93.0 33.7 %copy-start.3 = (f32[16,8192]{1,0:T(8,128)S(1)}, f32[16,8192]{1,0:T(8,128)}, u32[]{:S(2)}) copy-start(f32[16,8192]{1,0:T(8,128)} %m_ref.1) | copy-start | bytes 1572868
  93.0 27.4 %all-to-all-start.3 = ((f32[256,4,128]{2,1,0:T(4,128)}), f32[256,4,128]{2,1,0:T(4,128)S(1)}, u32[]{:S(2)}, u32[]{:S(2)}) async-start(f32[256,4,128]{2,1,0:T(4,128)} %get-tuple-element.61), calls=%async_computation.3 | async-start | bytes 1048576 | tf_op jit(solution)/shard_map/all_to_all | solution.py:29
  120.4 6.3 %collective-permute-start.3 = (f32[256,4,128]{2,1,0:T(4,128)S(1)}, f32[256,4,128]{2,1,0:T(4,128)S(1)}, u32[]{:S(2)}, u32[]{:S(2)}) collective-permute-start(f32[256,4,128]{2,1,0:T(4,128)S(1)} %all-to-all-done.3), channel_id=1, source_target_pairs={{0,1},{1,0},{2,3},{3,2},{4,5},{5,4},{6,7},{7,6},{8,9},{9,8},{10,11... | collective-permute-start | bytes 1572872 | tf_op jit(solution)/shard_map/ppermute | solution.py:435
Sparse Core Ops, SparseCore 0:
  41.1 52.9 all-gather.2

commit v11 on v10

--- a/solution.py
+++ b/solution.py
@@ -106,7 +106,10 @@
     pe_ref[...] = nt(e[...], q[...])
 
 
-def pack_kernel(x_ref, w_ref, out_ref):
+def pack_kernel(x_ref, w_ref, a_ref, p_ref, out_ref, near_ref, tile_ref, pe_ref):
+    near_ref[...] = x_ref[...]
+    tile_ref[...] = a_ref[...]
+    pe_ref[...] = p_ref[...]
     tokens, wide = x_ref.shape
     rows = w_ref.shape[0]
     out_ref[:tokens] = x_ref[...]
@@ -114,9 +117,7 @@
         out_ref[tokens + k * rows : tokens + (k + 1) * rows] = w_ref[:, k * wide : (k + 1) * wide]
 
 
-def turn_kernel(a_ref, b_ref, c_ref, d_ref, p_ref, x_ref, out_ref, pe_ref, near_ref):
-    pe_ref[...] = p_ref[...]
-    near_ref[...] = x_ref[...]
+def turn_kernel(a_ref, b_ref, c_ref, d_ref, out_ref):
     rest = (a_ref[...] + b_ref[...]) + (c_ref[...] + d_ref[...])
     rest = rest.reshape(out_ref.shape[1], LANES)
     same = (iota((LANES, LANES), 0) == iota((LANES, LANES), 1)).astype(BF16)
@@ -195,12 +196,11 @@
         total += dot(scratch[h, :, :width], move)
     total_ref[...] = total
 
-    p8 = jnp.concatenate([p_pack, jnp.zeros_like(p_pack)], 0)
-    spread = (iota((rows, SUB), 0) % 4 == iota((rows, SUB), 1)).astype(F32)
-    p16 = dot(spread, p8)
-    p16 = jnp.where(iota(p16.shape, 0) // 4 == iota(p16.shape, 1) // 32, p16, 0.0)
-    square = (LANES, LANES)
-    p16 = dot(p16, (iota(square, 0) % 32 == iota(square, 1) % 32).astype(F32))
+    p16 = jnp.concatenate([p_pack] * (rows // 4), 0)
+    turns = [p16] + [pltpu.roll(p16, 32 * d, 1) for d in range(1, 4)]
+    ahead = (iota(p16.shape, 1) // 32 - iota(p16.shape, 0) // 4) % 4
+    for d in range(1, 4):
+        p16 = jnp.where(ahead == d, turns[d], p16)
     p_all = jnp.concatenate([p16] * n_t, 0)
     for b in range(4):
         part = sum(got_ref[r, at + 1 :] for r in range(b, n_r, 4))
@@ -208,26 +208,20 @@
             for g in range(group // 4):
                 row = b * group + 4 * g
                 error[row : row + 4, h * width : (h + 1) * width] = part[h * (group // 4) + g][:, :width]
-    pieces = []
     for q in range(n_t // 4):
         mask = iota(p_all.shape, 0) // rows == 4 * q + iota(p_all.shape, 1) // 32
         out = dot(error[...], jnp.where(mask, p_all, 0.0))
-        rolled = [out] + [pltpu.roll(out, 32 * d, 1) for d in range(1, 4)]
+        turns = [out] + [pltpu.roll(out, 32 * d, 1) for d in range(1, 4)]
         row, lane = iota(out.shape, 0) // group, iota(out.shape, 1) // 32
         for s in range(4):
             kept = jnp.zeros(out.shape, F32)
             for b in range(4):
-                kept = jnp.where((row == b) & (lane == b), rolled[(b - s) % 4], kept)
-            pieces.append(kept)
-    every = jnp.concatenate(pieces, 0)
-    tall = max(group, SUB)
-    pick_row, pick_col = iota((n_t * tall, n_t * own), 0), iota((n_t * tall, n_t * own), 1)
-    pick = (pick_row // tall == pick_col // own) & (pick_row % tall == pick_col % group)
-    folded = dot(pick.astype(F32), every)
+                kept = jnp.where((row == b) & (lane == b), turns[(b - s) % 4], kept)
+            kept = sum(kept[b * group : (b + 1) * group] for b in range(4))
+            for g in range(group // 4):
+                send_ref[4 * q + s, 1 + g] = kept[4 * g : 4 * g + 4]
     for k in range(n_t):
         send_ref[k, 0] = p_pack
-        for g in range(group // 4):
-            send_ref[k, 1 + g] = folded[k * tall + 4 * g : k * tall + 4 * g + 4]
 
 
 def factor_kernel(n_r, pack_ref, total_ref, send_ref, gram_ref, inverse_ref, held, wide):
@@ -373,18 +367,19 @@
             pltpu.SemaphoreType.DMA((2,)),
         ],
     )(lax.axis_index("x")[None], error_late, q_prev)
-    tiles = [tiles[0]] + [
-        lax.ppermute(tiles[d], "x", [(i, (i + d) % 4) for i in range(4)]) for d in range(1, 4)
-    ]
-    error_t, p_error, x_near = call(
-        turn_kernel,
-        [((LANES, ff_win), F32), ((rows, rank), F32), (tokens_x.shape, BF16)],
-        [VMEM] * 6,
+    moved = [lax.ppermute(tiles[d], "x", [(i, (i + d) % 4) for i in range(4)]) for d in (2, 1, 3)]
+    bulk, x_near, tile, p_error = call(
+        pack_kernel,
+        [
+            ((tokens + rows * n_t, wide), BF16),
+            (tokens_x.shape, BF16),
+            ((n_t, rows, LANES), F32),
+            ((rows, rank), F32),
+        ],
+        [VMEM] * 4,
         moved=2**20,
-    )(*tiles, p_error, x_late)
-    (bulk,) = call(
-        pack_kernel, [((tokens + rows * n_t, wide), BF16)], [VMEM] * 2, moved=2**20
-    )(x_late, weight)
+    )(x_late, weight, tiles[0], p_error)
+    (error_t,) = call(turn_kernel, [((LANES, ff_win), F32)], [VMEM] * 4, moved=2**20)(tile, *moved)
     first = exchange(first, T)
     first, error_t, p_error, x_near, bulk = lax.optimization_barrier((first, error_t, p_error, x_near, bulk))
     bulk = lax.all_gather(bulk, T)

time: 137 us -> 134 us (0.978)
    unnamed x16 -> x14, local copies, waits for them, and re-layouts: 4.37 us -> 3.46 us
  transfers between devices with their start and end apart: 7 -> 7, of which waited for: 2 -> 1; matrix products, arithmetic and copies ran while one was open for 1% -> 1% of each run, Pallas kernels for 11% -> 11%
where the time goes in v11:
time: 134 us
  blocking collectives  45.7 us (34%)
  starting transfers between devices  36.9 us (28%)
  Pallas kernels  19.2 us (14%)
  between operations  14.3 us (11%)
  waiting for transfers between devices  13.2 us (10%)
  local copies, waits for them, and re-layouts  3.86 us (3%)
    all_to_all x2, blocking collectives, exchange(): return lax.all_to_all(parts, axes, 0, 0, tiled=True)  45.7 us
    all_to_all x2, starting transfers between devices, exchange(): return lax.all_to_all(parts, axes, 0, 0, tiled=True)  21.2 us
    all_to_all x2, waiting for transfers between devices, exchange(): return lax.all_to_all(parts, axes, 0, 0, tiled=True)  13.2 us
    ppermute x3, starting transfers between devices, body(): lax.ppermute(tiles[d], 'x', [(i, (i + d) % 4) for i in range(4)])  11.2 us
    ppermute x1, starting transfers between devices, body(): other = lax.ppermute(mine, 'core', [(0, 1), (1, 0)])  4.44 us
    pallas_call x1, Pallas kernels, body(): call(rows_kernel, [((rows, width), F32), ((tokens, wide), BF16)], [SMEM]...  3.91 us
    unnamed x14, local copies, waits for them, and re-layouts  3.46 us
    pallas_call x1, Pallas kernels, body(): call(functools.partial(factor_kernel, n_r), [((n_r * n_z, group, LANES),...  3.08 us
  transfers between devices with their start and end apart: 7, of which 1 were waited for; matrix products, arithmetic and copies ran while one was open for 1% of the time, Pallas kernels for 11%

profile of v11, /device:TPU:1, one launch (start us, length us, event | category | flops | bytes accessed | tf_op | source)
XLA Modules:
  0.0 133.7 jit_solution(13724898018858866426)
XLA Ops:
  7.2 2.1 %shard_map.93 = f32[16,16,384]{2,1,0:T(8,128)} custom-call(s32[1]{0:T(128)} %bitcast.t_ref, bf16[128,512]{1,0:T(8,128)(2,1)} %x_ref.2, bf16[16,128]{1,0:T(8,128)(2,1)} %c_ref.3, f32[32,8192]{1,0:T(8,128)} %q_ref.3), custom_call_target="tpu_custom_call" | custom-call | bytes 1048576 | tf_op jit(solution)/shard_map/pallas_call | solution.py:343
  9.3 11.8 %all-to-all-start = ((f32[16,16,384]{2,1,0:T(8,128)}), f32[16,16,384]{2,1,0:T(8,128)S(1)}, u32[]{:S(2)}, u32[]{:S(2)}) async-start(f32[16,16,384]{2,1,0:T(8,128)} %shard_map.93), calls=%async_computation | async-start | bytes 786432 | tf_op jit(solution)/shard_map/all_to_all | solution.py:29
  21.1 0.0 all-gather.3.cloned.1.call-start
  21.2 3.0 %shard_map.94 = (f32[16,16,128]{2,1,0:T(8,128)}, f32[16,16,128]{2,1,0:T(8,128)}, f32[16,16,128]{2,1,0:T(8,128)}, f32[16,16,128]{2,1,0:T(8,128)}, f32[16,32]{1,0:T(8,128)}) custom-call(s32[1]{0:T(128)} %bitcast.2.x_ref, f32[16,8192]{1,0:T(8,128)} %bitcast.17, f32[32,8192]{1,0:T(8,128)} %q_ref.3), custom_call_target="tpu_custom_call" | custom-call | flops 134217728 | bytes 3145728 | tf_op jit(solution)/shard_map/pallas_call | solution.py:357
  24.1 4.7 %collective-permute-start = (f32[16,16,128]{2,1,0:T(8,128)}, f32[16,16,128]{2,1,0:T(8,128)S(1)}, u32[]{:S(2)}, u32[]{:S(2)}) collective-permute-start(f32[16,16,128]{2,1,0:T(8,128)} %get-tuple-element.47), channel_id=1, source_target_pairs={{0,32},{16,48},{32,0},{48,16},{1,33},{17,49},{33,1},{49,17},{2,34}... | collective-permute-start | bytes 393224 | tf_op jit(solution)/shard_map/ppermute | solution.py:370
  28.8 2.2 %collective-permute-start.1 = (f32[16,16,128]{2,1,0:T(8,128)}, f32[16,16,128]{2,1,0:T(8,128)S(1)}, u32[]{:S(2)}, u32[]{:S(2)}) collective-permute-start(f32[16,16,128]{2,1,0:T(8,128)} %get-tuple-element.48), channel_id=1, source_target_pairs={{0,16},{16,32},{32,48},{48,0},{1,17},{17,33},{33,49},{49,1},{2,18}... | collective-permute-start | bytes 393224 | tf_op jit(solution)/shard_map/ppermute | solution.py:370
  31.0 4.3 %collective-permute-start.2 = (f32[16,16,128]{2,1,0:T(8,128)}, f32[16,16,128]{2,1,0:T(8,128)S(1)}, u32[]{:S(2)}, u32[]{:S(2)}) collective-permute-start(f32[16,16,128]{2,1,0:T(8,128)} %get-tuple-element.49), channel_id=1, source_target_pairs={{0,48},{16,0},{32,16},{48,32},{1,49},{17,1},{33,17},{49,33},{2,50}... | collective-permute-start | bytes 393224 | tf_op jit(solution)/shard_map/ppermute | solution.py:370
  35.3 0.9 copy-done.2
  36.2 0.9 copy-done.3
  37.2 0.9 copy-done.4
  38.1 0.7 copy-done.6
  38.8 0.8 shard_map.95
  39.6 0.2 shard_map.96.et_ref
  39.9 0.7 shard_map.97
  40.6 27.2 %all_to_all.20.got_ref = f32[32,11,4,128]{3,2,1,0:T(4,128)S(1)} all-to-all(f32[32,11,4,128]{3,2,1,0:T(4,128)S(1)} %get-tuple-element.60), channel_id=1, replica_groups=mesh['y'=8,'x'=4,'z'=8,'core'=2] {'y','x'}, dimensions={0} | all-to-all | bytes 1441792 | tf_op jit(solution)/shard_map/all_to_all | solution.py:29
  67.7 0.9 shard_map.99
  68.6 18.5 %all_to_all.21.pack_ref = f32[16,2,4,128]{3,2,1,0:T(4,128)S(1)} all-to-all(f32[16,2,4,128]{3,2,1,0:T(4,128)S(1)} %get-tuple-element.61), channel_id=1, replica_groups=mesh['y'=8,'x'=4,'z'=8,'core'=2] {'z','core'}, dimensions={0} | all-to-all | bytes 131072 | tf_op jit(solution)/shard_map/all_to_all | solution.py:29
  87.2 3.1 %shard_map.100 = (f32[256,4,128]{2,1,0:T(4,128)}, f32[32,32]{1,0:T(8,128)S(1)}, f32[32,32]{1,0:T(8,128)S(1)}) custom-call(f32[16,2,4,128]{3,2,1,0:T(4,128)S(1)} %all_to_all.21.pack_ref, f32[16,512]{1,0:T(8,128)S(1)} %get-tuple-element.62.total_ref), custom_call_target="tpu_custom_call" | custom-call | flops 536870912 | bytes 1048576 | tf_op jit(solution)/shard_map/pallas_call | solution.py:405
  90.3 9.4 %all-to-all-start.3 = ((f32[256,4,128]{2,1,0:T(4,128)}), f32[256,4,128]{2,1,0:T(4,128)S(1)}, u32[]{:S(2)}, u32[]{:S(2)}) async-start(f32[256,4,128]{2,1,0:T(4,128)} %get-tuple-element.63), calls=%async_computation.3 | async-start | bytes 1048576 | tf_op jit(solution)/shard_map/all_to_all | solution.py:29
  99.7 0.1 reshape_squeeze.3
  99.8 0.1 fusion.3
  99.9 0.1 tile.21.basis_ref
  100.0 0.1 fusion.1
  100.1 0.2 fusion.2
  100.4 0.2 tile.9
  100.5 0.1 fusion.weigh_ref
  100.7 0.0 all-gather.3.cloned.1.call-done
  100.7 3.9 %shard_map.98 = (f32[16,8192]{1,0:T(8,128)S(1)}, bf16[128,512]{1,0:T(8,128)(2,1)}) custom-call(s32[1]{0:T(128)} %bitcast.t_ref, bf16[16,128]{1,0:T(8,128)(2,1)S(1)} %copy-done.5, bf16[256,128]{1,0:T(8,128)(2,1)S(1)} %get-tuple-element.57.cot_ref, bf16[16,384,512]{2,1,0:T(8,128)(2,1)} %bitcast.22), custom_call_target="tpu_custom_call" | custom-call | flops 268435456 | bytes 8388608 | tf_op jit(solution)/shard_map/pallas_call | solution.py:414
  104.6 13.2 %all-to-all-done.3 = f32[256,4,128]{2,1,0:T(4,128)S(1)} async-done(((f32[256,4,128]{2,1,0:T(4,128)}), f32[256,4,128]{2,1,0:T(4,128)S(1)}, u32[]{:S(2)}, u32[]{:S(2)}) %all-to-all-start.3) | async-done | bytes 524320 | tf_op jit(solution)/shard_map/all_to_all | solution.py:29
  117.8 4.4 %collective-permute-start.3 = (f32[256,4,128]{2,1,0:T(4,128)S(1)}, f32[256,4,128]{2,1,0:T(4,128)S(1)}, u32[]{:S(2)}, u32[]{:S(2)}) collective-permute-start(f32[256,4,128]{2,1,0:T(4,128)S(1)} %all-to-all-done.3), channel_id=1, source_target_pairs={{0,1},{1,0},{2,3},{3,2},{4,5},{5,4},{6,7},{7,6},{8,9},{9,8},{10,11... | collective-permute-start | bytes 1572872 | tf_op jit(solution)/shard_map/ppermute | solution.py:430
  122.2 1.7 %shard_map.101 = (f32[32,8192]{1,0:T(8,128)}, f32[16,8192]{1,0:T(8,128)}, f32[8,16,512]{2,1,0:T(8,128)S(1)}, f32[128,128]{1,0:T(8,128)S(1)}) custom-call(s32[1]{0:T(128)} %bitcast.4.core_ref, f32[8,128,128]{2,1,0:T(8,128)S(1)} %bitcast.21, f32[16,128]{1,0:T(8,128)S(1)} %tile.21.basis_ref, f32[16,8192]{1,0:T(8,128)S(1)} %bitcast.18, ...), custom_call_target="tpu_custom_call" | custom-call | flops 1073741824 | bytes 3145728 | tf_op jit(solution)/shard_map/pallas_call | solution.py:439
  123.9 2.8 %shard_map.102 = (f32[32,8192]{1,0:T(8,128)}, f32[16,8192]{1,0:T(8,128)}, f32[16,8192]{1,0:T(8,128)}) custom-call(s32[1]{0:T(128)} %bitcast.4.core_ref, f32[8,128,128]{2,1,0:T(8,128)S(1)} %bitcast.20, f32[16,128]{1,0:T(8,128)S(1)} %tile.21.basis_ref, f32[16,8192]{1,0:T(8,128)S(1)} %bitcast.19, ...), custom_call_target="tpu_custom_call", output_to_operand_aliasing={{0}: (9, {}), {1}: (10, {})} | custom-call | flops 1073741824 | bytes 4194304 | tf_op jit(solution)/shard_map/pallas_call | solution.py:448
  (22 shorter events, 0.1 us)
Async XLA Ops:
  7.2 93.5 %copy-start.5 = (bf16[16,128]{1,0:T(8,128)(2,1)S(1)}, bf16[16,128]{1,0:T(8,128)(2,1)}, u32[]{:S(2)}) copy-start(bf16[16,128]{1,0:T(8,128)(2,1)} %c_ref.3) | copy-start | bytes 12292
  9.3 30.6 %all-to-all-start = ((f32[16,16,384]{2,1,0:T(8,128)}), f32[16,16,384]{2,1,0:T(8,128)S(1)}, u32[]{:S(2)}, u32[]{:S(2)}) async-start(f32[16,16,384]{2,1,0:T(8,128)} %shard_map.93), calls=%async_computation | async-start | bytes 786432 | tf_op jit(solution)/shard_map/all_to_all | solution.py:29
  21.1 79.6 %all-gather.3.cloned.1.call-start = ((), (), s32[]{:S(2)}) async-start(), calls=%async_computation.4 | async-start | bytes 6684672 | tf_op jit(solution)/shard_map/all_gather | solution.py:385
  24.1 15.4 %collective-permute-start = (f32[16,16,128]{2,1,0:T(8,128)}, f32[16,16,128]{2,1,0:T(8,128)S(1)}, u32[]{:S(2)}, u32[]{:S(2)}) collective-permute-start(f32[16,16,128]{2,1,0:T(8,128)} %get-tuple-element.47), channel_id=1, source_target_pairs={{0,32},{16,48},{32,0},{48,16},{1,33},{17,49},{33,1},{49,17},{2,34}... | collective-permute-start | bytes 393224 | tf_op jit(solution)/shard_map/ppermute | solution.py:370
  28.8 10.8 %collective-permute-start.1 = (f32[16,16,128]{2,1,0:T(8,128)}, f32[16,16,128]{2,1,0:T(8,128)S(1)}, u32[]{:S(2)}, u32[]{:S(2)}) collective-permute-start(f32[16,16,128]{2,1,0:T(8,128)} %get-tuple-element.48), channel_id=1, source_target_pairs={{0,16},{16,32},{32,48},{48,0},{1,17},{17,33},{33,49},{49,1},{2,18}... | collective-permute-start | bytes 393224 | tf_op jit(solution)/shard_map/ppermute | solution.py:370
  31.0 8.5 %collective-permute-start.2 = (f32[16,16,128]{2,1,0:T(8,128)}, f32[16,16,128]{2,1,0:T(8,128)S(1)}, u32[]{:S(2)}, u32[]{:S(2)}) collective-permute-start(f32[16,16,128]{2,1,0:T(8,128)} %get-tuple-element.49), channel_id=1, source_target_pairs={{0,48},{16,0},{32,16},{48,32},{1,49},{17,1},{33,17},{49,33},{2,50}... | collective-permute-start | bytes 393224 | tf_op jit(solution)/shard_map/ppermute | solution.py:370
  35.3 0.9 copy-start.2
  36.2 0.9 copy-start.3
  37.2 0.9 copy-start.4
  38.1 0.7 copy-start.6
  40.5 81.7 %copy-start = (f32[1,16,8192]{2,1,0:T(8,128)S(1)}, f32[1,16,8192]{2,1,0:T(8,128)}, u32[]{:S(2)}) copy-start(f32[1,16,8192]{2,1,0:T(8,128)} %param.9) | copy-start | bytes 1572868
  90.3 33.7 %copy-start.1 = (f32[16,8192]{1,0:T(8,128)S(1)}, f32[16,8192]{1,0:T(8,128)}, u32[]{:S(2)}) copy-start(f32[16,8192]{1,0:T(8,128)} %m_ref.1) | copy-start | bytes 1572868
  90.3 27.5 %all-to-all-start.3 = ((f32[256,4,128]{2,1,0:T(4,128)}), f32[256,4,128]{2,1,0:T(4,128)S(1)}, u32[]{:S(2)}, u32[]{:S(2)}) async-start(f32[256,4,128]{2,1,0:T(4,128)} %get-tuple-element.63), calls=%async_computation.3 | async-start | bytes 1048576 | tf_op jit(solution)/shard_map/all_to_all | solution.py:29
  117.8 6.2 %collective-permute-start.3 = (f32[256,4,128]{2,1,0:T(4,128)S(1)}, f32[256,4,128]{2,1,0:T(4,128)S(1)}, u32[]{:S(2)}, u32[]{:S(2)}) collective-permute-start(f32[256,4,128]{2,1,0:T(4,128)S(1)} %all-to-all-done.3), channel_id=1, source_target_pairs={{0,1},{1,0},{2,3},{3,2},{4,5},{5,4},{6,7},{7,6},{8,9},{9,8},{10,11... | collective-permute-start | bytes 1572872 | tf_op jit(solution)/shard_map/ppermute | solution.py:430
Sparse Core Ops, SparseCore 0:
  40.0 52.0 all-gather.2

commit v12 on v11

--- a/solution.py
+++ b/solution.py
@@ -93,15 +93,15 @@
             send_ref[k, :, at : at + tokens] = y[g * rows : (g + 1) * rows]
 
 
-def tiles_kernel(x_ref, e_ref, q_ref, *refs):
-    outs, pe_ref, (e, q, sems) = refs[:4], refs[4], refs[5:]
-    n_t = outs[0].shape[0]
+def tiles_kernel(x_ref, e_ref, q_ref, keep_ref, send_ref, pe_ref, e, q, sems):
+    n_t = keep_ref.shape[1]
+    half = x_ref[0] % 2
     copies = fetch([(e_ref, e), (q_ref, q)], sems)
     copies[0].wait()
-    for d, out in enumerate(outs):
-        b = lax.rem(x_ref[0] + d, 4)
-        for k in range(n_t):
-            out[k] = e[:, pl.ds(pl.multiple_of((4 * k + b) * LANES, LANES), LANES)]
+    for ref, first in ((keep_ref, 2 * half), (send_ref, 2 - 2 * half)):
+        for m in range(2):
+            for k in range(n_t):
+                ref[m, k] = e[:, pl.ds(pl.multiple_of((4 * k + first + m) * LANES, LANES), LANES)]
     copies[1].wait()
     pe_ref[...] = nt(e[...], q[...])
 
@@ -117,16 +117,16 @@
         out_ref[tokens + k * rows : tokens + (k + 1) * rows] = w_ref[:, k * wide : (k + 1) * wide]
 
 
-def turn_kernel(a_ref, b_ref, c_ref, d_ref, out_ref):
-    rest = (a_ref[...] + b_ref[...]) + (c_ref[...] + d_ref[...])
-    rest = rest.reshape(out_ref.shape[1], LANES)
+def turn_kernel(a_ref, b_ref, out_ref):
     same = (iota((LANES, LANES), 0) == iota((LANES, LANES), 1)).astype(BF16)
-    turned = jnp.zeros(out_ref.shape, F32)
-    for _ in range(3):
-        piece = rest.astype(BF16)
-        turned += nt(same, piece, None)
-        rest -= piece.astype(F32)
-    out_ref[...] = turned
+    for m in range(2):
+        rest = (a_ref[m] + b_ref[m]).reshape(out_ref.shape[1], LANES)
+        turned = jnp.zeros((LANES, rest.shape[0]), F32)
+        for _ in range(3):
+            piece = rest.astype(BF16)
+            turned += nt(same, piece, None)
+            rest -= piece.astype(F32)
+        out_ref[m * LANES : (m + 1) * LANES] = turned
 
 
 def merge_kernel(t_ref, got_ref, x_ref, pe_ref, et_ref, send_ref, cot_ref, turned_ref):
@@ -158,9 +158,11 @@
             for g in range(own // 4):
                 row = 4 * g // group * LANES + k * group + 4 * g % group
                 send_ref[k, h * (own // 4) + g, :, :width] = turned_ref[row : row + 4, lanes]
-            for g in range(group // 4):
-                row = k * group + 4 * g
-                send_ref[k, at + 1 + h * (group // 4) + g, :, :width] = et_ref[row : row + 4, lanes]
+            for m in range(2):
+                for g in range(group // 4):
+                    row = m * LANES + k * group + 4 * g
+                    block = at + 1 + (m * halves + h) * (group // 4) + g
+                    send_ref[k, block, :, :width] = et_ref[row : row + 4, lanes]
         send_ref[k, at] = p_pack[:4]
 
 
@@ -203,7 +205,9 @@
         p16 = jnp.where(ahead == d, turns[d], p16)
     p_all = jnp.concatenate([p16] * n_t, 0)
     for b in range(4):
-        part = sum(got_ref[r, at + 1 :] for r in range(b, n_r, 4))
+        tiles = halves * (group // 4)
+        start = at + 1 + b % 2 * tiles
+        part = sum(got_ref[r, start : start + tiles] for r in range(b // 2, n_r, 2))
         for h in range(halves):
             for g in range(group // 4):
                 row = b * group + 4 * g
@@ -354,9 +358,9 @@
         ],
     )(t, tokens_x, cotangent, q_prev)
     first, error_late, x_late = lax.optimization_barrier((first, error, tokens_x))
-    *tiles, p_error = call(
+    kept, given, p_error = call(
         tiles_kernel,
-        [((n_t, rows, LANES), F32)] * 4 + [((rows, rank), F32)],
+        [((2, n_t, rows, LANES), F32)] * 2 + [((rows, rank), F32)],
         [SMEM, HBM, HBM],
         flops=2**27,
         moved=3 * 2**20,
@@ -367,23 +371,23 @@
             pltpu.SemaphoreType.DMA((2,)),
         ],
     )(lax.axis_index("x")[None], error_late, q_prev)
-    moved = [lax.ppermute(tiles[d], "x", [(i, (i + d) % 4) for i in range(4)]) for d in (2, 1, 3)]
-    bulk, x_near, tile, p_error = call(
+    moved = lax.ppermute(given, "x", [(i, i ^ 1) for i in range(4)])
+    bulk, x_near, kept, p_error = call(
         pack_kernel,
         [
             ((tokens + rows * n_t, wide), BF16),
             (tokens_x.shape, BF16),
-            ((n_t, rows, LANES), F32),
+            (kept.shape, F32),
             ((rows, rank), F32),
         ],
         [VMEM] * 4,
         moved=2**20,
-    )(x_late, weight, tiles[0], p_error)
-    (error_t,) = call(turn_kernel, [((LANES, ff_win), F32)], [VMEM] * 4, moved=2**20)(tile, *moved)
+    )(x_late, weight, kept, p_error)
+    (error_t,) = call(turn_kernel, [((2 * LANES, ff_win), F32)], [VMEM] * 2, moved=2**20)(kept, moved)
     first = exchange(first, T)
     first, error_t, p_error, x_near, bulk = lax.optimization_barrier((first, error_t, p_error, x_near, bulk))
     bulk = lax.all_gather(bulk, T)
-    blocks_g, blocks_e = halves * own // 4, halves * group // 4
+    blocks_g, blocks_e = halves * own // 4, halves * group // 2
     second, cot_all = call(
         merge_kernel,
         [((n_r, blocks_g + 1 + blocks_e, 4, LANES), F32), ((ff_win, tokens), BF16)],

time: 134 us -> 133 us (level)
  starting transfers between devices: 36.9 us -> 29.4 us
  waiting for transfers between devices: 13.2 us -> 16.8 us
  blocking collectives: 45.7 us -> 48.4 us
    ppermute x3 -> x1, starting transfers between devices: 11.2 us -> 3.14 us  [body(): moved = lax.ppermute(given, 'x', [(i, i ^ 1) for i in range(4)])]
    all_to_all x2, blocking collectives: 45.7 us -> 48.4 us  [exchange(): return lax.all_to_all(parts, axes, 0, 0, tiled=True)]
    ppermute x3 -> x1, waiting for transfers between devices: 0.01 us -> 2.52 us  [body(): moved = lax.ppermute(given, 'x', [(i, i ^ 1) for i in range(4)])]
  transfers between devices with their start and end apart: 7 -> 5, of which waited for: 1 -> 3; matrix products, arithmetic and copies ran while one was open for 1% -> 1% of each run, Pallas kernels for 11% -> 11%
where the time goes in v12:
time: 133 us
  blocking collectives  48.4 us (36%)
  starting transfers between devices  29.4 us (22%)
  Pallas kernels  19.3 us (15%)
  waiting for transfers between devices  16.8 us (13%)
  between operations  14.3 us (11%)
  local copies, waits for them, and re-layouts  3.91 us (3%)
    all_to_all x2, blocking collectives, exchange(): return lax.all_to_all(parts, axes, 0, 0, tiled=True)  48.4 us
    all_to_all x2, starting transfers between devices, exchange(): return lax.all_to_all(parts, axes, 0, 0, tiled=True)  21.4 us
    all_to_all x2, waiting for transfers between devices, exchange(): return lax.all_to_all(parts, axes, 0, 0, tiled=True)  14.3 us
    ppermute x1, starting transfers between devices, body(): other = lax.ppermute(mine, 'core', [(0, 1), (1, 0)])  4.82 us
    pallas_call x1, Pallas kernels, body(): call(rows_kernel, [((rows, width), F32), ((tokens, wide), BF16)], [SMEM]...  3.91 us
    unnamed x14, local copies, waits for them, and re-layouts  3.51 us
    ppermute x1, starting transfers between devices, body(): moved = lax.ppermute(given, 'x', [(i, i ^ 1) for i in range(4)])  3.14 us
    pallas_call x1, Pallas kernels, body(): call(functools.partial(factor_kernel, n_r), [((n_r * n_z, group, LANES),...  3.08 us
  transfers between devices with their start and end apart: 5, of which 3 were waited for; matrix products, arithmetic and copies ran while one was open for 1% of the time, Pallas kernels for 11%

profile of v12, /device:TPU:1, one launch (start us, length us, event | category | flops | bytes accessed | tf_op | source)
XLA Modules:
  0.0 132.7 jit_solution(7687223534487717891)
XLA Ops:
  7.2 2.1 %shard_map.93 = f32[16,16,384]{2,1,0:T(8,128)} custom-call(s32[1]{0:T(128)} %bitcast.t_ref, bf16[128,512]{1,0:T(8,128)(2,1)} %x_ref.2, bf16[16,128]{1,0:T(8,128)(2,1)} %c_ref.3, f32[32,8192]{1,0:T(8,128)} %q_ref.3), custom_call_target="tpu_custom_call" | custom-call | bytes 1048576 | tf_op jit(solution)/shard_map/pallas_call | solution.py:347
  9.3 11.8 %all-to-all-start = ((f32[16,16,384]{2,1,0:T(8,128)}), f32[16,16,384]{2,1,0:T(8,128)S(1)}, u32[]{:S(2)}, u32[]{:S(2)}) async-start(f32[16,16,384]{2,1,0:T(8,128)} %shard_map.93), calls=%async_computation | async-start | bytes 786432 | tf_op jit(solution)/shard_map/all_to_all | solution.py:29
  21.1 0.0 all-gather.3.cloned.1.call-start
  21.2 3.0 %shard_map.94 = (f32[2,16,16,128]{3,2,1,0:T(8,128)}, f32[2,16,16,128]{3,2,1,0:T(8,128)}, f32[16,32]{1,0:T(8,128)}) custom-call(s32[1]{0:T(128)} %bitcast.2.x_ref, f32[16,8192]{1,0:T(8,128)} %bitcast.17, f32[32,8192]{1,0:T(8,128)} %q_ref.3), custom_call_target="tpu_custom_call" | custom-call | flops 134217728 | bytes 3145728 | tf_op jit(solution)/shard_map/pallas_call | solution.py:361
  24.1 3.1 %collective-permute-start = (f32[2,16,16,128]{3,2,1,0:T(8,128)}, f32[2,16,16,128]{3,2,1,0:T(8,128)S(1)}, u32[]{:S(2)}, u32[]{:S(2)}) collective-permute-start(f32[2,16,16,128]{3,2,1,0:T(8,128)} %get-tuple-element.45), channel_id=1, source_target_pairs={{0,16},{16,0},{32,48},{48,32},{1,17},{17,1},{33,49},{49,33},{2,18}... | collective-permute-start | bytes 786440 | tf_op jit(solution)/shard_map/ppermute | solution.py:374
  27.3 0.9 copy-done.2
  28.2 0.9 copy-done.3
  29.1 0.9 copy-done.4
  30.1 0.7 copy-done.6
  30.8 0.8 shard_map.95
  31.6 2.5 %collective-permute-done.b_ref = f32[2,16,16,128]{3,2,1,0:T(8,128)S(1)} collective-permute-done((f32[2,16,16,128]{3,2,1,0:T(8,128)}, f32[2,16,16,128]{3,2,1,0:T(8,128)S(1)}, u32[]{:S(2)}, u32[]{:S(2)}) %collective-permute-start) | collective-permute-done | bytes 262176 | tf_op jit(solution)/shard_map/ppermute | solution.py:374
  34.1 0.3 shard_map.96.et_ref
  34.4 1.3 all-to-all-done.got_ref
  35.7 0.7 shard_map.97
  36.4 32.9 %all_to_all.20.got_ref = f32[32,13,4,128]{3,2,1,0:T(4,128)S(1)} all-to-all(f32[32,13,4,128]{3,2,1,0:T(4,128)S(1)} %get-tuple-element.56), channel_id=1, replica_groups=mesh['y'=8,'x'=4,'z'=8,'core'=2] {'y','x'}, dimensions={0} | all-to-all | bytes 1703936 | tf_op jit(solution)/shard_map/all_to_all | solution.py:29
  69.3 0.9 shard_map.99
  70.2 15.6 %all_to_all.21.pack_ref = f32[16,2,4,128]{3,2,1,0:T(4,128)S(1)} all-to-all(f32[16,2,4,128]{3,2,1,0:T(4,128)S(1)} %get-tuple-element.57), channel_id=1, replica_groups=mesh['y'=8,'x'=4,'z'=8,'core'=2] {'z','core'}, dimensions={0} | all-to-all | bytes 131072 | tf_op jit(solution)/shard_map/all_to_all | solution.py:29
  85.8 3.1 %shard_map.100 = (f32[256,4,128]{2,1,0:T(4,128)}, f32[32,32]{1,0:T(8,128)S(1)}, f32[32,32]{1,0:T(8,128)S(1)}) custom-call(f32[16,2,4,128]{3,2,1,0:T(4,128)S(1)} %all_to_all.21.pack_ref, f32[16,512]{1,0:T(8,128)S(1)} %get-tuple-element.58.total_ref), custom_call_target="tpu_custom_call" | custom-call | flops 536870912 | bytes 1048576 | tf_op jit(solution)/shard_map/pallas_call | solution.py:409
  88.9 9.6 %all-to-all-start.3 = ((f32[256,4,128]{2,1,0:T(4,128)}), f32[256,4,128]{2,1,0:T(4,128)S(1)}, u32[]{:S(2)}, u32[]{:S(2)}) async-start(f32[256,4,128]{2,1,0:T(4,128)} %get-tuple-element.59), calls=%async_computation.3 | async-start | bytes 1048576 | tf_op jit(solution)/shard_map/all_to_all | solution.py:29
  98.5 0.1 reshape_squeeze.3
  98.6 0.1 fusion.3
  98.7 0.1 tile.21.basis_ref
  98.8 0.1 fusion.1
  98.9 0.2 fusion.2
  99.2 0.2 tile.9
  99.3 0.1 fusion.weigh_ref
  99.4 0.0 all-gather.3.cloned.1.call-done
  99.5 3.9 %shard_map.98 = (f32[16,8192]{1,0:T(8,128)S(1)}, bf16[128,512]{1,0:T(8,128)(2,1)}) custom-call(s32[1]{0:T(128)} %bitcast.t_ref, bf16[16,128]{1,0:T(8,128)(2,1)S(1)} %copy-done.5, bf16[256,128]{1,0:T(8,128)(2,1)S(1)} %get-tuple-element.53.cot_ref, bf16[16,384,512]{2,1,0:T(8,128)(2,1)} %bitcast.22), custom_call_target="tpu_custom_call" | custom-call | flops 268435456 | bytes 8388608 | tf_op jit(solution)/shard_map/pallas_call | solution.py:418
  103.4 13.0 %all-to-all-done.3 = f32[256,4,128]{2,1,0:T(4,128)S(1)} async-done(((f32[256,4,128]{2,1,0:T(4,128)}), f32[256,4,128]{2,1,0:T(4,128)S(1)}, u32[]{:S(2)}, u32[]{:S(2)}) %all-to-all-start.3) | async-done | bytes 524320 | tf_op jit(solution)/shard_map/all_to_all | solution.py:29
  116.4 4.8 %collective-permute-start.1 = (f32[256,4,128]{2,1,0:T(4,128)S(1)}, f32[256,4,128]{2,1,0:T(4,128)S(1)}, u32[]{:S(2)}, u32[]{:S(2)}) collective-permute-start(f32[256,4,128]{2,1,0:T(4,128)S(1)} %all-to-all-done.3), channel_id=1, source_target_pairs={{0,1},{1,0},{2,3},{3,2},{4,5},{5,4},{6,7},{7,6},{8,9},{9,8},{10,11... | collective-permute-start | bytes 1572872 | tf_op jit(solution)/shard_map/ppermute | solution.py:434
  121.3 1.7 %shard_map.101 = (f32[32,8192]{1,0:T(8,128)}, f32[16,8192]{1,0:T(8,128)}, f32[8,16,512]{2,1,0:T(8,128)S(1)}, f32[128,128]{1,0:T(8,128)S(1)}) custom-call(s32[1]{0:T(128)} %bitcast.4.core_ref, f32[8,128,128]{2,1,0:T(8,128)S(1)} %bitcast.21, f32[16,128]{1,0:T(8,128)S(1)} %tile.21.basis_ref, f32[16,8192]{1,0:T(8,128)S(1)} %bitcast.18, ...), custom_call_target="tpu_custom_call" | custom-call | flops 1073741824 | bytes 3145728 | tf_op jit(solution)/shard_map/pallas_call | solution.py:443
  123.0 2.9 %shard_map.102 = (f32[32,8192]{1,0:T(8,128)}, f32[16,8192]{1,0:T(8,128)}, f32[16,8192]{1,0:T(8,128)}) custom-call(s32[1]{0:T(128)} %bitcast.4.core_ref, f32[8,128,128]{2,1,0:T(8,128)S(1)} %bitcast.20, f32[16,128]{1,0:T(8,128)S(1)} %tile.21.basis_ref, f32[16,8192]{1,0:T(8,128)S(1)} %bitcast.19, ...), custom_call_target="tpu_custom_call", output_to_operand_aliasing={{0}: (9, {}), {1}: (10, {})} | custom-call | flops 1073741824 | bytes 4194304 | tf_op jit(solution)/shard_map/pallas_call | solution.py:452
  (18 shorter events, 0.1 us)
Async XLA Ops:
  7.2 92.3 %copy-start.5 = (bf16[16,128]{1,0:T(8,128)(2,1)S(1)}, bf16[16,128]{1,0:T(8,128)(2,1)}, u32[]{:S(2)}) copy-start(bf16[16,128]{1,0:T(8,128)(2,1)} %c_ref.3) | copy-start | bytes 12292
  9.3 26.4 %all-to-all-start = ((f32[16,16,384]{2,1,0:T(8,128)}), f32[16,16,384]{2,1,0:T(8,128)S(1)}, u32[]{:S(2)}, u32[]{:S(2)}) async-start(f32[16,16,384]{2,1,0:T(8,128)} %shard_map.93), calls=%async_computation | async-start | bytes 786432 | tf_op jit(solution)/shard_map/all_to_all | solution.py:29
  21.1 78.4 %all-gather.3.cloned.1.call-start = ((), (), s32[]{:S(2)}) async-start(), calls=%async_computation.4 | async-start | bytes 6684672 | tf_op jit(solution)/shard_map/all_gather | solution.py:389
  24.1 10.0 %collective-permute-start = (f32[2,16,16,128]{3,2,1,0:T(8,128)}, f32[2,16,16,128]{3,2,1,0:T(8,128)S(1)}, u32[]{:S(2)}, u32[]{:S(2)}) collective-permute-start(f32[2,16,16,128]{3,2,1,0:T(8,128)} %get-tuple-element.45), channel_id=1, source_target_pairs={{0,16},{16,0},{32,48},{48,32},{1,17},{17,1},{33,49},{49,33},{2,18}... | collective-permute-start | bytes 786440 | tf_op jit(solution)/shard_map/ppermute | solution.py:374
  27.3 0.9 copy-start.2
  28.2 0.9 copy-start.3
  29.1 0.9 copy-start.4
  30.1 0.7 copy-start.6
  36.4 84.9 %copy-start = (f32[1,16,8192]{2,1,0:T(8,128)S(1)}, f32[1,16,8192]{2,1,0:T(8,128)}, u32[]{:S(2)}) copy-start(f32[1,16,8192]{2,1,0:T(8,128)} %param.9) | copy-start | bytes 1572868
  88.8 34.1 %copy-start.1 = (f32[16,8192]{1,0:T(8,128)S(1)}, f32[16,8192]{1,0:T(8,128)}, u32[]{:S(2)}) copy-start(f32[16,8192]{1,0:T(8,128)} %m_ref.1) | copy-start | bytes 1572868
  88.9 27.6 %all-to-all-start.3 = ((f32[256,4,128]{2,1,0:T(4,128)}), f32[256,4,128]{2,1,0:T(4,128)S(1)}, u32[]{:S(2)}, u32[]{:S(2)}) async-start(f32[256,4,128]{2,1,0:T(4,128)} %get-tuple-element.59), calls=%async_computation.3 | async-start | bytes 1048576 | tf_op jit(solution)/shard_map/all_to_all | solution.py:29
  116.4 6.5 %collective-permute-start.1 = (f32[256,4,128]{2,1,0:T(4,128)S(1)}, f32[256,4,128]{2,1,0:T(4,128)S(1)}, u32[]{:S(2)}, u32[]{:S(2)}) collective-permute-start(f32[256,4,128]{2,1,0:T(4,128)S(1)} %all-to-all-done.3), channel_id=1, source_target_pairs={{0,1},{1,0},{2,3},{3,2},{4,5},{5,4},{6,7},{7,6},{8,9},{9,8},{10,11... | collective-permute-start | bytes 1572872 | tf_op jit(solution)/shard_map/ppermute | solution.py:434
Sparse Core Ops, SparseCore 0:
  35.8 51.4 all-gather.2

commit v13 on v12

--- a/solution.py
+++ b/solution.py
@@ -93,16 +93,21 @@
             send_ref[k, :, at : at + tokens] = y[g * rows : (g + 1) * rows]
 
 
-def tiles_kernel(x_ref, e_ref, q_ref, keep_ref, send_ref, pe_ref, e, q, sems):
+def tiles_kernel(x_ref, e_ref, keep_ref, send_ref, e, sem):
     n_t = keep_ref.shape[1]
     half = x_ref[0] % 2
-    copies = fetch([(e_ref, e), (q_ref, q)], sems)
-    copies[0].wait()
+    copy = pltpu.make_async_copy(e_ref, e, sem)
+    copy.start()
+    copy.wait()
     for ref, first in ((keep_ref, 2 * half), (send_ref, 2 - 2 * half)):
         for m in range(2):
             for k in range(n_t):
                 ref[m, k] = e[:, pl.ds(pl.multiple_of((4 * k + first + m) * LANES, LANES), LANES)]
-    copies[1].wait()
+
+
+def project_kernel(e_ref, q_ref, pe_ref, e, q, sems):
+    for copy in fetch([(e_ref, e), (q_ref, q)], sems):
+        copy.wait()
     pe_ref[...] = nt(e[...], q[...])
 
 
@@ -244,13 +249,13 @@
     row, lane = iota((rank, LANES), 0), iota((rank, LANES), 1)
     work = jnp.concatenate([gram, jnp.zeros((rank, LANES - rank), F32)], 1)
     work = jnp.where(lane == row + rank, 1.0, work)
-    for first in range(0, rank, 4):
-        columns = [jnp.broadcast_to(work[:, first + m : first + m + 1], work.shape) for m in range(4)]
-        for m in range(4):
+    for first in range(0, rank, 8):
+        columns = [jnp.broadcast_to(work[:, first + m : first + m + 1], work.shape) for m in range(8)]
+        for m in range(8):
             j = first + m
             factor = jnp.where(row > j, columns[m] * (1.0 / columns[m][j : j + 1, :]), 0.0)
             work -= factor * work[j : j + 1, :]
-            for n in range(m + 1, 4):
+            for n in range(m + 1, 8):
                 columns[n] -= factor * columns[n][j : j + 1, :]
     diagonal = jnp.sum(jnp.where(lane == row, work, 0.0), 1, keepdims=True)
     inverse = (work * lax.rsqrt(diagonal))[:, rank : 2 * rank]
@@ -316,7 +321,7 @@
         copy.wait()
 
 
-def far_kernel(limit, core_ref, other_ref, basis_ref, e_ref, g_ref, gram_ref, approx_ref, weigh_ref, m_ref, q_old, error_old, q_hbm, error_hbm, momentum_ref, q, error, sems, far):
+def far_kernel(limit, core_ref, other_ref, basis_ref, e_ref, g_ref, gram_ref, approx_ref, weigh_ref, m_ref, q_old, error_old, q_hbm, error_hbm, momentum_hbm, q, error, sems, far, out, out_sems):
     core = core_ref[0]
     gram, copies = place_blocks(
         1 - core, other_ref, basis_ref, e_ref, g_ref, q_hbm, error_hbm, q, error, sems, far, gram_ref[...]
@@ -324,9 +329,11 @@
     total = jnp.sum(gram * weigh_ref[...], keepdims=True)
     scale = jnp.minimum(1.0, limit / jnp.sqrt(total))
     for z in range(other_ref.shape[0]):
-        for ref, c in ((approx_ref, core), (far, 1 - core)):
+        for i, ref, c in ((0, approx_ref, core), (1, far, 1 - core)):
             at = pl.ds(pl.multiple_of((2 * z + c) * 4 * LANES, 4 * LANES), 4 * LANES)
-            momentum_ref[:, at] = BETA * m_ref[:, at] + scale * ref[z]
+            out[i, z] = BETA * m_ref[:, at] + scale * ref[z]
+            copies.append(pltpu.make_async_copy(out.at[i, z], momentum_hbm.at[:, at], out_sems.at[i, z]))
+            copies[-1].start()
     for copy in copies:
         copy.wait()
 
@@ -358,20 +365,29 @@
         ],
     )(t, tokens_x, cotangent, q_prev)
     first, error_late, x_late = lax.optimization_barrier((first, error, tokens_x))
-    kept, given, p_error = call(
+    kept, given = call(
         tiles_kernel,
-        [((2, n_t, rows, LANES), F32)] * 2 + [((rows, rank), F32)],
-        [SMEM, HBM, HBM],
+        [((2, n_t, rows, LANES), F32)] * 2,
+        [SMEM, HBM],
+        moved=2 * 2**20,
+        limit=None,
+        scratch_shapes=[pltpu.VMEM(error.shape, F32), pltpu.SemaphoreType.DMA(())],
+    )(lax.axis_index("x")[None], error_late)
+    kept, given, error_late = lax.optimization_barrier((kept, given, error_late))
+    moved = lax.ppermute(given, "x", [(i, i ^ 1) for i in range(4)])
+    (p_error,) = call(
+        project_kernel,
+        [((rows, rank), F32)],
+        [HBM, HBM],
         flops=2**27,
-        moved=3 * 2**20,
+        moved=2 * 2**20,
         limit=None,
         scratch_shapes=[
             pltpu.VMEM(error.shape, F32),
             pltpu.VMEM(q_prev.shape, F32),
             pltpu.SemaphoreType.DMA((2,)),
         ],
-    )(lax.axis_index("x")[None], error_late, q_prev)
-    moved = lax.ppermute(given, "x", [(i, i ^ 1) for i in range(4)])
+    )(error_late, q_prev)
     bulk, x_near, kept, p_error = call(
         pack_kernel,
         [
@@ -453,10 +469,15 @@
         functools.partial(far_kernel, limit),
         [*whole, ((rows, width), F32)],
         [SMEM] + [VMEM] * 8 + [HBM, HBM],
-        [HBM, HBM, VMEM],
+        [HBM] * 3,
         flops=2**30,
         moved=4 * 2**20,
-        scratch_shapes=[*scratch, pltpu.VMEM((n_z, rows, wide), F32)],
+        scratch_shapes=[
+            *scratch,
+            pltpu.VMEM((n_z, rows, wide), F32),
+            pltpu.VMEM((2, n_z, rows, wide), F32),
+            pltpu.SemaphoreType.DMA((2, n_z)),
+        ],
         input_output_aliases={9: 0, 10: 1},
     )(core, other.reshape(blocks), basis4, error, grad_rows, q_gram, approx, weigh, momentum, q_new, error_new)
     return (input_grad, error_new[None], momentum_new, q_new)

time: 133 us -> 132 us (level)
  waiting for transfers between devices: 16.8 us -> 15.1 us
    ppermute x1, waiting for transfers between devices: 2.52 us -> 0.01 us  [body(): moved = lax.ppermute(given, 'x', [(i, i ^ 1) for i in range(4)])]
    pallas_call x1 -> x2, Pallas kernels: 2.96 us -> 4.88 us  [the longest x1 2.96 us: body(): call(project_kernel, [((rows, rank), F32)], [HBM, HBM], flops=2 ** 27, mo...]
  transfers between devices with their start and end apart: 5 -> 5, of which waited for: 3 -> 2; matrix products, arithmetic and copies ran while one was open for 1% -> 1% of each run, Pallas kernels for 11% -> 12%
where the time goes in v13:
time: 132 us; the launch traced here: 131 us
  blocking collectives  47.9 us (36%)
  starting transfers between devices  29.1 us (22%)
  Pallas kernels  20.4 us (15%)
  waiting for transfers between devices  15.1 us (11%)
  between operations  14.3 us (11%)
  local copies, waits for them, and re-layouts  3.91 us (3%)
    all_to_all x2, blocking collectives, exchange(): return lax.all_to_all(parts, axes, 0, 0, tiled=True)  47.9 us
    all_to_all x2, starting transfers between devices, exchange(): return lax.all_to_all(parts, axes, 0, 0, tiled=True)  21.5 us
    all_to_all x2, waiting for transfers between devices, exchange(): return lax.all_to_all(parts, axes, 0, 0, tiled=True)  15.1 us
    ppermute x1, starting transfers between devices, body(): other = lax.ppermute(mine, 'core', [(0, 1), (1, 0)])  4.38 us
    pallas_call x1, Pallas kernels, body(): call(rows_kernel, [((rows, width), F32), ((tokens, wide), BF16)], [SMEM]...  3.91 us
    unnamed x14, local copies, waits for them, and re-layouts  3.51 us
    ppermute x1, starting transfers between devices, body(): moved = lax.ppermute(given, 'x', [(i, i ^ 1) for i in range(4)])  3.14 us
    pallas_call x1, Pallas kernels, body(): call(project_kernel, [((rows, rank), F32)], [HBM, HBM], flops=2 ** 27, mo...  2.96 us
  transfers between devices with their start and end apart: 5, of which 2 were waited for; matrix products, arithmetic and copies ran while one was open for 1% of the time, Pallas kernels for 12%

profile of v13, /device:TPU:1, one launch (start us, length us, event | category | flops | bytes accessed | tf_op | source)
XLA Modules:
  0.0 131.2 jit_solution(261142298524506968)
XLA Ops:
  7.2 2.1 %shard_map.93 = f32[16,16,384]{2,1,0:T(8,128)} custom-call(s32[1]{0:T(128)} %bitcast.t_ref, bf16[128,512]{1,0:T(8,128)(2,1)} %x_ref.2, bf16[16,128]{1,0:T(8,128)(2,1)} %c_ref.3, f32[32,8192]{1,0:T(8,128)} %q_ref.3), custom_call_target="tpu_custom_call" | custom-call | bytes 1048576 | tf_op jit(solution)/shard_map/pallas_call | solution.py:354
  9.3 11.8 %all-to-all-start = ((f32[16,16,384]{2,1,0:T(8,128)}), f32[16,16,384]{2,1,0:T(8,128)S(1)}, u32[]{:S(2)}, u32[]{:S(2)}) async-start(f32[16,16,384]{2,1,0:T(8,128)} %shard_map.93), calls=%async_computation | async-start | bytes 786432 | tf_op jit(solution)/shard_map/all_to_all | solution.py:29
  21.1 0.0 all-gather.3.cloned.1.call-start
  21.2 1.9 %shard_map.94 = (f32[2,16,16,128]{3,2,1,0:T(8,128)}, f32[2,16,16,128]{3,2,1,0:T(8,128)}) custom-call(s32[1]{0:T(128)} %bitcast.2.x_ref, f32[16,8192]{1,0:T(8,128)} %bitcast.17), custom_call_target="tpu_custom_call" | custom-call | bytes 2097152 | tf_op jit(solution)/shard_map/pallas_call | solution.py:368
  23.1 3.1 %collective-permute-start = (f32[2,16,16,128]{3,2,1,0:T(8,128)}, f32[2,16,16,128]{3,2,1,0:T(8,128)S(1)}, u32[]{:S(2)}, u32[]{:S(2)}) collective-permute-start(f32[2,16,16,128]{3,2,1,0:T(8,128)} %get-tuple-element.49), channel_id=1, source_target_pairs={{0,16},{16,0},{32,48},{48,32},{1,17},{17,1},{33,49},{49,33},{2,18}... | collective-permute-start | bytes 786440 | tf_op jit(solution)/shard_map/ppermute | solution.py:377
  26.2 3.0 %shard_map.95.p_ref = f32[16,32]{1,0:T(8,128)} custom-call(f32[16,8192]{1,0:T(8,128)} %bitcast.18, f32[32,8192]{1,0:T(8,128)} %q_ref.3), custom_call_target="tpu_custom_call" | custom-call | flops 134217728 | bytes 2097152 | tf_op jit(solution)/shard_map/pallas_call | solution.py:378
  29.2 0.9 copy-done.2
  30.1 0.9 copy-done.3
  31.1 0.9 copy-done.4
  32.0 0.7 copy-done.5
  32.7 0.8 shard_map.96
  33.5 0.3 shard_map.97.et_ref
  33.8 1.9 %all-to-all-done.got_ref = f32[16,16,384]{2,1,0:T(8,128)S(1)} async-done(((f32[16,16,384]{2,1,0:T(8,128)}), f32[16,16,384]{2,1,0:T(8,128)S(1)}, u32[]{:S(2)}, u32[]{:S(2)}) %all-to-all-start) | async-done | bytes 393248 | tf_op jit(solution)/shard_map/all_to_all | solution.py:29
  35.7 0.7 shard_map.98
  36.4 33.7 %all_to_all.20.got_ref = f32[32,13,4,128]{3,2,1,0:T(4,128)S(1)} all-to-all(f32[32,13,4,128]{3,2,1,0:T(4,128)S(1)} %get-tuple-element.60), channel_id=1, replica_groups=mesh['y'=8,'x'=4,'z'=8,'core'=2] {'y','x'}, dimensions={0} | all-to-all | bytes 1703936 | tf_op jit(solution)/shard_map/all_to_all | solution.py:29
  70.1 0.9 shard_map.100
  71.1 14.1 %all_to_all.21.pack_ref = f32[16,2,4,128]{3,2,1,0:T(4,128)S(1)} all-to-all(f32[16,2,4,128]{3,2,1,0:T(4,128)S(1)} %get-tuple-element.61), channel_id=1, replica_groups=mesh['y'=8,'x'=4,'z'=8,'core'=2] {'z','core'}, dimensions={0} | all-to-all | bytes 131072 | tf_op jit(solution)/shard_map/all_to_all | solution.py:29
  85.2 2.6 %shard_map.101 = (f32[256,4,128]{2,1,0:T(4,128)}, f32[32,32]{1,0:T(8,128)S(1)}, f32[32,32]{1,0:T(8,128)S(1)}) custom-call(f32[16,2,4,128]{3,2,1,0:T(4,128)S(1)} %all_to_all.21.pack_ref, f32[16,512]{1,0:T(8,128)S(1)} %get-tuple-element.62.total_ref), custom_call_target="tpu_custom_call" | custom-call | flops 536870912 | bytes 1048576 | tf_op jit(solution)/shard_map/pallas_call | solution.py:425
  87.8 9.7 %all-to-all-start.3 = ((f32[256,4,128]{2,1,0:T(4,128)}), f32[256,4,128]{2,1,0:T(4,128)S(1)}, u32[]{:S(2)}, u32[]{:S(2)}) async-start(f32[256,4,128]{2,1,0:T(4,128)} %get-tuple-element.63), calls=%async_computation.3 | async-start | bytes 1048576 | tf_op jit(solution)/shard_map/all_to_all | solution.py:29
  97.5 0.1 reshape_squeeze.3
  97.6 0.1 fusion.3
  97.8 0.1 tile.21.basis_ref
  97.9 0.1 fusion.1
  98.0 0.2 fusion.2
  98.2 0.2 tile.9
  98.4 0.1 fusion.weigh_ref
  98.5 0.0 all-gather.3.cloned.1.call-done
  98.6 3.9 %shard_map.99 = (f32[16,8192]{1,0:T(8,128)S(1)}, bf16[128,512]{1,0:T(8,128)(2,1)}) custom-call(s32[1]{0:T(128)} %bitcast.t_ref, bf16[16,128]{1,0:T(8,128)(2,1)S(1)} %copy-done.6, bf16[256,128]{1,0:T(8,128)(2,1)S(1)} %get-tuple-element.57.cot_ref, bf16[16,384,512]{2,1,0:T(8,128)(2,1)} %bitcast.23), custom_call_target="tpu_custom_call" | custom-call | flops 268435456 | bytes 8388608 | tf_op jit(solution)/shard_map/pallas_call | solution.py:434
  102.5 13.2 %all-to-all-done.3 = f32[256,4,128]{2,1,0:T(4,128)S(1)} async-done(((f32[256,4,128]{2,1,0:T(4,128)}), f32[256,4,128]{2,1,0:T(4,128)S(1)}, u32[]{:S(2)}, u32[]{:S(2)}) %all-to-all-start.3) | async-done | bytes 524320 | tf_op jit(solution)/shard_map/all_to_all | solution.py:29
  115.7 4.4 %collective-permute-start.1 = (f32[256,4,128]{2,1,0:T(4,128)S(1)}, f32[256,4,128]{2,1,0:T(4,128)S(1)}, u32[]{:S(2)}, u32[]{:S(2)}) collective-permute-start(f32[256,4,128]{2,1,0:T(4,128)S(1)} %all-to-all-done.3), channel_id=1, source_target_pairs={{0,1},{1,0},{2,3},{3,2},{4,5},{5,4},{6,7},{7,6},{8,9},{9,8},{10,11... | collective-permute-start | bytes 1572872 | tf_op jit(solution)/shard_map/ppermute | solution.py:450
  120.1 1.7 %shard_map.102 = (f32[32,8192]{1,0:T(8,128)}, f32[16,8192]{1,0:T(8,128)}, f32[8,16,512]{2,1,0:T(8,128)S(1)}, f32[128,128]{1,0:T(8,128)S(1)}) custom-call(s32[1]{0:T(128)} %bitcast.4.core_ref, f32[8,128,128]{2,1,0:T(8,128)S(1)} %bitcast.22, f32[16,128]{1,0:T(8,128)S(1)} %tile.21.basis_ref, f32[16,8192]{1,0:T(8,128)S(1)} %bitcast.19, ...), custom_call_target="tpu_custom_call" | custom-call | flops 1073741824 | bytes 3145728 | tf_op jit(solution)/shard_map/pallas_call | solution.py:459
  121.8 2.5 %shard_map.103 = (f32[32,8192]{1,0:T(8,128)}, f32[16,8192]{1,0:T(8,128)}, f32[16,8192]{1,0:T(8,128)}) custom-call(s32[1]{0:T(128)} %bitcast.4.core_ref, f32[8,128,128]{2,1,0:T(8,128)S(1)} %bitcast.21, f32[16,128]{1,0:T(8,128)S(1)} %tile.21.basis_ref, f32[16,8192]{1,0:T(8,128)S(1)} %bitcast.20, ...), custom_call_target="tpu_custom_call", output_to_operand_aliasing={{0}: (9, {}), {1}: (10, {})} | custom-call | flops 1073741824 | bytes 4194304 | tf_op jit(solution)/shard_map/pallas_call | solution.py:468
  (19 shorter events, 0.1 us)
Async XLA Ops:
  9.3 89.3 %copy-start.6 = (bf16[16,128]{1,0:T(8,128)(2,1)S(1)}, bf16[16,128]{1,0:T(8,128)(2,1)}, u32[]{:S(2)}) copy-start(bf16[16,128]{1,0:T(8,128)(2,1)} %c_ref.3) | copy-start | bytes 12292
  9.3 26.4 %all-to-all-start = ((f32[16,16,384]{2,1,0:T(8,128)}), f32[16,16,384]{2,1,0:T(8,128)S(1)}, u32[]{:S(2)}, u32[]{:S(2)}) async-start(f32[16,16,384]{2,1,0:T(8,128)} %shard_map.93), calls=%async_computation | async-start | bytes 786432 | tf_op jit(solution)/shard_map/all_to_all | solution.py:29
  21.1 77.4 %all-gather.3.cloned.1.call-start = ((), (), s32[]{:S(2)}) async-start(), calls=%async_computation.4 | async-start | bytes 6684672 | tf_op jit(solution)/shard_map/all_gather | solution.py:405
  23.1 10.4 %collective-permute-start = (f32[2,16,16,128]{3,2,1,0:T(8,128)}, f32[2,16,16,128]{3,2,1,0:T(8,128)S(1)}, u32[]{:S(2)}, u32[]{:S(2)}) collective-permute-start(f32[2,16,16,128]{3,2,1,0:T(8,128)} %get-tuple-element.49), channel_id=1, source_target_pairs={{0,16},{16,0},{32,48},{48,32},{1,17},{17,1},{33,49},{49,33},{2,18}... | collective-permute-start | bytes 786440 | tf_op jit(solution)/shard_map/ppermute | solution.py:377
  29.2 0.9 copy-start.2
  30.1 0.9 copy-start.3
  31.1 0.9 copy-start.4
  32.0 0.7 copy-start.5
  36.4 83.7 %copy-start = (f32[1,16,8192]{2,1,0:T(8,128)S(1)}, f32[1,16,8192]{2,1,0:T(8,128)}, u32[]{:S(2)}) copy-start(f32[1,16,8192]{2,1,0:T(8,128)} %param.9) | copy-start | bytes 1572868
  87.8 34.0 %copy-start.1 = (f32[16,8192]{1,0:T(8,128)S(1)}, f32[16,8192]{1,0:T(8,128)}, u32[]{:S(2)}) copy-start(f32[16,8192]{1,0:T(8,128)} %m_ref.1) | copy-start | bytes 1572868
  87.8 27.8 %all-to-all-start.3 = ((f32[256,4,128]{2,1,0:T(4,128)}), f32[256,4,128]{2,1,0:T(4,128)S(1)}, u32[]{:S(2)}, u32[]{:S(2)}) async-start(f32[256,4,128]{2,1,0:T(4,128)} %get-tuple-element.63), calls=%async_computation.3 | async-start | bytes 1048576 | tf_op jit(solution)/shard_map/all_to_all | solution.py:29
  115.7 6.1 %collective-permute-start.1 = (f32[256,4,128]{2,1,0:T(4,128)S(1)}, f32[256,4,128]{2,1,0:T(4,128)S(1)}, u32[]{:S(2)}, u32[]{:S(2)}) collective-permute-start(f32[256,4,128]{2,1,0:T(4,128)S(1)} %all-to-all-done.3), channel_id=1, source_target_pairs={{0,1},{1,0},{2,3},{3,2},{4,5},{5,4},{6,7},{7,6},{8,9},{9,8},{10,11... | collective-permute-start | bytes 1572872 | tf_op jit(solution)/shard_map/ppermute | solution.py:450
Sparse Core Ops, SparseCore 0:
  35.8 50.2 all-gather.2

commit v14 on v13

--- a/solution.py
+++ b/solution.py
@@ -18,7 +18,8 @@
 
 T = ("z", "core")
 R = ("y", "x")
-CHIPS = ("z", "y", "x")
+OWNERS = ("x", "y")
+CHIPS = ("z", *OWNERS)
 
 VMEM = pl.BlockSpec(memory_space=pltpu.VMEM)
 SMEM = pl.BlockSpec(memory_space=pltpu.SMEM)
@@ -84,7 +85,13 @@
     start = pl.multiple_of(t_ref[0] * wide, wide)
     for copy in fetch([(q_ref.at[:, pl.ds(start, wide)], q), (x_ref, x), (c_ref, c)], sems):
         copy.wait()
-    y = nt(q[...], x[...].astype(F32))
+    rest, pieces = q[...], []
+    for _ in range(3):
+        pieces.append(rest.astype(BF16))
+        rest -= pieces[-1].astype(F32)
+    rank = rest.shape[0]
+    y = nt(jnp.concatenate(pieces, 0), x[...], None)
+    y = y[:rank] + (y[rank : 2 * rank] + y[2 * rank :])
     cot = c[...].astype(F32)
     for k in range(n_t):
         send_ref[k, :, :tokens] = cot
@@ -212,7 +219,7 @@
     for b in range(4):
         tiles = halves * (group // 4)
         start = at + 1 + b % 2 * tiles
-        part = sum(got_ref[r, start : start + tiles] for r in range(b // 2, n_r, 2))
+        part = sum(got_ref[r, start : start + tiles] for r in range(n_r) if r // (n_r // 4) % 2 == b // 2)
         for h in range(halves):
             for g in range(group // 4):
                 row = b * group + 4 * g
@@ -233,11 +240,11 @@
         send_ref[k, 0] = p_pack
 
 
-def factor_kernel(n_r, pack_ref, total_ref, send_ref, gram_ref, inverse_ref, held, wide):
+def factor_kernel(n_r, pack_ref, total_ref, send_ref, inverse_ref, held, wide):
     wide[...] = jnp.zeros(wide.shape, F32)
     span = held.shape[0]
     own = total_ref.shape[0]
-    rank = gram_ref.shape[0]
+    rank = inverse_ref.shape[0]
     group = own // 4
     held[...] = jnp.zeros(held.shape, F32)
     for k in range(pack_ref.shape[0]):
@@ -245,7 +252,6 @@
     pack = held[...]
     gram4 = tn(pack, pack)
     gram = sum(gram4[b * rank : (b + 1) * rank, b * rank : (b + 1) * rank] for b in range(4))
-    gram_ref[...] = gram
     row, lane = iota((rank, LANES), 0), iota((rank, LANES), 1)
     work = jnp.concatenate([gram, jnp.zeros((rank, LANES - rank), F32)], 1)
     work = jnp.where(lane == row + rank, 1.0, work)
@@ -411,7 +417,7 @@
         moved=2 * 2**20,
         scratch_shapes=[pltpu.VMEM((wide, ff_win), F32)],
     )(t, first, x_near, p_error, error_t)
-    second = exchange(second, R)
+    second = exchange(second, OWNERS)
     total_t, third = call(
         sum_kernel,
         [((own, 2 * ff_win), F32), ((n_t, 1 + group // 4, 4, LANES), F32)],
@@ -422,9 +428,9 @@
     p_pack = third[0, 0]
     third = exchange(third, T)
 
-    q_send, gram, inverse = call(
+    q_send, inverse = call(
         functools.partial(factor_kernel, n_r),
-        [((n_r * n_z, group, LANES), F32), ((rank, rank), F32), ((rank, rank), F32)],
+        [((n_r * n_z, group, LANES), F32), ((rank, rank), F32)],
         [VMEM] * 2,
         flops=2**29,
         moved=2**20,
@@ -439,7 +445,8 @@
         moved=8 * 2**20,
         scratch_shapes=[pltpu.VMEM((ff_win, wide), BF16)],
     )(t, cotangent, cot_all, bulk)
-    basis_gram = dot(dot(inverse, gram), inverse.T)
+    basis = dot(third[:, 0].reshape(ff_win, rank), inverse.T)
+    basis_gram = tn(basis, basis)
     p_rows = p_pack.reshape(4, 4, rank).transpose(1, 0, 2).reshape(rows, rank)
     basis4 = jnp.tile(dot(p_rows, inverse.T), (1, 4))
     square = (LANES, LANES)

time: 132 us -> 134 us (1.015)
  blocking collectives: 47.9 us -> 33.4 us
  waiting for transfers between devices: 15.1 us -> 23.8 us
  starting transfers between devices: 29.1 us -> 35.4 us
    all_to_all x2 -> x1, blocking collectives: 47.9 us -> 33.4 us  [exchange(): return lax.all_to_all(parts, axes, 0, 0, tiled=True)]
    all_to_all x2 -> x3, waiting for transfers between devices: 15.1 us -> 23.8 us  [exchange(): return lax.all_to_all(parts, axes, 0, 0, tiled=True)]
    all_to_all x2 -> x3, starting transfers between devices: 21.5 us -> 27.7 us  [exchange(): return lax.all_to_all(parts, axes, 0, 0, tiled=True)]
  transfers between devices with their start and end apart: 5 -> 6, of which waited for: 2 -> 3; matrix products, arithmetic and copies ran while one was open for 1% -> 2% of each run, Pallas kernels for 12% -> 12%
where the time goes in v14:
time: 134 us; the launch traced here: 133 us
  starting transfers between devices  35.4 us (26%)
  blocking collectives  33.4 us (25%)
  waiting for transfers between devices  23.8 us (18%)
  Pallas kernels  20.9 us (16%)
  between operations  14.2 us (11%)
  local copies, waits for them, and re-layouts  4.7 us (4%)
    all_to_all x1, blocking collectives, exchange(): return lax.all_to_all(parts, axes, 0, 0, tiled=True)  33.4 us
    all_to_all x3, starting transfers between devices, exchange(): return lax.all_to_all(parts, axes, 0, 0, tiled=True)  27.7 us
    all_to_all x3, waiting for transfers between devices, exchange(): return lax.all_to_all(parts, axes, 0, 0, tiled=True)  23.8 us
    ppermute x1, starting transfers between devices, body(): other = lax.ppermute(mine, 'core', [(0, 1), (1, 0)])  4.51 us
    pallas_call x1, Pallas kernels, body(): call(rows_kernel, [((rows, width), F32), ((tokens, wide), BF16)], [SMEM]...  3.91 us
    unnamed x14, local copies, waits for them, and re-layouts  3.51 us
    ppermute x1, starting transfers between devices, body(): moved = lax.ppermute(given, 'x', [(i, i ^ 1) for i in range(4)])  3.15 us
    pallas_call x1, Pallas kernels, body(): call(project_kernel, [((rows, rank), F32)], [HBM, HBM], flops=2 ** 27, mo...  2.96 us
  transfers between devices with their start and end apart: 6, of which 3 were waited for; matrix products, arithmetic and copies ran while one was open for 2% of the time, Pallas kernels for 12%

profile of v14, /device:TPU:1, one launch (start us, length us, event | category | flops | bytes accessed | tf_op | source)
XLA Modules:
  0.0 133.3 jit_solution(4850664426261672618)
XLA Ops:
  7.2 1.9 %shard_map.93 = f32[16,16,384]{2,1,0:T(8,128)} custom-call(s32[1]{0:T(128)} %bitcast.t_ref, bf16[128,512]{1,0:T(8,128)(2,1)} %x_ref.2, bf16[16,128]{1,0:T(8,128)(2,1)} %c_ref.3, f32[32,8192]{1,0:T(8,128)} %q_ref.3), custom_call_target="tpu_custom_call" | custom-call | bytes 1048576 | tf_op jit(solution)/shard_map/pallas_call | solution.py:360
  9.1 11.8 %all-to-all-start = ((f32[16,16,384]{2,1,0:T(8,128)}), f32[16,16,384]{2,1,0:T(8,128)S(1)}, u32[]{:S(2)}, u32[]{:S(2)}) async-start(f32[16,16,384]{2,1,0:T(8,128)} %shard_map.93), calls=%async_computation | async-start | bytes 786432 | tf_op jit(solution)/shard_map/all_to_all | solution.py:30
  21.0 1.9 %shard_map.94 = (f32[2,16,16,128]{3,2,1,0:T(8,128)}, f32[2,16,16,128]{3,2,1,0:T(8,128)}) custom-call(s32[1]{0:T(128)} %bitcast.2.x_ref, f32[16,8192]{1,0:T(8,128)} %bitcast.17), custom_call_target="tpu_custom_call" | custom-call | bytes 2097152 | tf_op jit(solution)/shard_map/pallas_call | solution.py:374
  22.9 3.1 %collective-permute-start = (f32[2,16,16,128]{3,2,1,0:T(8,128)}, f32[2,16,16,128]{3,2,1,0:T(8,128)S(1)}, u32[]{:S(2)}, u32[]{:S(2)}) collective-permute-start(f32[2,16,16,128]{3,2,1,0:T(8,128)} %get-tuple-element.48), channel_id=1, source_target_pairs={{0,16},{16,0},{32,48},{48,32},{1,17},{17,1},{33,49},{49,33},{2,18}... | collective-permute-start | bytes 786440 | tf_op jit(solution)/shard_map/ppermute | solution.py:383
  26.1 3.0 %shard_map.95.p_ref = f32[16,32]{1,0:T(8,128)} custom-call(f32[16,8192]{1,0:T(8,128)} %bitcast.18, f32[32,8192]{1,0:T(8,128)} %q_ref.3), custom_call_target="tpu_custom_call" | custom-call | flops 134217728 | bytes 2097152 | tf_op jit(solution)/shard_map/pallas_call | solution.py:384
  29.1 0.9 copy-done.2
  30.0 0.9 copy-done.3
  30.9 0.9 copy-done.4
  31.9 0.7 copy-done.5
  32.5 0.8 shard_map.96
  33.3 0.3 shard_map.97.et_ref
  33.6 1.9 %all-to-all-done.got_ref = f32[16,16,384]{2,1,0:T(8,128)S(1)} async-done(((f32[16,16,384]{2,1,0:T(8,128)}), f32[16,16,384]{2,1,0:T(8,128)S(1)}, u32[]{:S(2)}, u32[]{:S(2)}) %all-to-all-start) | async-done | bytes 393248 | tf_op jit(solution)/shard_map/all_to_all | solution.py:30
  35.5 0.7 shard_map.98
  36.2 33.4 %all_to_all.20.got_ref = f32[32,13,4,128]{3,2,1,0:T(4,128)S(1)} all-to-all(f32[32,13,4,128]{3,2,1,0:T(4,128)S(1)} %get-tuple-element.59), channel_id=1, replica_groups=mesh['y'=8,'x'=4,'z'=8,'core'=2] {'x','y'}, dimensions={0} | all-to-all | bytes 1703936 | tf_op jit(solution)/shard_map/all_to_all | solution.py:30
  69.6 1.5 %shard_map.100 = (f32[16,512]{1,0:T(8,128)S(1)}, f32[16,2,4,128]{3,2,1,0:T(4,128)}) custom-call(f32[32,13,4,128]{3,2,1,0:T(4,128)S(1)} %all_to_all.20.got_ref), custom_call_target="tpu_custom_call" | custom-call | bytes 1048576 | tf_op jit(solution)/shard_map/pallas_call | solution.py:421
  71.1 6.6 %all-to-all-start.2 = ((f32[16,2,4,128]{3,2,1,0:T(4,128)}), f32[16,2,4,128]{3,2,1,0:T(4,128)S(1)}, u32[]{:S(2)}, u32[]{:S(2)}) async-start(f32[16,2,4,128]{3,2,1,0:T(4,128)} %get-tuple-element.60), calls=%async_computation.2 | async-start | bytes 131072 | tf_op jit(solution)/shard_map/all_to_all | solution.py:30
  77.7 8.4 %all-to-all-done.2.pack_ref = f32[16,2,4,128]{3,2,1,0:T(4,128)S(1)} async-done(((f32[16,2,4,128]{3,2,1,0:T(4,128)}), f32[16,2,4,128]{3,2,1,0:T(4,128)S(1)}, u32[]{:S(2)}, u32[]{:S(2)}) %all-to-all-start.2) | async-done | bytes 65568 | tf_op jit(solution)/shard_map/all_to_all | solution.py:30
  86.1 2.6 %shard_map.101 = (f32[256,4,128]{2,1,0:T(4,128)}, f32[32,32]{1,0:T(8,128)S(1)}) custom-call(f32[16,2,4,128]{3,2,1,0:T(4,128)S(1)} %all-to-all-done.2.pack_ref, f32[16,512]{1,0:T(8,128)S(1)} %get-tuple-element.61.total_ref), custom_call_target="tpu_custom_call" | custom-call | flops 536870912 | bytes 1048576 | tf_op jit(solution)/shard_map/pallas_call | solution.py:431
  88.7 9.3 %all-to-all-start.3 = ((f32[256,4,128]{2,1,0:T(4,128)}), f32[256,4,128]{2,1,0:T(4,128)S(1)}, u32[]{:S(2)}, u32[]{:S(2)}) async-start(f32[256,4,128]{2,1,0:T(4,128)} %get-tuple-element.62), calls=%async_computation.3 | async-start | bytes 1048576 | tf_op jit(solution)/shard_map/all_to_all | solution.py:30
  98.0 0.7 slice.7
  98.7 0.1 reshape_squeeze.7
  98.8 0.1 fusion.3
  99.1 0.1 reshape_squeeze.6
  99.2 0.3 fusion.1
  99.4 0.4 fusion.2
  99.8 0.2 tile.9
  100.0 0.1 fusion.weigh_ref
  100.2 3.9 %shard_map.99 = (f32[16,8192]{1,0:T(8,128)S(1)}, bf16[128,512]{1,0:T(8,128)(2,1)}) custom-call(s32[1]{0:T(128)} %bitcast.t_ref, bf16[16,128]{1,0:T(8,128)(2,1)S(1)} %copy-done.6, bf16[256,128]{1,0:T(8,128)(2,1)S(1)} %get-tuple-element.56.cot_ref, bf16[16,384,512]{2,1,0:T(8,128)(2,1)} %bitcast.23), custom_call_target="tpu_custom_call" | custom-call | flops 268435456 | bytes 8388608 | tf_op jit(solution)/shard_map/pallas_call | solution.py:440
  104.1 13.5 %all-to-all-done.3 = f32[256,4,128]{2,1,0:T(4,128)S(1)} async-done(((f32[256,4,128]{2,1,0:T(4,128)}), f32[256,4,128]{2,1,0:T(4,128)S(1)}, u32[]{:S(2)}, u32[]{:S(2)}) %all-to-all-start.3) | async-done | bytes 524320 | tf_op jit(solution)/shard_map/all_to_all | solution.py:30
  117.6 4.5 %collective-permute-start.1 = (f32[256,4,128]{2,1,0:T(4,128)S(1)}, f32[256,4,128]{2,1,0:T(4,128)S(1)}, u32[]{:S(2)}, u32[]{:S(2)}) collective-permute-start(f32[256,4,128]{2,1,0:T(4,128)S(1)} %all-to-all-done.3), channel_id=1, source_target_pairs={{0,1},{1,0},{2,3},{3,2},{4,5},{5,4},{6,7},{7,6},{8,9},{9,8},{10,11... | collective-permute-start | bytes 1572872 | tf_op jit(solution)/shard_map/ppermute | solution.py:457
  122.2 1.7 %shard_map.102 = (f32[32,8192]{1,0:T(8,128)}, f32[16,8192]{1,0:T(8,128)}, f32[8,16,512]{2,1,0:T(8,128)S(1)}, f32[128,128]{1,0:T(8,128)S(1)}) custom-call(s32[1]{0:T(128)} %bitcast.4.core_ref, f32[8,128,128]{2,1,0:T(8,128)S(1)} %bitcast.22, f32[16,128]{1,0:T(8,128)S(1)} %tile.21.basis_ref, f32[16,8192]{1,0:T(8,128)S(1)} %bitcast.19, ...), custom_call_target="tpu_custom_call" | custom-call | flops 1073741824 | bytes 3145728 | tf_op jit(solution)/shard_map/pallas_call | solution.py:466
  123.9 2.5 %shard_map.103 = (f32[32,8192]{1,0:T(8,128)}, f32[16,8192]{1,0:T(8,128)}, f32[16,8192]{1,0:T(8,128)}) custom-call(s32[1]{0:T(128)} %bitcast.4.core_ref, f32[8,128,128]{2,1,0:T(8,128)S(1)} %bitcast.21, f32[16,128]{1,0:T(8,128)S(1)} %tile.21.basis_ref, f32[16,8192]{1,0:T(8,128)S(1)} %bitcast.20, ...), custom_call_target="tpu_custom_call", output_to_operand_aliasing={{0}: (9, {}), {1}: (10, {})} | custom-call | flops 1073741824 | bytes 4194304 | tf_op jit(solution)/shard_map/pallas_call | solution.py:475
  (22 shorter events, 0.3 us)
Async XLA Ops:
  9.1 91.1 %copy-start.6 = (bf16[16,128]{1,0:T(8,128)(2,1)S(1)}, bf16[16,128]{1,0:T(8,128)(2,1)}, u32[]{:S(2)}) copy-start(bf16[16,128]{1,0:T(8,128)(2,1)} %c_ref.3) | copy-start | bytes 12292
  9.1 26.4 %all-to-all-start = ((f32[16,16,384]{2,1,0:T(8,128)}), f32[16,16,384]{2,1,0:T(8,128)S(1)}, u32[]{:S(2)}, u32[]{:S(2)}) async-start(f32[16,16,384]{2,1,0:T(8,128)} %shard_map.93), calls=%async_computation | async-start | bytes 786432 | tf_op jit(solution)/shard_map/all_to_all | solution.py:30
  20.9 79.2 %all-gather.3.cloned.1.call-start = ((), (), s32[]{:S(2)}) async-start(), calls=%async_computation.4 | async-start | bytes 6684672 | tf_op jit(solution)/shard_map/all_gather | solution.py:411
  22.9 10.4 %collective-permute-start = (f32[2,16,16,128]{3,2,1,0:T(8,128)}, f32[2,16,16,128]{3,2,1,0:T(8,128)S(1)}, u32[]{:S(2)}, u32[]{:S(2)}) collective-permute-start(f32[2,16,16,128]{3,2,1,0:T(8,128)} %get-tuple-element.48), channel_id=1, source_target_pairs={{0,16},{16,0},{32,48},{48,32},{1,17},{17,1},{33,49},{49,33},{2,18}... | collective-permute-start | bytes 786440 | tf_op jit(solution)/shard_map/ppermute | solution.py:383
  29.0 0.9 copy-start.2
  29.9 0.9 copy-start.3
  30.9 0.9 copy-start.4
  31.9 0.7 copy-start.5
  69.6 52.6 %copy-start = (f32[1,16,8192]{2,1,0:T(8,128)S(1)}, f32[1,16,8192]{2,1,0:T(8,128)}, u32[]{:S(2)}) copy-start(f32[1,16,8192]{2,1,0:T(8,128)} %param.9) | copy-start | bytes 1572868
  71.1 15.0 %all-to-all-start.2 = ((f32[16,2,4,128]{3,2,1,0:T(4,128)}), f32[16,2,4,128]{3,2,1,0:T(4,128)S(1)}, u32[]{:S(2)}, u32[]{:S(2)}) async-start(f32[16,2,4,128]{3,2,1,0:T(4,128)} %get-tuple-element.60), calls=%async_computation.2 | async-start | bytes 131072 | tf_op jit(solution)/shard_map/all_to_all | solution.py:30
  88.7 35.2 %copy-start.1 = (f32[16,8192]{1,0:T(8,128)S(1)}, f32[16,8192]{1,0:T(8,128)}, u32[]{:S(2)}) copy-start(f32[16,8192]{1,0:T(8,128)} %m_ref.1) | copy-start | bytes 1572868
  88.7 28.9 %all-to-all-start.3 = ((f32[256,4,128]{2,1,0:T(4,128)}), f32[256,4,128]{2,1,0:T(4,128)S(1)}, u32[]{:S(2)}, u32[]{:S(2)}) async-start(f32[256,4,128]{2,1,0:T(4,128)} %get-tuple-element.62), calls=%async_computation.3 | async-start | bytes 1048576 | tf_op jit(solution)/shard_map/all_to_all | solution.py:30
  117.6 6.2 %collective-permute-start.1 = (f32[256,4,128]{2,1,0:T(4,128)S(1)}, f32[256,4,128]{2,1,0:T(4,128)S(1)}, u32[]{:S(2)}, u32[]{:S(2)}) collective-permute-start(f32[256,4,128]{2,1,0:T(4,128)S(1)} %all-to-all-done.3), channel_id=1, source_target_pairs={{0,1},{1,0},{2,3},{3,2},{4,5},{5,4},{6,7},{7,6},{8,9},{9,8},{10,11... | collective-permute-start | bytes 1572872 | tf_op jit(solution)/shard_map/ppermute | solution.py:457
Sparse Core Ops, SparseCore 0:
  35.6 49.9 all-gather.2

commit v15 on v13

--- a/solution.py
+++ b/solution.py
@@ -18,7 +18,7 @@
 
 T = ("z", "core")
 R = ("y", "x")
-CHIPS = ("z", "y", "x")
+CHIPS = ("y", "x", "z")
 
 VMEM = pl.BlockSpec(memory_space=pltpu.VMEM)
 SMEM = pl.BlockSpec(memory_space=pltpu.SMEM)
@@ -84,7 +84,13 @@
     start = pl.multiple_of(t_ref[0] * wide, wide)
     for copy in fetch([(q_ref.at[:, pl.ds(start, wide)], q), (x_ref, x), (c_ref, c)], sems):
         copy.wait()
-    y = nt(q[...], x[...].astype(F32))
+    rest, pieces = q[...], []
+    for _ in range(3):
+        pieces.append(rest.astype(BF16))
+        rest -= pieces[-1].astype(F32)
+    rank = rest.shape[0]
+    y = nt(jnp.concatenate(pieces, 0), x[...], None)
+    y = y[:rank] + (y[rank : 2 * rank] + y[2 * rank :])
     cot = c[...].astype(F32)
     for k in range(n_t):
         send_ref[k, :, :tokens] = cot
@@ -279,8 +285,12 @@
     send_ref[...] = jnp.broadcast_to(q_pack[None], send_ref.shape)
 
 
-def place_blocks(near_core, blocks_ref, basis_ref, e_ref, g_ref, q_hbm, error_hbm, q, error, sems, approx_ref, gram):
-    n_z = blocks_ref.shape[0]
+def place_blocks(near_core, blocks_ref, near, basis_ref, e_ref, g_ref, q_hbm, error_hbm, q, error, sems, approx_ref, gram):
+    n_r, n_z, group, _ = blocks_ref.shape
+    for z in range(n_z):
+        for r in range(n_r):
+            row = z * LANES + r * group
+            near[row : row + group] = blocks_ref[r, z]
     rows = e_ref.shape[0]
     rank = q.shape[1]
     square = (LANES, LANES)
@@ -291,18 +301,18 @@
         0,
     )
     copies = []
-    blocks = blocks_ref[...].reshape(n_z * LANES, LANES)
+    blocks = near[...]
     every = nt(stack, blocks)
     for z in range(n_z):
         both = every[:, z * LANES : (z + 1) * LANES]
         start = pl.multiple_of((2 * z + near_core) * 4 * LANES, 4 * LANES)
         for b in range(4):
-            near = both[LANES + b * rows : LANES + (b + 1) * rows]
+            close = both[LANES + b * rows : LANES + (b + 1) * rows]
             at = pl.ds(pl.multiple_of(start + b * LANES, LANES), LANES)
             to = slice(b * LANES, (b + 1) * LANES)
             q[z, :, to] = both[b * rank : (b + 1) * rank]
-            approx_ref[z, :, to] = near
-            error[z, :, to] = e_ref[:, at] + g_ref[:, at] - near
+            approx_ref[z, :, to] = close
+            error[z, :, to] = e_ref[:, at] + g_ref[:, at] - close
         span = pl.ds(start, 4 * LANES)
         copies.append(pltpu.make_async_copy(q.at[z], q_hbm.at[:, span], sems.at[0, z]))
         copies.append(pltpu.make_async_copy(error.at[z], error_hbm.at[:, span], sems.at[1, z]))
@@ -311,9 +321,9 @@
     return gram + tn(blocks, blocks), copies
 
 
-def near_kernel(core_ref, mine_ref, basis_ref, e_ref, g_ref, q_hbm, error_hbm, approx_ref, gram_ref, q, error, sems):
+def near_kernel(core_ref, mine_ref, basis_ref, e_ref, g_ref, q_hbm, error_hbm, approx_ref, gram_ref, q, error, sems, near):
     gram, copies = place_blocks(
-        core_ref[0], mine_ref, basis_ref, e_ref, g_ref, q_hbm, error_hbm, q, error, sems, approx_ref,
+        core_ref[0], mine_ref, near, basis_ref, e_ref, g_ref, q_hbm, error_hbm, q, error, sems, approx_ref,
         jnp.zeros((LANES, LANES), F32),
     )
     gram_ref[...] = gram
@@ -321,14 +331,14 @@
         copy.wait()
 
 
-def far_kernel(limit, core_ref, other_ref, basis_ref, e_ref, g_ref, gram_ref, approx_ref, weigh_ref, m_ref, q_old, error_old, q_hbm, error_hbm, momentum_hbm, q, error, sems, far, out, out_sems):
+def far_kernel(limit, core_ref, other_ref, basis_ref, e_ref, g_ref, gram_ref, approx_ref, weigh_ref, m_ref, q_old, error_old, q_hbm, error_hbm, momentum_hbm, q, error, sems, near, far, out, out_sems):
     core = core_ref[0]
     gram, copies = place_blocks(
-        1 - core, other_ref, basis_ref, e_ref, g_ref, q_hbm, error_hbm, q, error, sems, far, gram_ref[...]
+        1 - core, other_ref, near, basis_ref, e_ref, g_ref, q_hbm, error_hbm, q, error, sems, far, gram_ref[...]
     )
     total = jnp.sum(gram * weigh_ref[...], keepdims=True)
     scale = jnp.minimum(1.0, limit / jnp.sqrt(total))
-    for z in range(other_ref.shape[0]):
+    for z in range(other_ref.shape[1]):
         for i, ref, c in ((0, approx_ref, core), (1, far, 1 - core)):
             at = pl.ds(pl.multiple_of((2 * z + c) * 4 * LANES, 4 * LANES), 4 * LANES)
             out[i, z] = BETA * m_ref[:, at] + scale * ref[z]
@@ -448,12 +458,13 @@
     )
     mine, grad_rows, weigh, basis4 = lax.optimization_barrier((mine, grad_rows, weigh, basis4))
     other = lax.ppermute(mine, "core", [(0, 1), (1, 0)])
-    blocks = (n_z, LANES, LANES)
+    blocks = (n_r, n_z, group, LANES)
     limit = CLIPPING * math.sqrt(ff_win * width)
     scratch = [
         pltpu.VMEM((n_z, rank, wide), F32),
         pltpu.VMEM((n_z, rows, wide), F32),
         pltpu.SemaphoreType.DMA((2, n_z)),
+        pltpu.VMEM((n_z * LANES, LANES), F32),
     ]
     whole = [((rank, width), F32), ((rows, width), F32)]
     q_new, error_new, approx, q_gram = call(

time: 132 us -> 132 us (level)
  no operation moved by 1% of the time
where the time goes in v15:
time: 132 us
  blocking collectives  47.9 us (36%)
  starting transfers between devices  28.5 us (22%)
  Pallas kernels  20.3 us (15%)
  waiting for transfers between devices  16.2 us (12%)
  between operations  14.3 us (11%)
  local copies, waits for them, and re-layouts  3.91 us (3%)
    all_to_all x2, blocking collectives, exchange(): return lax.all_to_all(parts, axes, 0, 0, tiled=True)  47.9 us
    all_to_all x2, starting transfers between devices, exchange(): return lax.all_to_all(parts, axes, 0, 0, tiled=True)  21.5 us
    all_to_all x2, waiting for transfers between devices, exchange(): return lax.all_to_all(parts, axes, 0, 0, tiled=True)  16.2 us
    pallas_call x1, Pallas kernels, body(): call(rows_kernel, [((rows, width), F32), ((tokens, wide), BF16)], [SMEM]...  3.91 us
    ppermute x1, starting transfers between devices, body(): other = lax.ppermute(mine, 'core', [(0, 1), (1, 0)])  3.83 us
    unnamed x14, local copies, waits for them, and re-layouts  3.51 us
    ppermute x1, starting transfers between devices, body(): moved = lax.ppermute(given, 'x', [(i, i ^ 1) for i in range(4)])  3.14 us
    pallas_call x1, Pallas kernels, body(): call(project_kernel, [((rows, rank), F32)], [HBM, HBM], flops=2 ** 27, mo...  2.96 us
  transfers between devices with their start and end apart: 5, of which 2 were waited for; matrix products, arithmetic and copies ran while one was open for 1% of the time, Pallas kernels for 12%

profile of v15, /device:TPU:1, one launch (start us, length us, event | category | flops | bytes accessed | tf_op | source)
XLA Modules:
  0.0 131.7 jit_solution(3297159896734743309)
XLA Ops:
  7.2 1.9 %shard_map.93 = f32[16,16,384]{2,1,0:T(8,128)} custom-call(s32[1]{0:T(128)} %bitcast.t_ref, bf16[128,512]{1,0:T(8,128)(2,1)} %x_ref.2, bf16[16,128]{1,0:T(8,128)(2,1)} %c_ref.3, f32[32,8192]{1,0:T(8,128)} %q_ref.3), custom_call_target="tpu_custom_call" | custom-call | bytes 1048576 | tf_op jit(solution)/shard_map/pallas_call | solution.py:364
  9.1 11.8 %all-to-all-start = ((f32[16,16,384]{2,1,0:T(8,128)}), f32[16,16,384]{2,1,0:T(8,128)S(1)}, u32[]{:S(2)}, u32[]{:S(2)}) async-start(f32[16,16,384]{2,1,0:T(8,128)} %shard_map.93), calls=%async_computation | async-start | bytes 786432 | tf_op jit(solution)/shard_map/all_to_all | solution.py:29
  20.9 0.0 all-gather.3.cloned.1.call-start
  21.0 1.9 %shard_map.94 = (f32[2,16,16,128]{3,2,1,0:T(8,128)}, f32[2,16,16,128]{3,2,1,0:T(8,128)}) custom-call(s32[1]{0:T(128)} %bitcast.2.x_ref, f32[16,8192]{1,0:T(8,128)} %bitcast.17), custom_call_target="tpu_custom_call" | custom-call | bytes 2097152 | tf_op jit(solution)/shard_map/pallas_call | solution.py:378
  22.9 3.1 %collective-permute-start = (f32[2,16,16,128]{3,2,1,0:T(8,128)}, f32[2,16,16,128]{3,2,1,0:T(8,128)S(1)}, u32[]{:S(2)}, u32[]{:S(2)}) collective-permute-start(f32[2,16,16,128]{3,2,1,0:T(8,128)} %get-tuple-element.49), channel_id=1, source_target_pairs={{0,16},{16,0},{32,48},{48,32},{1,17},{17,1},{33,49},{49,33},{2,18}... | collective-permute-start | bytes 786440 | tf_op jit(solution)/shard_map/ppermute | solution.py:387
  26.1 3.0 %shard_map.95.p_ref = f32[16,32]{1,0:T(8,128)} custom-call(f32[16,8192]{1,0:T(8,128)} %bitcast.18, f32[32,8192]{1,0:T(8,128)} %q_ref.3), custom_call_target="tpu_custom_call" | custom-call | flops 134217728 | bytes 2097152 | tf_op jit(solution)/shard_map/pallas_call | solution.py:388
  29.0 0.9 copy-done.2
  29.9 0.9 copy-done.3
  30.9 0.9 copy-done.4
  31.8 0.7 copy-done.5
  32.5 0.8 shard_map.96
  33.3 0.3 shard_map.97.et_ref
  33.6 1.9 %all-to-all-done.got_ref = f32[16,16,384]{2,1,0:T(8,128)S(1)} async-done(((f32[16,16,384]{2,1,0:T(8,128)}), f32[16,16,384]{2,1,0:T(8,128)S(1)}, u32[]{:S(2)}, u32[]{:S(2)}) %all-to-all-start) | async-done | bytes 393248 | tf_op jit(solution)/shard_map/all_to_all | solution.py:29
  35.5 0.7 shard_map.98
  36.2 33.7 %all_to_all.20.got_ref = f32[32,13,4,128]{3,2,1,0:T(4,128)S(1)} all-to-all(f32[32,13,4,128]{3,2,1,0:T(4,128)S(1)} %get-tuple-element.60), channel_id=1, replica_groups=mesh['y'=8,'x'=4,'z'=8,'core'=2] {'y','x'}, dimensions={0} | all-to-all | bytes 1703936 | tf_op jit(solution)/shard_map/all_to_all | solution.py:29
  70.0 0.9 shard_map.100
  70.9 14.1 %all_to_all.21.pack_ref = f32[16,2,4,128]{3,2,1,0:T(4,128)S(1)} all-to-all(f32[16,2,4,128]{3,2,1,0:T(4,128)S(1)} %get-tuple-element.61), channel_id=1, replica_groups=mesh['y'=8,'x'=4,'z'=8,'core'=2] {'z','core'}, dimensions={0} | all-to-all | bytes 131072 | tf_op jit(solution)/shard_map/all_to_all | solution.py:29
  85.0 2.6 %shard_map.101 = (f32[256,4,128]{2,1,0:T(4,128)}, f32[32,32]{1,0:T(8,128)S(1)}, f32[32,32]{1,0:T(8,128)S(1)}) custom-call(f32[16,2,4,128]{3,2,1,0:T(4,128)S(1)} %all_to_all.21.pack_ref, f32[16,512]{1,0:T(8,128)S(1)} %get-tuple-element.62.total_ref), custom_call_target="tpu_custom_call" | custom-call | flops 536870912 | bytes 1048576 | tf_op jit(solution)/shard_map/pallas_call | solution.py:435
  87.7 9.7 %all-to-all-start.3 = ((f32[256,4,128]{2,1,0:T(4,128)}), f32[256,4,128]{2,1,0:T(4,128)S(1)}, u32[]{:S(2)}, u32[]{:S(2)}) async-start(f32[256,4,128]{2,1,0:T(4,128)} %get-tuple-element.63), calls=%async_computation.3 | async-start | bytes 1048576 | tf_op jit(solution)/shard_map/all_to_all | solution.py:29
  97.4 0.1 reshape_squeeze.3
  97.5 0.1 fusion.3
  97.6 0.1 tile.21.basis_ref
  97.7 0.1 fusion.1
  97.8 0.2 fusion.2
  98.1 0.2 tile.9
  98.2 0.1 fusion.weigh_ref
  98.3 0.0 all-gather.3.cloned.1.call-done
  98.4 3.9 %shard_map.99 = (f32[16,8192]{1,0:T(8,128)S(1)}, bf16[128,512]{1,0:T(8,128)(2,1)}) custom-call(s32[1]{0:T(128)} %bitcast.t_ref, bf16[16,128]{1,0:T(8,128)(2,1)S(1)} %copy-done.6, bf16[256,128]{1,0:T(8,128)(2,1)S(1)} %get-tuple-element.57.cot_ref, bf16[16,384,512]{2,1,0:T(8,128)(2,1)} %bitcast.23), custom_call_target="tpu_custom_call" | custom-call | flops 268435456 | bytes 8388608 | tf_op jit(solution)/shard_map/pallas_call | solution.py:444
  102.3 14.3 %all-to-all-done.3 = f32[256,4,128]{2,1,0:T(4,128)S(1)} async-done(((f32[256,4,128]{2,1,0:T(4,128)}), f32[256,4,128]{2,1,0:T(4,128)S(1)}, u32[]{:S(2)}, u32[]{:S(2)}) %all-to-all-start.3) | async-done | bytes 524320 | tf_op jit(solution)/shard_map/all_to_all | solution.py:29
  116.6 3.8 %collective-permute-start.1 = (f32[256,4,128]{2,1,0:T(4,128)S(1)}, f32[256,4,128]{2,1,0:T(4,128)S(1)}, u32[]{:S(2)}, u32[]{:S(2)}) collective-permute-start(f32[256,4,128]{2,1,0:T(4,128)S(1)} %all-to-all-done.3), channel_id=1, source_target_pairs={{0,1},{1,0},{2,3},{3,2},{4,5},{5,4},{6,7},{7,6},{8,9},{9,8},{10,11... | collective-permute-start | bytes 1572872 | tf_op jit(solution)/shard_map/ppermute | solution.py:460
  120.5 1.8 %shard_map.102 = (f32[32,8192]{1,0:T(8,128)}, f32[16,8192]{1,0:T(8,128)}, f32[8,16,512]{2,1,0:T(8,128)S(1)}, f32[128,128]{1,0:T(8,128)S(1)}) custom-call(s32[1]{0:T(128)} %bitcast.4.core_ref, f32[32,8,4,128]{3,2,1,0:T(4,128)S(1)} %bitcast.22, f32[16,128]{1,0:T(8,128)S(1)} %tile.21.basis_ref, f32[16,8192]{1,0:T(8,128)S(1)} %bitcast.19, ...), custom_call_target="tpu_custom_call" | custom-call | flops 1073741824 | bytes 3145728 | tf_op jit(solution)/shard_map/pallas_call | solution.py:470
  122.2 2.6 %shard_map.103 = (f32[32,8192]{1,0:T(8,128)}, f32[16,8192]{1,0:T(8,128)}, f32[16,8192]{1,0:T(8,128)}) custom-call(s32[1]{0:T(128)} %bitcast.4.core_ref, f32[32,8,4,128]{3,2,1,0:T(4,128)S(1)} %bitcast.21, f32[16,128]{1,0:T(8,128)S(1)} %tile.21.basis_ref, f32[16,8192]{1,0:T(8,128)S(1)} %bitcast.20, ...), custom_call_target="tpu_custom_call", output_to_operand_aliasing={{0}: (9, {}), {1}: (10, {})} | custom-call | flops 1073741824 | bytes 4194304 | tf_op jit(solution)/shard_map/pallas_call | solution.py:479
  (19 shorter events, 0.1 us)
Async XLA Ops:
  9.1 89.3 %copy-start.6 = (bf16[16,128]{1,0:T(8,128)(2,1)S(1)}, bf16[16,128]{1,0:T(8,128)(2,1)}, u32[]{:S(2)}) copy-start(bf16[16,128]{1,0:T(8,128)(2,1)} %c_ref.3) | copy-start | bytes 12292
  9.1 26.4 %all-to-all-start = ((f32[16,16,384]{2,1,0:T(8,128)}), f32[16,16,384]{2,1,0:T(8,128)S(1)}, u32[]{:S(2)}, u32[]{:S(2)}) async-start(f32[16,16,384]{2,1,0:T(8,128)} %shard_map.93), calls=%async_computation | async-start | bytes 786432 | tf_op jit(solution)/shard_map/all_to_all | solution.py:29
  20.9 77.4 %all-gather.3.cloned.1.call-start = ((), (), s32[]{:S(2)}) async-start(), calls=%async_computation.4 | async-start | bytes 6684672 | tf_op jit(solution)/shard_map/all_gather | solution.py:415
  22.9 10.4 %collective-permute-start = (f32[2,16,16,128]{3,2,1,0:T(8,128)}, f32[2,16,16,128]{3,2,1,0:T(8,128)S(1)}, u32[]{:S(2)}, u32[]{:S(2)}) collective-permute-start(f32[2,16,16,128]{3,2,1,0:T(8,128)} %get-tuple-element.49), channel_id=1, source_target_pairs={{0,16},{16,0},{32,48},{48,32},{1,17},{17,1},{33,49},{49,33},{2,18}... | collective-permute-start | bytes 786440 | tf_op jit(solution)/shard_map/ppermute | solution.py:387
  29.0 0.9 copy-start.2
  29.9 0.9 copy-start.3
  30.9 0.9 copy-start.4
  31.8 0.7 copy-start.5
  36.2 84.2 %copy-start = (f32[1,16,8192]{2,1,0:T(8,128)S(1)}, f32[1,16,8192]{2,1,0:T(8,128)}, u32[]{:S(2)}) copy-start(f32[1,16,8192]{2,1,0:T(8,128)} %param.9) | copy-start | bytes 1572868
  87.7 34.6 %copy-start.1 = (f32[16,8192]{1,0:T(8,128)S(1)}, f32[16,8192]{1,0:T(8,128)}, u32[]{:S(2)}) copy-start(f32[16,8192]{1,0:T(8,128)} %m_ref.1) | copy-start | bytes 1572868
  87.7 28.9 %all-to-all-start.3 = ((f32[256,4,128]{2,1,0:T(4,128)}), f32[256,4,128]{2,1,0:T(4,128)S(1)}, u32[]{:S(2)}, u32[]{:S(2)}) async-start(f32[256,4,128]{2,1,0:T(4,128)} %get-tuple-element.63), calls=%async_computation.3 | async-start | bytes 1048576 | tf_op jit(solution)/shard_map/all_to_all | solution.py:29
  116.6 5.6 %collective-permute-start.1 = (f32[256,4,128]{2,1,0:T(4,128)S(1)}, f32[256,4,128]{2,1,0:T(4,128)S(1)}, u32[]{:S(2)}, u32[]{:S(2)}) collective-permute-start(f32[256,4,128]{2,1,0:T(4,128)S(1)} %all-to-all-done.3), channel_id=1, source_target_pairs={{0,1},{1,0},{2,3},{3,2},{4,5},{5,4},{6,7},{7,6},{8,9},{9,8},{10,11... | collective-permute-start | bytes 1572872 | tf_op jit(solution)/shard_map/ppermute | solution.py:460
Sparse Core Ops, SparseCore 0:
  35.6 50.2 all-gather.2
